TPU v7x, 32 devices: a whole 2x2x4 slice. The times are simulated.
32 devices in a mesh: grp: 4 (over z), blk: 8 (over y, x, core).
Axes of the slice: x: 2, y: 2, z: 4, core: 2. Of those that a mesh axis runs over, the one named last changes fastest.
Arguments:
- embeddings: bfloat16 [8192, 768], P(('grp', 'blk')), may hold values from -6 to 6
- target: int32 [8192, 1], P(('grp', 'blk')), may hold values from 0 to 31; in each aligned block of 256 rows (0 to 255, 256 to 511, ...) at most 16 rows name the same one
- cluster: int32 [8192], P(('grp', 'blk')), may hold values from 0 to 15
Outputs:
- nearest: float32 [8192], P(('grp', 'blk'))
Inputs may be any that keep to these rules, and one draw needn't show every extreme that they name: The rows of one device send at most 16 rows to any one target.
All inputs are finite; a program needn't handle non-finite values.
Results may differ from a plain program's by a relative error of at most 0.0014.
Values may be sent and summed in bfloat16 or wider, within the bound.
No kernel may reach another device: no remote copies, remote signals or barrier semaphores. Data moves between devices by JAX's collectives and lax.ppermute only.
A program may use at most 64 MiB of HBM per device.

v0:
```python
import functools

import jax
import jax.numpy as jnp
from jax import lax
from jax.experimental import pallas as pl
from jax.experimental.pallas import tpu as pltpu
from jax.sharding import PartitionSpec as P

CLUSTERS = 64
TAIL = 16
VMEM = 24 << 20
VMEM_SMALL = 8 << 20


def pack_kernel(per_group, emb_ref, target_ref, cluster_ref, out_ref):
    rows, width = emb_ref.shape
    x = emb_ref[...].astype(jnp.float32)
    scale = lax.rsqrt(jnp.sum(x * x, axis=1, keepdims=True) + 1e-06)
    out_ref[:rows, :] = (x * scale).astype(jnp.bfloat16)
    key = target_ref[...] // per_group * CLUSTERS + cluster_ref[...] + 1
    key = jnp.concatenate([key, jnp.zeros((1, width - rows), jnp.int32)], axis=1)
    key = jnp.broadcast_to(key.astype(jnp.float32), (TAIL, width))
    out_ref[rows:, :] = key.astype(jnp.bfloat16)


def pack(embeddings, target, cluster, per_group):
    rows, width = embeddings.shape
    return pl.pallas_call(
        functools.partial(pack_kernel, per_group),
        out_shape=jax.ShapeDtypeStruct((rows + TAIL, width), jnp.bfloat16),
        compiler_params=pltpu.CompilerParams(vmem_limit_bytes=VMEM_SMALL),
        name="pack",
    )(embeddings, target.reshape(1, rows), cluster.reshape(1, rows))


def whole(pieces):
    return pieces[0][...] if len(pieces) == 1 else jnp.concatenate([ref[...] for ref in pieces], axis=0)


def score_kernel(counts, n_cols, pairs, want_rows, known, rows_known, outs, places, *refs):
    *plane, cols, cols_in, rows_in, col_outs, rows_outs = take(
        refs, counts + (n_cols, bool(known), bool(rows_known), len(outs), 2 if places else 1)
    )
    rows = col_outs[0].shape[2]
    low = jnp.full((1, rows), -1.0, jnp.float32)
    best, rows_best = [low] * n_cols, [low] * len(plane)
    for at, col in enumerate(known):
        best[col] = cols_in[0][at]
    for at, k in enumerate(rows_known):
        rows_best[k] = rows_in[0][at]
    for k, pieces in enumerate(plane):
        mine = [at for one, at, _ in pairs if one == k]
        if not mine:
            continue
        diagonal = [at for one, at, same in pairs if one == k and same]
        block = whole(pieces)
        row_keys = jnp.transpose(jnp.broadcast_to(block[rows:, :rows].astype(jnp.float32)[:1], (128, rows)))
        row_keys = jnp.concatenate([row_keys] * (rows // 128), axis=1)
        row_best = None
        for at in mine:
            scores = lax.dot_general(
                block[:rows], cols[at][:rows, :], (((1,), (1,)), ((), ())), preferred_element_type=jnp.float32
            )
            allowed = row_keys == cols[at][rows:, :rows].astype(jnp.float32)[:1]
            if at in diagonal:
                one = lax.broadcasted_iota(jnp.int32, scores.shape, 0)
                other = lax.broadcasted_iota(jnp.int32, scores.shape, 1)
                allowed = allowed & (one != other)
            masked = jnp.where(allowed, scores, -1.0)
            best[at] = jnp.maximum(best[at], jnp.max(masked, axis=0, keepdims=True))
            if at in want_rows:
                for lane in range(0, rows, 128):
                    part = masked[:, lane : lane + 128]
                    row_best = part if row_best is None else jnp.maximum(row_best, part)
        if row_best is not None:
            got = jnp.max(jnp.transpose(row_best), axis=0, keepdims=True)
            rows_best[k] = jnp.maximum(rows_best[k], got)
    for ref, held in zip(col_outs, outs):
        for at, col in enumerate(held):
            ref[at] = best[col]
    for k, value in enumerate(rows_best):
        if places:
            rows_outs[places[k] % 2][places[k] // 2] = value
        else:
            rows_outs[0][k] = value


def take(refs, counts):
    groups, at = [], 0
    for count in counts:
        groups.append(refs[at : at + count])
        at += count
    return groups


def score(name, plane, cols, pairs, want_rows, outs, known=(), cols_in=(), rows_known=(), rows_in=(), places=None):
    length, width = cols[0].shape
    rows = length - TAIL
    kernel = functools.partial(
        score_kernel,
        tuple(len(pieces) for pieces in plane),
        len(cols),
        tuple(pairs),
        tuple(want_rows),
        tuple(known),
        tuple(rows_known),
        tuple(outs),
        places,
    )
    shapes = [len(held) for held in outs] + ([len(plane) // 2] * 2 if places else [len(plane)])
    return pl.pallas_call(
        kernel,
        out_shape=[jax.ShapeDtypeStruct((count, 1, rows), jnp.float32) for count in shapes],
        compiler_params=pltpu.CompilerParams(vmem_limit_bytes=VMEM),
        cost_estimate=pl.CostEstimate(
            flops=2 * len(pairs) * rows * rows * width,
            bytes_accessed=2 * (len(plane) + len(cols)) * length * width,
            transcendentals=0,
        ),
        name=name,
    )(*[piece for pieces in plane for piece in pieces], *cols, *cols_in, *rows_in)


def join_kernel(n, *refs):
    for at in range(n):
        refs[n + 1 + at][...] = jnp.maximum(refs[at][...], refs[n][at])


def join(here, got):
    return pl.pallas_call(
        functools.partial(join_kernel, len(here)),
        out_shape=[jax.ShapeDtypeStruct((1, x.shape[-1]), x.dtype) for x in here],
        compiler_params=pltpu.CompilerParams(vmem_limit_bytes=VMEM_SMALL),
        name="join",
    )(*[x.reshape(1, -1) for x in here], got)


def halve_kernel(keep_ref, got_ref, even_ref, odd_ref):
    for at in range(keep_ref.shape[0]):
        value = jnp.maximum(keep_ref[at], got_ref[at])
        (odd_ref if at % 2 else even_ref)[at // 2] = value


def halve(keep, got):
    half = jax.ShapeDtypeStruct((keep.shape[0] // 2, *keep.shape[1:]), keep.dtype)
    return pl.pallas_call(
        halve_kernel,
        out_shape=[half, half],
        compiler_params=pltpu.CompilerParams(vmem_limit_bytes=VMEM_SMALL),
        name="halve",
    )(keep, got)


def plane_shift(x, mask):
    size = lax.axis_size("blk")
    return lax.ppermute(x, "blk", [(i, i ^ mask) for i in range(size)])


def grp_shift(x, shift, mask=0):
    groups, size = lax.axis_size("grp"), lax.axis_size("blk")
    if not mask:
        return lax.ppermute(x, "grp", [(z, (z + shift) % groups) for z in range(groups)])
    pairs = [
        (z * size + i, (z + shift) % groups * size + (i ^ mask)) for z in range(groups) for i in range(size)
    ]
    return lax.ppermute(x, ("grp", "blk"), pairs)


def relay_half_way(x):
    groups = lax.axis_size("grp")
    return lax.ppermute(x, "grp", [((z + 1) % groups, z) for z in range(groups // 2)])


def fetch_plane(packed, per_group, first):
    half = (packed.shape[0] - TAIL) // 2
    plane = {0: (packed,)}
    halves = {}
    masks = range(2, per_group, 2)
    for mask in sorted(masks, key=lambda mask: mask.bit_count()):
        low, high = mask & -mask, 1 << (mask.bit_length() - 1)
        if low == high:
            block = plane_shift(packed, mask)
            plane[mask] = (block,)
            block = lax.optimization_barrier((block, first))[0]
            halves[mask] = (block[:half], block[half:])
        else:
            plane[mask] = halves[mask] = (
                plane_shift(halves[mask ^ low][0], low),
                plane_shift(halves[mask ^ high][1], high),
            )
    return plane


def body(embeddings, target, cluster):
    groups = lax.axis_size("grp")
    per_group = lax.axis_size("blk")
    packed = pack(embeddings, target, cluster, per_group)
    next_one = grp_shift(packed, -1)
    half_way = relay_half_way(next_one)
    blocks = fetch_plane(packed, per_group, next_one)
    plane = list(blocks.values())
    n_direct = sum(len(pieces) == 1 for pieces in plane)
    places = tuple(mask // 2 for mask in blocks)
    every = range(len(plane))

    own_then = lax.optimization_barrier((packed, next_one))[0]
    cols = [packed, plane_shift(own_then, 1), next_one, plane_shift(next_one, 1)]
    pairs = [(k, at, k == at == 0) for k in every for at in range(4)]
    early = [pair for pair in pairs if pair[0] < n_direct]
    best, rows_best = score("compare_direct", plane[:n_direct], cols, early, (2, 3), [(0, 1, 2, 3)])
    own, next_best, twins, rows_best = score(
        "compare_relayed",
        plane,
        cols,
        [pair for pair in pairs if pair not in early],
        (2, 3),
        [(0,), (2,), (1, 3)],
        known=range(4),
        cols_in=[best],
        rows_known=range(n_direct),
        rows_in=[rows_best],
    )
    own, next_best = join([own, next_best], plane_shift(twins, 1))
    found = [own, grp_shift(next_best, 1)]

    half_then = lax.optimization_barrier((half_way, own))[0]
    half_twin = plane_shift(half_then, 1)
    rest = dict(pairs=[(k, 0, False) for k in every], want_rows=(0,), outs=[(0,)], rows_known=every)
    half_best, rows_best = score("compare_half_way", plane, [half_way], rows_in=[rows_best], **rest)
    found.append(grp_shift(half_best.reshape(1, -1), groups // 2))
    half_twin = lax.optimization_barrier((half_twin, found[1]))[0]
    twin_best, even, odd = score("compare_twin", plane, [half_twin], rows_in=[rows_best], places=places, **rest)
    found.append(grp_shift(twin_best.reshape(1, -1), groups // 2, 1))

    odd = lax.optimization_barrier((odd, found[2]))[0]
    mask = 2
    while len(even) > 1:
        even, odd = halve(even, plane_shift(odd, mask))
        mask *= 2
    found += [even.reshape(1, -1), plane_shift(odd, mask).reshape(1, -1)]
    return functools.reduce(jnp.maximum, found).reshape(-1)


def solution(mesh):
    return jax.shard_map(
        body,
        mesh=mesh,
        in_specs=(P(("grp", "blk"), None), P(("grp", "blk"), None), P(("grp", "blk"))),
        out_specs=P(("grp", "blk")),
        check_vma=False,
    )
```

profile of v0, /device:TPU:0, one launch (start us, length us, event | category | flops | bytes accessed | tf_op | source)
XLA Modules:
  0.0 43.7 jit_solution(18143445359826911605)
XLA Ops:
  0.0 0.7 %copy-done.2 = s32[256]{0:T(256)S(1)} copy-done((s32[256]{0:T(256)S(1)}, s32[256]{0:T(256)}, u32[]{:S(2)}) %copy-start.2) | copy-done | bytes 1048
  0.7 0.0 copy-done.1
  0.7 1.0 %copy-done = bf16[256,768]{1,0:T(8,128)(2,1)S(1)} copy-done((bf16[256,768]{1,0:T(8,128)(2,1)S(1)}, bf16[256,768]{1,0:T(8,128)(2,1)}, u32[]{:S(2)}) %copy-start) | copy-done | bytes 393240
  1.7 0.2 pack.1.refs_0_.refs_3_.refs_5_
  1.9 5.1 %collective-permute-start.2 = (bf16[272,768]{1,0:T(8,128)(2,1)S(1)}, bf16[272,768]{1,0:T(8,128)(2,1)S(1)}, u32[]{:S(2)}, u32[]{:S(2)}) collective-permute-start(bf16[272,768]{1,0:T(8,128)(2,1)S(1)} %pack.1.refs_0_.refs_3_.refs_5_), channel_id=1, source_target_pairs={{0,24},{8,0},{16,8},{24,16},{1,25},{9,1},{17,9},{25,17},{2,26},{10... | collective-permute-start | bytes 1253384 | tf_op jit(solution)/shard_map/ppermute | solution.py:163
  7.0 1.5 %collective-permute-start = (bf16[272,768]{1,0:T(8,128)(2,1)S(1)}, bf16[272,768]{1,0:T(8,128)(2,1)S(1)}, u32[]{:S(2)}, u32[]{:S(2)}) collective-permute-start(bf16[272,768]{1,0:T(8,128)(2,1)S(1)} %pack.1.refs_0_.refs_3_.refs_5_), channel_id=1, source_target_pairs={{0,2},{1,3},{2,0},{3,1},{4,6},{5,7},{6,4},{7,5},{8,10},{9,11},{10,... | collective-permute-start | bytes 1253384 | tf_op jit(solution)/shard_map/ppermute | solution.py:157
  8.5 1.5 %collective-permute-start.1 = (bf16[272,768]{1,0:T(8,128)(2,1)S(1)}, bf16[272,768]{1,0:T(8,128)(2,1)S(1)}, u32[]{:S(2)}, u32[]{:S(2)}) collective-permute-start(bf16[272,768]{1,0:T(8,128)(2,1)S(1)} %pack.1.refs_0_.refs_3_.refs_5_), channel_id=1, source_target_pairs={{0,4},{1,5},{2,6},{3,7},{4,0},{5,1},{6,2},{7,3},{8,12},{9,13},{10,... | collective-permute-start | bytes 1253384 | tf_op jit(solution)/shard_map/ppermute | solution.py:157
  10.0 5.9 %collective-permute-done.2.refs_5_.refs_7_ = bf16[272,768]{1,0:T(8,128)(2,1)S(1)} collective-permute-done((bf16[272,768]{1,0:T(8,128)(2,1)S(1)}, bf16[272,768]{1,0:T(8,128)(2,1)S(1)}, u32[]{:S(2)}, u32[]{:S(2)}) %collective-permute-start.2) | collective-permute-done | bytes 417824 | tf_op jit(solution)/shard_map/ppermute | solution.py:163
  15.9 0.0 collective-permute-start.5
  15.9 0.5 %collective-permute-start.6 = (bf16[272,768]{1,0:T(8,128)(2,1)S(1)}, bf16[272,768]{1,0:T(8,128)(2,1)S(1)}, u32[]{:S(2)}, u32[]{:S(2)}) collective-permute-start(bf16[272,768]{1,0:T(8,128)(2,1)S(1)} %collective-permute-done.2.refs_5_.refs_7_), channel_id=1, source_target_pairs={{0,1},{1,0},{2,3},{3,2},{4,5},{5,4},{6,7},{7,6},{8,9},{9,8},{10,11... | collective-permute-start | bytes 1253384 | tf_op jit(solution)/shard_map/ppermute | solution.py:157
  16.4 1.3 %collective-permute-start.9 = (bf16[272,768]{1,0:T(8,128)(2,1)S(1)}, bf16[272,768]{1,0:T(8,128)(2,1)S(1)}, u32[]{:S(2)}, u32[]{:S(2)}) collective-permute-start(bf16[272,768]{1,0:T(8,128)(2,1)S(1)} %collective-permute-done.2.refs_5_.refs_7_), channel_id=1, source_target_pairs={{8,0},{16,8},{9,1},{17,9},{10,2},{18,10},{11,3},{19,11},{12,4},{20... | collective-permute-start | bytes 1253384 | tf_op jit(solution)/shard_map/ppermute | solution.py:172
  17.7 0.4 collective-permute-done.refs_1_
  18.1 1.6 %collective-permute-start.4 = (bf16[144,768]{1,0:T(8,128)(2,1)S(1)}, bf16[144,768]{1,0:T(8,128)(2,1)S(1)}, u32[]{:S(2)}, u32[]{:S(2)}) collective-permute-start(bf16[144,768]{1,0:T(8,128)(2,1)S(1)} %slice.7), channel_id=1, source_target_pairs={{0,4},{1,5},{2,6},{3,7},{4,0},{5,1},{6,2},{7,3},{8,12},{9,13},{10,... | collective-permute-start | bytes 663560 | tf_op jit(solution)/shard_map/ppermute | solution.py:157
  19.7 1.6 %collective-permute-start.3 = (bf16[128,768]{1,0:T(8,128)(2,1)S(1)}, bf16[128,768]{1,0:T(8,128)(2,1)S(1)}, u32[]{:S(2)}, u32[]{:S(2)}) collective-permute-start(bf16[128,768]{1,0:T(8,128)(2,1)S(1)} %slice.6), channel_id=1, source_target_pairs={{0,2},{1,3},{2,0},{3,1},{4,6},{5,7},{6,4},{7,5},{8,10},{9,11},{10,... | collective-permute-start | bytes 589832 | tf_op jit(solution)/shard_map/ppermute | solution.py:157
  21.2 0.0 collective-permute-done.6.refs_6_.refs_8_
  21.2 1.5 %compare_direct.1 = (f32[4,1,256]{2,1,0:T(1,128)S(1)}, f32[3,1,256]{2,1,0:T(1,128)S(1)}) custom-call(bf16[272,768]{1,0:T(8,128)(2,1)S(1)} %pack.1.refs_0_.refs_3_.refs_5_, bf16[272,768]{1,0:T(8,128)(2,1)S(1)} %collective-permute-done.refs_1_, bf16[272,768]{1,0:T(8,128)(2,1)S(1)} %collective-permute-done.1.refs_2_, ...), custom_call_target="tpu_custom_call" | custom-call | flops 1207959552 | bytes 2924544 | tf_op jit(solution)/shard_map/compare_direct/pallas_call | solution.py:112
  22.8 3.1 %collective-permute-done.3.refs_3_ = bf16[128,768]{1,0:T(8,128)(2,1)S(1)} collective-permute-done((bf16[128,768]{1,0:T(8,128)(2,1)S(1)}, bf16[128,768]{1,0:T(8,128)(2,1)S(1)}, u32[]{:S(2)}, u32[]{:S(2)}) %collective-permute-start.3) | collective-permute-done | bytes 196640 | tf_op jit(solution)/shard_map/ppermute | solution.py:157
  25.9 0.7 %compare_relayed.1 = (f32[1,1,256]{2,1,0:T(1,128)S(1)}, f32[1,1,256]{2,1,0:T(1,128)S(1)}, f32[2,1,256]{2,1,0:T(1,128)S(1)}, f32[4,1,256]{2,1,0:T(1,128)S(1)}) custom-call(bf16[272,768]{1,0:T(8,128)(2,1)S(1)} %pack.1.refs_0_.refs_3_.refs_5_, bf16[272,768]{1,0:T(8,128)(2,1)S(1)} %collective-permute-done.refs_1_, ...), custom_call_target="tpu_custom_call" | custom-call | flops 402653184 | bytes 3342336 | tf_op jit(solution)/shard_map/compare_relayed/pallas_call | solution.py:112
  26.6 0.1 collective-permute-start.7
  26.7 1.1 %collective-permute-done.7.refs_2_ = f32[2,1,256]{2,1,0:T(1,128)S(1)} collective-permute-done((f32[2,1,256]{2,1,0:T(1,128)S(1)}, f32[2,1,256]{2,1,0:T(1,128)S(1)}, u32[]{:S(2)}, u32[]{:S(2)}) %collective-permute-start.7) | collective-permute-done | bytes 2080 | tf_op jit(solution)/shard_map/ppermute | solution.py:157
  27.8 2.0 %collective-permute-done.9.refs_5_ = bf16[272,768]{1,0:T(8,128)(2,1)S(1)} collective-permute-done((bf16[272,768]{1,0:T(8,128)(2,1)S(1)}, bf16[272,768]{1,0:T(8,128)(2,1)S(1)}, u32[]{:S(2)}, u32[]{:S(2)}) %collective-permute-start.9) | collective-permute-done | bytes 417824 | tf_op jit(solution)/shard_map/ppermute | solution.py:172
  29.8 0.6 %collective-permute-start.8 = (f32[1,256]{1,0:T(1,128)S(1)}, f32[1,256]{1,0:T(1,128)S(1)}, u32[]{:S(2)}, u32[]{:S(2)}) collective-permute-start(f32[1,256]{1,0:T(1,128)S(1)} %get-tuple-element.35), channel_id=1, source_target_pairs={{0,8},{8,16},{16,24},{24,0},{1,9},{9,17},{17,25},{25,1},{2,10},{10... | collective-permute-start | bytes 3080 | tf_op jit(solution)/shard_map/ppermute | solution.py:163
  30.4 0.7 %compare_half_way.1 = (f32[1,1,256]{2,1,0:T(1,128)S(1)}, f32[4,1,256]{2,1,0:T(1,128)S(1)}) custom-call(bf16[272,768]{1,0:T(8,128)(2,1)S(1)} %pack.1.refs_0_.refs_3_.refs_5_, bf16[272,768]{1,0:T(8,128)(2,1)S(1)} %collective-permute-done.refs_1_, bf16[272,768]{1,0:T(8,128)(2,1)S(1)} %collective-permute-done.1.refs_2_, ...), custom_call_target="tpu_custom_call" | custom-call | flops 402653184 | bytes 2088960 | tf_op jit(solution)/shard_map/compare_half_way/pallas_call | solution.py:112
  31.1 2.0 %collective-permute-start.10 = (f32[1,256]{1,0:T(1,128)S(1)}, f32[1,256]{1,0:T(1,128)S(1)}, u32[]{:S(2)}, u32[]{:S(2)}) collective-permute-start(f32[1,256]{1,0:T(1,128)S(1)} %bitcast.18), channel_id=1, source_target_pairs={{0,16},{8,24},{16,0},{24,8},{1,17},{9,25},{17,1},{25,9},{2,18},{10... | collective-permute-start | bytes 3080 | tf_op jit(solution)/shard_map/ppermute | solution.py:163
  33.1 2.1 %collective-permute-done.8 = f32[1,256]{1,0:T(1,128)S(1)} collective-permute-done((f32[1,256]{1,0:T(1,128)S(1)}, f32[1,256]{1,0:T(1,128)S(1)}, u32[]{:S(2)}, u32[]{:S(2)}) %collective-permute-start.8) | collective-permute-done | bytes 1056 | tf_op jit(solution)/shard_map/ppermute | solution.py:163
  35.2 0.7 %compare_twin.1 = (f32[1,1,256]{2,1,0:T(1,128)S(1)}, f32[2,1,256]{2,1,0:T(1,128)S(1)}, f32[2,1,256]{2,1,0:T(1,128)S(1)}) custom-call(bf16[272,768]{1,0:T(8,128)(2,1)S(1)} %pack.1.refs_0_.refs_3_.refs_5_, bf16[272,768]{1,0:T(8,128)(2,1)S(1)} %collective-permute-done.refs_1_, bf16[272,768]{1,0:T(8,128)(2,1)S(1)} %collective-permute-done.1.refs_2_, ...), custom_call_target="tpu_custom_call" | custom-call | flops 402653184 | bytes 2088960 | tf_op jit(solution)/shard_map/compare_twin/pallas_call | solution.py:112
  35.9 1.6 %collective-permute-start.13 = (f32[2,1,256]{2,1,0:T(1,128)S(1)}, f32[2,1,256]{2,1,0:T(1,128)S(1)}, u32[]{:S(2)}, u32[]{:S(2)}) collective-permute-start(f32[2,1,256]{2,1,0:T(1,128)S(1)} %get-tuple-element.44), channel_id=1, source_target_pairs={{0,2},{1,3},{2,0},{3,1},{4,6},{5,7},{6,4},{7,5},{8,10},{9,11},{10,... | collective-permute-start | bytes 6152 | tf_op jit(solution)/shard_map/ppermute | solution.py:157
  37.5 2.1 %collective-permute-done.13.got_ref = f32[2,1,256]{2,1,0:T(1,128)S(1)} collective-permute-done((f32[2,1,256]{2,1,0:T(1,128)S(1)}, f32[2,1,256]{2,1,0:T(1,128)S(1)}, u32[]{:S(2)}, u32[]{:S(2)}) %collective-permute-start.13) | collective-permute-done | bytes 2080 | tf_op jit(solution)/shard_map/ppermute | solution.py:157
  39.6 1.5 %collective-permute-start.14 = (f32[1,1,256]{2,1,0:T(1,128)S(1)}, f32[1,1,256]{2,1,0:T(1,128)S(1)}, u32[]{:S(2)}, u32[]{:S(2)}) collective-permute-start(f32[1,1,256]{2,1,0:T(1,128)S(1)} %get-tuple-element.46), channel_id=1, source_target_pairs={{0,4},{1,5},{2,6},{3,7},{4,0},{5,1},{6,2},{7,3},{8,12},{9,13},{10,... | collective-permute-start | bytes 3080 | tf_op jit(solution)/shard_map/ppermute | solution.py:157
  41.1 0.3 collective-permute-done.12
  41.4 1.8 %collective-permute-done.14 = f32[1,1,256]{2,1,0:T(1,128)S(1)} collective-permute-done((f32[1,1,256]{2,1,0:T(1,128)S(1)}, f32[1,1,256]{2,1,0:T(1,128)S(1)}, u32[]{:S(2)}, u32[]{:S(2)}) %collective-permute-start.14) | collective-permute-done | bytes 1056 | tf_op jit(solution)/shard_map/ppermute | solution.py:157
  43.1 0.6 %bitcast_maximum_fusion = f32[1,256]{1,0:T(1,128)} fusion(f32[1,1,256]{2,1,0:T(1,128)S(1)} %collective-permute-done.14, f32[1,1,256]{2,1,0:T(1,128)S(1)} %get-tuple-element.45, f32[1,256]{1,0:T(1,128)S(1)} %collective-permute-done.12, f32[1,256]{1,0:T(1,128)S(1)} %collective-permute-done.10, f32[1,256]{1,0:T(1,128)S(1)} %get-tuple-element.34, ...), kind=kLoop, calls=%fused_computation | loop fusion | flops 1280 | bytes 7168 | tf_op jit(solution)/shard_map/max | solution.py:242
  (14 shorter events, 0.1 us)
Async XLA Ops:
  0.0 0.7 %copy-start.2 = (s32[256]{0:T(256)S(1)}, s32[256]{0:T(256)}, u32[]{:S(2)}) copy-start(s32[256]{0:T(256)} %param.5) | copy-start | bytes 3076
  0.0 0.7 %copy-start.1 = (s32[256,1]{0,1:T(1,128)S(1)}, s32[256,1]{0,1:T(1,128)}, u32[]{:S(2)}) copy-start(s32[256,1]{0,1:T(1,128)} %param.4) | copy-start | bytes 3076
  0.7 1.0 %copy-start = (bf16[256,768]{1,0:T(8,128)(2,1)S(1)}, bf16[256,768]{1,0:T(8,128)(2,1)}, u32[]{:S(2)}) copy-start(bf16[256,768]{1,0:T(8,128)(2,1)} %emb_ref.1) | copy-start | bytes 1179652
  1.9 14.0 %collective-permute-start.2 = (bf16[272,768]{1,0:T(8,128)(2,1)S(1)}, bf16[272,768]{1,0:T(8,128)(2,1)S(1)}, u32[]{:S(2)}, u32[]{:S(2)}) collective-permute-start(bf16[272,768]{1,0:T(8,128)(2,1)S(1)} %pack.1.refs_0_.refs_3_.refs_5_), channel_id=1, source_target_pairs={{0,24},{8,0},{16,8},{24,16},{1,25},{9,1},{17,9},{25,17},{2,26},{10... | collective-permute-start | bytes 1253384 | tf_op jit(solution)/shard_map/ppermute | solution.py:163
  7.0 11.1 %collective-permute-start = (bf16[272,768]{1,0:T(8,128)(2,1)S(1)}, bf16[272,768]{1,0:T(8,128)(2,1)S(1)}, u32[]{:S(2)}, u32[]{:S(2)}) collective-permute-start(bf16[272,768]{1,0:T(8,128)(2,1)S(1)} %pack.1.refs_0_.refs_3_.refs_5_), channel_id=1, source_target_pairs={{0,2},{1,3},{2,0},{3,1},{4,6},{5,7},{6,4},{7,5},{8,10},{9,11},{10,... | collective-permute-start | bytes 1253384 | tf_op jit(solution)/shard_map/ppermute | solution.py:157
  8.5 11.2 %collective-permute-start.1 = (bf16[272,768]{1,0:T(8,128)(2,1)S(1)}, bf16[272,768]{1,0:T(8,128)(2,1)S(1)}, u32[]{:S(2)}, u32[]{:S(2)}) collective-permute-start(bf16[272,768]{1,0:T(8,128)(2,1)S(1)} %pack.1.refs_0_.refs_3_.refs_5_), channel_id=1, source_target_pairs={{0,4},{1,5},{2,6},{3,7},{4,0},{5,1},{6,2},{7,3},{8,12},{9,13},{10,... | collective-permute-start | bytes 1253384 | tf_op jit(solution)/shard_map/ppermute | solution.py:157
  15.9 5.4 %collective-permute-start.5 = (bf16[272,768]{1,0:T(8,128)(2,1)S(1)}, bf16[272,768]{1,0:T(8,128)(2,1)S(1)}, u32[]{:S(2)}, u32[]{:S(2)}) collective-permute-start(bf16[272,768]{1,0:T(8,128)(2,1)S(1)} %pack.1.refs_0_.refs_3_.refs_5_), channel_id=1, source_target_pairs={{0,1},{1,0},{2,3},{3,2},{4,5},{5,4},{6,7},{7,6},{8,9},{9,8},{10,11... | collective-permute-start | bytes 1253384 | tf_op jit(solution)/shard_map/ppermute | solution.py:157
  15.9 5.4 %collective-permute-start.6 = (bf16[272,768]{1,0:T(8,128)(2,1)S(1)}, bf16[272,768]{1,0:T(8,128)(2,1)S(1)}, u32[]{:S(2)}, u32[]{:S(2)}) collective-permute-start(bf16[272,768]{1,0:T(8,128)(2,1)S(1)} %collective-permute-done.2.refs_5_.refs_7_), channel_id=1, source_target_pairs={{0,1},{1,0},{2,3},{3,2},{4,5},{5,4},{6,7},{7,6},{8,9},{9,8},{10,11... | collective-permute-start | bytes 1253384 | tf_op jit(solution)/shard_map/ppermute | solution.py:157
  16.4 13.4 %collective-permute-start.9 = (bf16[272,768]{1,0:T(8,128)(2,1)S(1)}, bf16[272,768]{1,0:T(8,128)(2,1)S(1)}, u32[]{:S(2)}, u32[]{:S(2)}) collective-permute-start(bf16[272,768]{1,0:T(8,128)(2,1)S(1)} %collective-permute-done.2.refs_5_.refs_7_), channel_id=1, source_target_pairs={{8,0},{16,8},{9,1},{17,9},{10,2},{18,10},{11,3},{19,11},{12,4},{20... | collective-permute-start | bytes 1253384 | tf_op jit(solution)/shard_map/ppermute | solution.py:172
  18.1 7.8 %collective-permute-start.4 = (bf16[144,768]{1,0:T(8,128)(2,1)S(1)}, bf16[144,768]{1,0:T(8,128)(2,1)S(1)}, u32[]{:S(2)}, u32[]{:S(2)}) collective-permute-start(bf16[144,768]{1,0:T(8,128)(2,1)S(1)} %slice.7), channel_id=1, source_target_pairs={{0,4},{1,5},{2,6},{3,7},{4,0},{5,1},{6,2},{7,3},{8,12},{9,13},{10,... | collective-permute-start | bytes 663560 | tf_op jit(solution)/shard_map/ppermute | solution.py:157
  19.7 6.2 %collective-permute-start.3 = (bf16[128,768]{1,0:T(8,128)(2,1)S(1)}, bf16[128,768]{1,0:T(8,128)(2,1)S(1)}, u32[]{:S(2)}, u32[]{:S(2)}) collective-permute-start(bf16[128,768]{1,0:T(8,128)(2,1)S(1)} %slice.6), channel_id=1, source_target_pairs={{0,2},{1,3},{2,0},{3,1},{4,6},{5,7},{6,4},{7,5},{8,10},{9,11},{10,... | collective-permute-start | bytes 589832 | tf_op jit(solution)/shard_map/ppermute | solution.py:157
  26.6 1.2 %collective-permute-start.7 = (f32[2,1,256]{2,1,0:T(1,128)S(1)}, f32[2,1,256]{2,1,0:T(1,128)S(1)}, u32[]{:S(2)}, u32[]{:S(2)}) collective-permute-start(f32[2,1,256]{2,1,0:T(1,128)S(1)} %get-tuple-element.33), channel_id=1, source_target_pairs={{0,1},{1,0},{2,3},{3,2},{4,5},{5,4},{6,7},{7,6},{8,9},{9,8},{10,11... | collective-permute-start | bytes 6152 | tf_op jit(solution)/shard_map/ppermute | solution.py:157
  29.8 5.4 %collective-permute-start.11 = (bf16[272,768]{1,0:T(8,128)(2,1)S(1)}, bf16[272,768]{1,0:T(8,128)(2,1)S(1)}, u32[]{:S(2)}, u32[]{:S(2)}) collective-permute-start(bf16[272,768]{1,0:T(8,128)(2,1)S(1)} %collective-permute-done.9.refs_5_), channel_id=1, source_target_pairs={{0,1},{1,0},{2,3},{3,2},{4,5},{5,4},{6,7},{7,6},{8,9},{9,8},{10,11... | collective-permute-start | bytes 1253384 | tf_op jit(solution)/shard_map/ppermute | solution.py:157
  29.8 5.4 %collective-permute-start.8 = (f32[1,256]{1,0:T(1,128)S(1)}, f32[1,256]{1,0:T(1,128)S(1)}, u32[]{:S(2)}, u32[]{:S(2)}) collective-permute-start(f32[1,256]{1,0:T(1,128)S(1)} %get-tuple-element.35), channel_id=1, source_target_pairs={{0,8},{8,16},{16,24},{24,0},{1,9},{9,17},{17,25},{25,1},{2,10},{10... | collective-permute-start | bytes 3080 | tf_op jit(solution)/shard_map/ppermute | solution.py:163
  31.1 4.8 %collective-permute-start.10 = (f32[1,256]{1,0:T(1,128)S(1)}, f32[1,256]{1,0:T(1,128)S(1)}, u32[]{:S(2)}, u32[]{:S(2)}) collective-permute-start(f32[1,256]{1,0:T(1,128)S(1)} %bitcast.18), channel_id=1, source_target_pairs={{0,16},{8,24},{16,0},{24,8},{1,17},{9,25},{17,1},{25,9},{2,18},{10... | collective-permute-start | bytes 3080 | tf_op jit(solution)/shard_map/ppermute | solution.py:163
  35.9 3.7 %collective-permute-start.13 = (f32[2,1,256]{2,1,0:T(1,128)S(1)}, f32[2,1,256]{2,1,0:T(1,128)S(1)}, u32[]{:S(2)}, u32[]{:S(2)}) collective-permute-start(f32[2,1,256]{2,1,0:T(1,128)S(1)} %get-tuple-element.44), channel_id=1, source_target_pairs={{0,2},{1,3},{2,0},{3,1},{4,6},{5,7},{6,4},{7,5},{8,10},{9,11},{10,... | collective-permute-start | bytes 6152 | tf_op jit(solution)/shard_map/ppermute | solution.py:157
  37.5 3.9 %collective-permute-start.12 = (f32[1,256]{1,0:T(1,128)S(1)}, f32[1,256]{1,0:T(1,128)S(1)}, u32[]{:S(2)}, u32[]{:S(2)}) collective-permute-start(f32[1,256]{1,0:T(1,128)S(1)} %bitcast.17), channel_id=1, source_target_pairs={{0,17},{1,16},{2,19},{3,18},{4,21},{5,20},{6,23},{7,22},{8,25},{9,... | collective-permute-start | bytes 3080 | tf_op jit(solution)/shard_map/ppermute | solution.py:167
  39.6 3.6 %collective-permute-start.14 = (f32[1,1,256]{2,1,0:T(1,128)S(1)}, f32[1,1,256]{2,1,0:T(1,128)S(1)}, u32[]{:S(2)}, u32[]{:S(2)}) collective-permute-start(f32[1,1,256]{2,1,0:T(1,128)S(1)} %get-tuple-element.46), channel_id=1, source_target_pairs={{0,4},{1,5},{2,6},{3,7},{4,0},{5,1},{6,2},{7,3},{8,12},{9,13},{10,... | collective-permute-start | bytes 3080 | tf_op jit(solution)/shard_map/ppermute | solution.py:157
where the time goes:
time: 43.9 us; the launch traced here: 43.7 us
  starting transfers between devices  18.8 us (43%)
  waiting for transfers between devices  18.8 us (43%)
  Pallas kernels  3.83 us (9%)
  local copies, waits for them, and re-layouts  1.72 us (4%)
  other arithmetic  0.57 us (1%)
    ppermute x10, starting transfers between devices, plane_shift(): return lax.ppermute(x, 'blk', [(i, i ^ mask) for i in range(size)])  9.81 us
    ppermute x10, waiting for transfers between devices, plane_shift(): return lax.ppermute(x, 'blk', [(i, i ^ mask) for i in range(size)])  8.56 us
    ppermute x3, waiting for transfers between devices, grp_shift(): lax.ppermute(x, 'grp', [(z, (z + shift) % groups) for z in range(groups)])  7.96 us
    ppermute x3, starting transfers between devices, grp_shift(): lax.ppermute(x, 'grp', [(z, (z + shift) % groups) for z in range(groups)])  7.67 us
    pallas_call x4, Pallas kernels, score(): pl.pallas_call(kernel, out_shape=[jax.ShapeDtypeStruct((count, 1, rows),...  3.66 us
    ppermute x1, waiting for transfers between devices, relay_half_way(): lax.ppermute(x, 'grp', [((z + 1) % groups, z) for z in range(groups // 2)])  1.98 us
    unnamed x6, local copies, waits for them, and re-layouts  1.69 us
    ppermute x1, starting transfers between devices, relay_half_way(): lax.ppermute(x, 'grp', [((z + 1) % groups, z) for z in range(groups // 2)])  1.28 us
  transfers between devices with their start and end apart: 15, of which 9 were waited for; matrix products, arithmetic and copies ran while one was open for 0% of the time, Pallas kernels for 8%

commit v1 on v0

--- a/solution.py
+++ b/solution.py
@@ -169,7 +169,7 @@
 
 def relay_half_way(x):
     groups = lax.axis_size("grp")
-    return lax.ppermute(x, "grp", [((z + 1) % groups, z) for z in range(groups // 2)])
+    return lax.ppermute(x, "grp", [(z - 1, z) for z in range(groups // 2, groups)])
 
 
 def fetch_plane(packed, per_group, first):
@@ -196,20 +196,20 @@
     groups = lax.axis_size("grp")
     per_group = lax.axis_size("blk")
     packed = pack(embeddings, target, cluster, per_group)
-    next_one = grp_shift(packed, -1)
-    half_way = relay_half_way(next_one)
-    blocks = fetch_plane(packed, per_group, next_one)
+    one_off = grp_shift(packed, 1)
+    half_way = relay_half_way(one_off)
+    blocks = fetch_plane(packed, per_group, one_off)
     plane = list(blocks.values())
     n_direct = sum(len(pieces) == 1 for pieces in plane)
     places = tuple(mask // 2 for mask in blocks)
     every = range(len(plane))
 
-    own_then = lax.optimization_barrier((packed, next_one))[0]
-    cols = [packed, plane_shift(own_then, 1), next_one, plane_shift(next_one, 1)]
+    own_then = lax.optimization_barrier((packed, one_off))[0]
+    cols = [packed, plane_shift(own_then, 1), one_off, plane_shift(one_off, 1)]
     pairs = [(k, at, k == at == 0) for k in every for at in range(4)]
     early = [pair for pair in pairs if pair[0] < n_direct]
     best, rows_best = score("compare_direct", plane[:n_direct], cols, early, (2, 3), [(0, 1, 2, 3)])
-    own, next_best, twins, rows_best = score(
+    own, one_off_best, twins, rows_best = score(
         "compare_relayed",
         plane,
         cols,
@@ -221,19 +221,17 @@
         rows_known=range(n_direct),
         rows_in=[rows_best],
     )
-    own, next_best = join([own, next_best], plane_shift(twins, 1))
-    found = [own, grp_shift(next_best, 1)]
+    own, one_off_best = join([own, one_off_best], plane_shift(twins, 1))
+    found = [own, grp_shift(one_off_best, -1)]
 
     half_then = lax.optimization_barrier((half_way, own))[0]
     half_twin = plane_shift(half_then, 1)
     rest = dict(pairs=[(k, 0, False) for k in every], want_rows=(0,), outs=[(0,)], rows_known=every)
     half_best, rows_best = score("compare_half_way", plane, [half_way], rows_in=[rows_best], **rest)
     found.append(grp_shift(half_best.reshape(1, -1), groups // 2))
-    half_twin = lax.optimization_barrier((half_twin, found[1]))[0]
     twin_best, even, odd = score("compare_twin", plane, [half_twin], rows_in=[rows_best], places=places, **rest)
     found.append(grp_shift(twin_best.reshape(1, -1), groups // 2, 1))
 
-    odd = lax.optimization_barrier((odd, found[2]))[0]
     mask = 2
     while len(even) > 1:
         even, odd = halve(even, plane_shift(odd, mask))

time: 43.9 us -> 41.6 us (0.948)
  waiting for transfers between devices: 18.8 us -> 16.3 us
    ppermute x10, waiting for transfers between devices: 8.56 us -> 5.84 us  [plane_shift(): return lax.ppermute(x, 'blk', [(i, i ^ mask) for i in range(size)])]
    ppermute x1, waiting for transfers between devices: 1.98 us -> 0.01 us  [relay_half_way(): lax.ppermute(x, 'grp', [(z - 1, z) for z in range(groups // 2, groups)])]
    ppermute x1, waiting for transfers between devices: 0.28 us -> 1.69 us  [grp_shift(): return lax.ppermute(x, ('grp', 'blk'), pairs)]
    ppermute x3, waiting for transfers between devices: 7.96 us -> 8.76 us  [grp_shift(): lax.ppermute(x, 'grp', [(z, (z + shift) % groups) for z in range(groups)])]
    ppermute x1, starting transfers between devices: 1.28 us -> 0.68 us  [relay_half_way(): lax.ppermute(x, 'grp', [(z - 1, z) for z in range(groups // 2, groups)])]
    ppermute x1, starting transfers between devices: 0.01 us -> 0.57 us  [grp_shift(): return lax.ppermute(x, ('grp', 'blk'), pairs)]
  transfers between devices with their start and end apart: 15 -> 15, of which waited for: 9 -> 7; matrix products, arithmetic and copies ran while one was open for 0% -> 0% of each run, Pallas kernels for 8% -> 7%
where the time goes in v1:
time: 41.6 us; the launch traced here: 41.4 us
  starting transfers between devices  18.9 us (45%)
  waiting for transfers between devices  16.3 us (39%)
  Pallas kernels  3.82 us (9%)
  local copies, waits for them, and re-layouts  1.72 us (4%)
  other arithmetic  0.57 us (1%)
    ppermute x10, starting transfers between devices, plane_shift(): return lax.ppermute(x, 'blk', [(i, i ^ mask) for i in range(size)])  10 us
    ppermute x3, waiting for transfers between devices, grp_shift(): lax.ppermute(x, 'grp', [(z, (z + shift) % groups) for z in range(groups)])  8.76 us
    ppermute x3, starting transfers between devices, grp_shift(): lax.ppermute(x, 'grp', [(z, (z + shift) % groups) for z in range(groups)])  7.69 us
    ppermute x10, waiting for transfers between devices, plane_shift(): return lax.ppermute(x, 'blk', [(i, i ^ mask) for i in range(size)])  5.84 us
    pallas_call x4, Pallas kernels, score(): pl.pallas_call(kernel, out_shape=[jax.ShapeDtypeStruct((count, 1, rows),...  3.65 us
    ppermute x1, waiting for transfers between devices, grp_shift(): return lax.ppermute(x, ('grp', 'blk'), pairs)  1.69 us
    unnamed x6, local copies, waits for them, and re-layouts  1.69 us
  transfers between devices with their start and end apart: 15, of which 7 were waited for; matrix products, arithmetic and copies ran while one was open for 0% of the time, Pallas kernels for 7%

profile of v1, /device:TPU:0, one launch (start us, length us, event | category | flops | bytes accessed | tf_op | source)
XLA Modules:
  0.0 41.4 jit_solution(9045202853163778518)
XLA Ops:
  0.0 0.7 %copy-done.2 = s32[256]{0:T(256)S(1)} copy-done((s32[256]{0:T(256)S(1)}, s32[256]{0:T(256)}, u32[]{:S(2)}) %copy-start.2) | copy-done | bytes 1048
  0.7 0.0 copy-done.1
  0.7 1.0 %copy-done = bf16[256,768]{1,0:T(8,128)(2,1)S(1)} copy-done((bf16[256,768]{1,0:T(8,128)(2,1)S(1)}, bf16[256,768]{1,0:T(8,128)(2,1)}, u32[]{:S(2)}) %copy-start) | copy-done | bytes 393240
  1.7 0.2 pack.1.refs_0_.refs_3_.refs_5_
  1.9 3.1 %collective-permute-start.2 = (bf16[272,768]{1,0:T(8,128)(2,1)S(1)}, bf16[272,768]{1,0:T(8,128)(2,1)S(1)}, u32[]{:S(2)}, u32[]{:S(2)}) collective-permute-start(bf16[272,768]{1,0:T(8,128)(2,1)S(1)} %pack.1.refs_0_.refs_3_.refs_5_), channel_id=1, source_target_pairs={{0,8},{8,16},{16,24},{24,0},{1,9},{9,17},{17,25},{25,1},{2,10},{10... | collective-permute-start | bytes 1253384 | tf_op jit(solution)/shard_map/ppermute | solution.py:163
  4.9 1.5 %collective-permute-start = (bf16[272,768]{1,0:T(8,128)(2,1)S(1)}, bf16[272,768]{1,0:T(8,128)(2,1)S(1)}, u32[]{:S(2)}, u32[]{:S(2)}) collective-permute-start(bf16[272,768]{1,0:T(8,128)(2,1)S(1)} %pack.1.refs_0_.refs_3_.refs_5_), channel_id=1, source_target_pairs={{0,2},{1,3},{2,0},{3,1},{4,6},{5,7},{6,4},{7,5},{8,10},{9,11},{10,... | collective-permute-start | bytes 1253384 | tf_op jit(solution)/shard_map/ppermute | solution.py:157
  6.4 1.5 %collective-permute-start.1 = (bf16[272,768]{1,0:T(8,128)(2,1)S(1)}, bf16[272,768]{1,0:T(8,128)(2,1)S(1)}, u32[]{:S(2)}, u32[]{:S(2)}) collective-permute-start(bf16[272,768]{1,0:T(8,128)(2,1)S(1)} %pack.1.refs_0_.refs_3_.refs_5_), channel_id=1, source_target_pairs={{0,4},{1,5},{2,6},{3,7},{4,0},{5,1},{6,2},{7,3},{8,12},{9,13},{10,... | collective-permute-start | bytes 1253384 | tf_op jit(solution)/shard_map/ppermute | solution.py:157
  7.9 8.7 %collective-permute-done.2.refs_5_.refs_7_ = bf16[272,768]{1,0:T(8,128)(2,1)S(1)} collective-permute-done((bf16[272,768]{1,0:T(8,128)(2,1)S(1)}, bf16[272,768]{1,0:T(8,128)(2,1)S(1)}, u32[]{:S(2)}, u32[]{:S(2)}) %collective-permute-start.2) | collective-permute-done | bytes 417824 | tf_op jit(solution)/shard_map/ppermute | solution.py:163
  16.6 0.0 collective-permute-start.5
  16.6 0.5 %collective-permute-start.6 = (bf16[272,768]{1,0:T(8,128)(2,1)S(1)}, bf16[272,768]{1,0:T(8,128)(2,1)S(1)}, u32[]{:S(2)}, u32[]{:S(2)}) collective-permute-start(bf16[272,768]{1,0:T(8,128)(2,1)S(1)} %collective-permute-done.2.refs_5_.refs_7_), channel_id=1, source_target_pairs={{0,1},{1,0},{2,3},{3,2},{4,5},{5,4},{6,7},{7,6},{8,9},{9,8},{10,11... | collective-permute-start | bytes 1253384 | tf_op jit(solution)/shard_map/ppermute | solution.py:157
  17.1 0.7 %collective-permute-start.9 = (bf16[272,768]{1,0:T(8,128)(2,1)S(1)}, bf16[272,768]{1,0:T(8,128)(2,1)S(1)}, u32[]{:S(2)}, u32[]{:S(2)}) collective-permute-start(bf16[272,768]{1,0:T(8,128)(2,1)S(1)} %collective-permute-done.2.refs_5_.refs_7_), channel_id=1, source_target_pairs={{8,16},{16,24},{9,17},{17,25},{10,18},{18,26},{11,19},{19,27},{12,... | collective-permute-start | bytes 1253384 | tf_op jit(solution)/shard_map/ppermute | solution.py:172
  17.8 1.6 %collective-permute-start.4 = (bf16[144,768]{1,0:T(8,128)(2,1)S(1)}, bf16[144,768]{1,0:T(8,128)(2,1)S(1)}, u32[]{:S(2)}, u32[]{:S(2)}) collective-permute-start(bf16[144,768]{1,0:T(8,128)(2,1)S(1)} %slice.7), channel_id=1, source_target_pairs={{0,4},{1,5},{2,6},{3,7},{4,0},{5,1},{6,2},{7,3},{8,12},{9,13},{10,... | collective-permute-start | bytes 663560 | tf_op jit(solution)/shard_map/ppermute | solution.py:157
  19.4 1.6 %collective-permute-start.3 = (bf16[128,768]{1,0:T(8,128)(2,1)S(1)}, bf16[128,768]{1,0:T(8,128)(2,1)S(1)}, u32[]{:S(2)}, u32[]{:S(2)}) collective-permute-start(bf16[128,768]{1,0:T(8,128)(2,1)S(1)} %slice.6), channel_id=1, source_target_pairs={{0,2},{1,3},{2,0},{3,1},{4,6},{5,7},{6,4},{7,5},{8,10},{9,11},{10,... | collective-permute-start | bytes 589832 | tf_op jit(solution)/shard_map/ppermute | solution.py:157
  21.0 0.0 collective-permute-done.5.refs_4_.refs_6_
  21.0 1.5 %compare_direct.1 = (f32[4,1,256]{2,1,0:T(1,128)S(1)}, f32[3,1,256]{2,1,0:T(1,128)S(1)}) custom-call(bf16[272,768]{1,0:T(8,128)(2,1)S(1)} %pack.1.refs_0_.refs_3_.refs_5_, bf16[272,768]{1,0:T(8,128)(2,1)S(1)} %collective-permute-done.refs_1_, bf16[272,768]{1,0:T(8,128)(2,1)S(1)} %collective-permute-done.1.refs_2_, ...), custom_call_target="tpu_custom_call" | custom-call | flops 1207959552 | bytes 2924544 | tf_op jit(solution)/shard_map/compare_direct/pallas_call | solution.py:112
  22.5 3.5 %collective-permute-done.3.refs_3_ = bf16[128,768]{1,0:T(8,128)(2,1)S(1)} collective-permute-done((bf16[128,768]{1,0:T(8,128)(2,1)S(1)}, bf16[128,768]{1,0:T(8,128)(2,1)S(1)}, u32[]{:S(2)}, u32[]{:S(2)}) %collective-permute-start.3) | collective-permute-done | bytes 196640 | tf_op jit(solution)/shard_map/ppermute | solution.py:157
  26.0 0.7 %compare_relayed.1 = (f32[1,1,256]{2,1,0:T(1,128)S(1)}, f32[1,1,256]{2,1,0:T(1,128)S(1)}, f32[2,1,256]{2,1,0:T(1,128)S(1)}, f32[4,1,256]{2,1,0:T(1,128)S(1)}) custom-call(bf16[272,768]{1,0:T(8,128)(2,1)S(1)} %pack.1.refs_0_.refs_3_.refs_5_, bf16[272,768]{1,0:T(8,128)(2,1)S(1)} %collective-permute-done.refs_1_, ...), custom_call_target="tpu_custom_call" | custom-call | flops 402653184 | bytes 3342336 | tf_op jit(solution)/shard_map/compare_relayed/pallas_call | solution.py:112
  26.7 0.1 collective-permute-start.7
  26.8 1.1 %collective-permute-done.7.refs_2_ = f32[2,1,256]{2,1,0:T(1,128)S(1)} collective-permute-done((f32[2,1,256]{2,1,0:T(1,128)S(1)}, f32[2,1,256]{2,1,0:T(1,128)S(1)}, u32[]{:S(2)}, u32[]{:S(2)}) %collective-permute-start.7) | collective-permute-done | bytes 2080 | tf_op jit(solution)/shard_map/ppermute | solution.py:157
  28.0 0.2 collective-permute-start.11
  28.1 0.7 %compare_half_way.1 = (f32[1,1,256]{2,1,0:T(1,128)S(1)}, f32[4,1,256]{2,1,0:T(1,128)S(1)}) custom-call(bf16[272,768]{1,0:T(8,128)(2,1)S(1)} %pack.1.refs_0_.refs_3_.refs_5_, bf16[272,768]{1,0:T(8,128)(2,1)S(1)} %collective-permute-done.refs_1_, bf16[272,768]{1,0:T(8,128)(2,1)S(1)} %collective-permute-done.1.refs_2_, ...), custom_call_target="tpu_custom_call" | custom-call | flops 402653184 | bytes 2088960 | tf_op jit(solution)/shard_map/compare_half_way/pallas_call | solution.py:112
  28.9 0.9 %collective-permute-done.11.refs_5_ = bf16[272,768]{1,0:T(8,128)(2,1)S(1)} collective-permute-done((bf16[272,768]{1,0:T(8,128)(2,1)S(1)}, bf16[272,768]{1,0:T(8,128)(2,1)S(1)}, u32[]{:S(2)}, u32[]{:S(2)}) %collective-permute-start.11) | collective-permute-done | bytes 417824 | tf_op jit(solution)/shard_map/ppermute | solution.py:157
  29.8 0.7 %compare_twin.1 = (f32[1,1,256]{2,1,0:T(1,128)S(1)}, f32[2,1,256]{2,1,0:T(1,128)S(1)}, f32[2,1,256]{2,1,0:T(1,128)S(1)}) custom-call(bf16[272,768]{1,0:T(8,128)(2,1)S(1)} %pack.1.refs_0_.refs_3_.refs_5_, bf16[272,768]{1,0:T(8,128)(2,1)S(1)} %collective-permute-done.refs_1_, bf16[272,768]{1,0:T(8,128)(2,1)S(1)} %collective-permute-done.1.refs_2_, ...), custom_call_target="tpu_custom_call" | custom-call | flops 402653184 | bytes 2088960 | tf_op jit(solution)/shard_map/compare_twin/pallas_call | solution.py:112
  30.5 1.6 %collective-permute-start.13 = (f32[2,1,256]{2,1,0:T(1,128)S(1)}, f32[2,1,256]{2,1,0:T(1,128)S(1)}, u32[]{:S(2)}, u32[]{:S(2)}) collective-permute-start(f32[2,1,256]{2,1,0:T(1,128)S(1)} %get-tuple-element.40), channel_id=1, source_target_pairs={{0,2},{1,3},{2,0},{3,1},{4,6},{5,7},{6,4},{7,5},{8,10},{9,11},{10,... | collective-permute-start | bytes 6152 | tf_op jit(solution)/shard_map/ppermute | solution.py:157
  32.1 3.2 %collective-permute-start.10 = (f32[1,256]{1,0:T(1,128)S(1)}, f32[1,256]{1,0:T(1,128)S(1)}, u32[]{:S(2)}, u32[]{:S(2)}) collective-permute-start(f32[1,256]{1,0:T(1,128)S(1)} %bitcast.17), channel_id=1, source_target_pairs={{0,16},{8,24},{16,0},{24,8},{1,17},{9,25},{17,1},{25,9},{2,18},{10... | collective-permute-start | bytes 3080 | tf_op jit(solution)/shard_map/ppermute | solution.py:163
  35.3 1.4 %collective-permute-start.8 = (f32[1,256]{1,0:T(1,128)S(1)}, f32[1,256]{1,0:T(1,128)S(1)}, u32[]{:S(2)}, u32[]{:S(2)}) collective-permute-start(f32[1,256]{1,0:T(1,128)S(1)} %get-tuple-element.33), channel_id=1, source_target_pairs={{0,24},{8,0},{16,8},{24,16},{1,25},{9,1},{17,9},{25,17},{2,26},{10... | collective-permute-start | bytes 3080 | tf_op jit(solution)/shard_map/ppermute | solution.py:163
  36.7 0.6 %collective-permute-start.12 = (f32[1,256]{1,0:T(1,128)S(1)}, f32[1,256]{1,0:T(1,128)S(1)}, u32[]{:S(2)}, u32[]{:S(2)}) collective-permute-start(f32[1,256]{1,0:T(1,128)S(1)} %bitcast.18), channel_id=1, source_target_pairs={{0,17},{1,16},{2,19},{3,18},{4,21},{5,20},{6,23},{7,22},{8,25},{9,... | collective-permute-start | bytes 3080 | tf_op jit(solution)/shard_map/ppermute | solution.py:167
  37.3 1.5 %collective-permute-start.14 = (f32[1,1,256]{2,1,0:T(1,128)S(1)}, f32[1,1,256]{2,1,0:T(1,128)S(1)}, u32[]{:S(2)}, u32[]{:S(2)}) collective-permute-start(f32[1,1,256]{2,1,0:T(1,128)S(1)} %get-tuple-element.42), channel_id=1, source_target_pairs={{0,4},{1,5},{2,6},{3,7},{4,0},{5,1},{6,2},{7,3},{8,12},{9,13},{10,... | collective-permute-start | bytes 3080 | tf_op jit(solution)/shard_map/ppermute | solution.py:157
  38.8 0.1 collective-permute-done.8
  38.9 1.7 %collective-permute-done.12 = f32[1,256]{1,0:T(1,128)S(1)} collective-permute-done((f32[1,256]{1,0:T(1,128)S(1)}, f32[1,256]{1,0:T(1,128)S(1)}, u32[]{:S(2)}, u32[]{:S(2)}) %collective-permute-start.12) | collective-permute-done | bytes 1056 | tf_op jit(solution)/shard_map/ppermute | solution.py:167
  40.6 0.3 collective-permute-done.14
  40.8 0.6 %bitcast_maximum_fusion = f32[1,256]{1,0:T(1,128)} fusion(f32[1,1,256]{2,1,0:T(1,128)S(1)} %collective-permute-done.14, f32[1,1,256]{2,1,0:T(1,128)S(1)} %get-tuple-element.41, f32[1,256]{1,0:T(1,128)S(1)} %collective-permute-done.12, f32[1,256]{1,0:T(1,128)S(1)} %collective-permute-done.10, f32[1,256]{1,0:T(1,128)S(1)} %get-tuple-element.32, ...), kind=kLoop, calls=%fused_computation | loop fusion | flops 1280 | bytes 7168 | tf_op jit(solution)/shard_map/max | solution.py:240
  (14 shorter events, 0.1 us)
Async XLA Ops:
  0.0 0.7 %copy-start.2 = (s32[256]{0:T(256)S(1)}, s32[256]{0:T(256)}, u32[]{:S(2)}) copy-start(s32[256]{0:T(256)} %param.5) | copy-start | bytes 3076
  0.0 0.7 %copy-start.1 = (s32[256,1]{0,1:T(1,128)S(1)}, s32[256,1]{0,1:T(1,128)}, u32[]{:S(2)}) copy-start(s32[256,1]{0,1:T(1,128)} %param.4) | copy-start | bytes 3076
  0.7 1.0 %copy-start = (bf16[256,768]{1,0:T(8,128)(2,1)S(1)}, bf16[256,768]{1,0:T(8,128)(2,1)}, u32[]{:S(2)}) copy-start(bf16[256,768]{1,0:T(8,128)(2,1)} %emb_ref.1) | copy-start | bytes 1179652
  1.9 14.7 %collective-permute-start.2 = (bf16[272,768]{1,0:T(8,128)(2,1)S(1)}, bf16[272,768]{1,0:T(8,128)(2,1)S(1)}, u32[]{:S(2)}, u32[]{:S(2)}) collective-permute-start(bf16[272,768]{1,0:T(8,128)(2,1)S(1)} %pack.1.refs_0_.refs_3_.refs_5_), channel_id=1, source_target_pairs={{0,8},{8,16},{16,24},{24,0},{1,9},{9,17},{17,25},{25,1},{2,10},{10... | collective-permute-start | bytes 1253384 | tf_op jit(solution)/shard_map/ppermute | solution.py:163
  4.9 12.9 %collective-permute-start = (bf16[272,768]{1,0:T(8,128)(2,1)S(1)}, bf16[272,768]{1,0:T(8,128)(2,1)S(1)}, u32[]{:S(2)}, u32[]{:S(2)}) collective-permute-start(bf16[272,768]{1,0:T(8,128)(2,1)S(1)} %pack.1.refs_0_.refs_3_.refs_5_), channel_id=1, source_target_pairs={{0,2},{1,3},{2,0},{3,1},{4,6},{5,7},{6,4},{7,5},{8,10},{9,11},{10,... | collective-permute-start | bytes 1253384 | tf_op jit(solution)/shard_map/ppermute | solution.py:157
  6.4 13.0 %collective-permute-start.1 = (bf16[272,768]{1,0:T(8,128)(2,1)S(1)}, bf16[272,768]{1,0:T(8,128)(2,1)S(1)}, u32[]{:S(2)}, u32[]{:S(2)}) collective-permute-start(bf16[272,768]{1,0:T(8,128)(2,1)S(1)} %pack.1.refs_0_.refs_3_.refs_5_), channel_id=1, source_target_pairs={{0,4},{1,5},{2,6},{3,7},{4,0},{5,1},{6,2},{7,3},{8,12},{9,13},{10,... | collective-permute-start | bytes 1253384 | tf_op jit(solution)/shard_map/ppermute | solution.py:157
  16.6 4.4 %collective-permute-start.5 = (bf16[272,768]{1,0:T(8,128)(2,1)S(1)}, bf16[272,768]{1,0:T(8,128)(2,1)S(1)}, u32[]{:S(2)}, u32[]{:S(2)}) collective-permute-start(bf16[272,768]{1,0:T(8,128)(2,1)S(1)} %pack.1.refs_0_.refs_3_.refs_5_), channel_id=1, source_target_pairs={{0,1},{1,0},{2,3},{3,2},{4,5},{5,4},{6,7},{7,6},{8,9},{9,8},{10,11... | collective-permute-start | bytes 1253384 | tf_op jit(solution)/shard_map/ppermute | solution.py:157
  16.6 4.4 %collective-permute-start.6 = (bf16[272,768]{1,0:T(8,128)(2,1)S(1)}, bf16[272,768]{1,0:T(8,128)(2,1)S(1)}, u32[]{:S(2)}, u32[]{:S(2)}) collective-permute-start(bf16[272,768]{1,0:T(8,128)(2,1)S(1)} %collective-permute-done.2.refs_5_.refs_7_), channel_id=1, source_target_pairs={{0,1},{1,0},{2,3},{3,2},{4,5},{5,4},{6,7},{7,6},{8,9},{9,8},{10,11... | collective-permute-start | bytes 1253384 | tf_op jit(solution)/shard_map/ppermute | solution.py:157
  17.1 10.8 %collective-permute-start.9 = (bf16[272,768]{1,0:T(8,128)(2,1)S(1)}, bf16[272,768]{1,0:T(8,128)(2,1)S(1)}, u32[]{:S(2)}, u32[]{:S(2)}) collective-permute-start(bf16[272,768]{1,0:T(8,128)(2,1)S(1)} %collective-permute-done.2.refs_5_.refs_7_), channel_id=1, source_target_pairs={{8,16},{16,24},{9,17},{17,25},{10,18},{18,26},{11,19},{19,27},{12,... | collective-permute-start | bytes 1253384 | tf_op jit(solution)/shard_map/ppermute | solution.py:172
  17.8 8.2 %collective-permute-start.4 = (bf16[144,768]{1,0:T(8,128)(2,1)S(1)}, bf16[144,768]{1,0:T(8,128)(2,1)S(1)}, u32[]{:S(2)}, u32[]{:S(2)}) collective-permute-start(bf16[144,768]{1,0:T(8,128)(2,1)S(1)} %slice.7), channel_id=1, source_target_pairs={{0,4},{1,5},{2,6},{3,7},{4,0},{5,1},{6,2},{7,3},{8,12},{9,13},{10,... | collective-permute-start | bytes 663560 | tf_op jit(solution)/shard_map/ppermute | solution.py:157
  19.4 6.6 %collective-permute-start.3 = (bf16[128,768]{1,0:T(8,128)(2,1)S(1)}, bf16[128,768]{1,0:T(8,128)(2,1)S(1)}, u32[]{:S(2)}, u32[]{:S(2)}) collective-permute-start(bf16[128,768]{1,0:T(8,128)(2,1)S(1)} %slice.6), channel_id=1, source_target_pairs={{0,2},{1,3},{2,0},{3,1},{4,6},{5,7},{6,4},{7,5},{8,10},{9,11},{10,... | collective-permute-start | bytes 589832 | tf_op jit(solution)/shard_map/ppermute | solution.py:157
  26.7 1.2 %collective-permute-start.7 = (f32[2,1,256]{2,1,0:T(1,128)S(1)}, f32[2,1,256]{2,1,0:T(1,128)S(1)}, u32[]{:S(2)}, u32[]{:S(2)}) collective-permute-start(f32[2,1,256]{2,1,0:T(1,128)S(1)} %get-tuple-element.31), channel_id=1, source_target_pairs={{0,1},{1,0},{2,3},{3,2},{4,5},{5,4},{6,7},{7,6},{8,9},{9,8},{10,11... | collective-permute-start | bytes 6152 | tf_op jit(solution)/shard_map/ppermute | solution.py:157
  28.0 1.8 %collective-permute-start.11 = (bf16[272,768]{1,0:T(8,128)(2,1)S(1)}, bf16[272,768]{1,0:T(8,128)(2,1)S(1)}, u32[]{:S(2)}, u32[]{:S(2)}) collective-permute-start(bf16[272,768]{1,0:T(8,128)(2,1)S(1)} %collective-permute-done.9.refs_5_), channel_id=1, source_target_pairs={{0,1},{1,0},{2,3},{3,2},{4,5},{5,4},{6,7},{7,6},{8,9},{9,8},{10,11... | collective-permute-start | bytes 1253384 | tf_op jit(solution)/shard_map/ppermute | solution.py:157
  30.5 6.7 %collective-permute-start.13 = (f32[2,1,256]{2,1,0:T(1,128)S(1)}, f32[2,1,256]{2,1,0:T(1,128)S(1)}, u32[]{:S(2)}, u32[]{:S(2)}) collective-permute-start(f32[2,1,256]{2,1,0:T(1,128)S(1)} %get-tuple-element.40), channel_id=1, source_target_pairs={{0,2},{1,3},{2,0},{3,1},{4,6},{5,7},{6,4},{7,5},{8,10},{9,11},{10,... | collective-permute-start | bytes 6152 | tf_op jit(solution)/shard_map/ppermute | solution.py:157
  32.1 6.7 %collective-permute-start.10 = (f32[1,256]{1,0:T(1,128)S(1)}, f32[1,256]{1,0:T(1,128)S(1)}, u32[]{:S(2)}, u32[]{:S(2)}) collective-permute-start(f32[1,256]{1,0:T(1,128)S(1)} %bitcast.17), channel_id=1, source_target_pairs={{0,16},{8,24},{16,0},{24,8},{1,17},{9,25},{17,1},{25,9},{2,18},{10... | collective-permute-start | bytes 3080 | tf_op jit(solution)/shard_map/ppermute | solution.py:163
  35.3 3.6 %collective-permute-start.8 = (f32[1,256]{1,0:T(1,128)S(1)}, f32[1,256]{1,0:T(1,128)S(1)}, u32[]{:S(2)}, u32[]{:S(2)}) collective-permute-start(f32[1,256]{1,0:T(1,128)S(1)} %get-tuple-element.33), channel_id=1, source_target_pairs={{0,24},{8,0},{16,8},{24,16},{1,25},{9,1},{17,9},{25,17},{2,26},{10... | collective-permute-start | bytes 3080 | tf_op jit(solution)/shard_map/ppermute | solution.py:163
  36.7 3.9 %collective-permute-start.12 = (f32[1,256]{1,0:T(1,128)S(1)}, f32[1,256]{1,0:T(1,128)S(1)}, u32[]{:S(2)}, u32[]{:S(2)}) collective-permute-start(f32[1,256]{1,0:T(1,128)S(1)} %bitcast.18), channel_id=1, source_target_pairs={{0,17},{1,16},{2,19},{3,18},{4,21},{5,20},{6,23},{7,22},{8,25},{9,... | collective-permute-start | bytes 3080 | tf_op jit(solution)/shard_map/ppermute | solution.py:167
  37.3 3.6 %collective-permute-start.14 = (f32[1,1,256]{2,1,0:T(1,128)S(1)}, f32[1,1,256]{2,1,0:T(1,128)S(1)}, u32[]{:S(2)}, u32[]{:S(2)}) collective-permute-start(f32[1,1,256]{2,1,0:T(1,128)S(1)} %get-tuple-element.42), channel_id=1, source_target_pairs={{0,4},{1,5},{2,6},{3,7},{4,0},{5,1},{6,2},{7,3},{8,12},{9,13},{10,... | collective-permute-start | bytes 3080 | tf_op jit(solution)/shard_map/ppermute | solution.py:157

commit v2 on v1

v2 whole, which is shorter than its diff:
```python
import functools

import jax
import jax.numpy as jnp
from jax import lax
from jax.experimental import pallas as pl
from jax.experimental.pallas import tpu as pltpu
from jax.sharding import PartitionSpec as P

CLUSTERS = 64
TAIL = 16
VMEM = 24 << 20
VMEM_SMALL = 8 << 20


def pack_kernel(per_group, emb_ref, target_ref, cluster_ref, out_ref):
    rows, width = emb_ref.shape
    x = emb_ref[...].astype(jnp.float32)
    scale = lax.rsqrt(jnp.sum(x * x, axis=1, keepdims=True) + 1e-06)
    out_ref[:rows, :] = (x * scale).astype(jnp.bfloat16)
    key = target_ref[...] // per_group * CLUSTERS + cluster_ref[...] + 1
    key = jnp.concatenate([key, jnp.zeros((1, width - rows), jnp.int32)], axis=1)
    key = jnp.broadcast_to(key.astype(jnp.float32), (TAIL, width))
    out_ref[rows:, :] = key.astype(jnp.bfloat16)


def pack(embeddings, target, cluster, per_group):
    rows, width = embeddings.shape
    return pl.pallas_call(
        functools.partial(pack_kernel, per_group),
        out_shape=jax.ShapeDtypeStruct((rows + TAIL, width), jnp.bfloat16),
        compiler_params=pltpu.CompilerParams(vmem_limit_bytes=VMEM_SMALL),
        name="pack",
    )(embeddings, target.reshape(1, rows), cluster.reshape(1, rows))


def whole(pieces):
    return pieces[0][...] if len(pieces) == 1 else jnp.concatenate([ref[...] for ref in pieces], axis=0)


def score_kernel(counts, n_cols, pairs, want_rows, known, outs, *refs):
    n_rows = len(counts) if want_rows else 0
    *plane, cols, cols_in, col_outs, row_outs = take(refs, counts + (n_cols, bool(known), len(outs), n_rows))
    rows = col_outs[0].shape[2]
    best = [jnp.full((1, rows), -1.0, jnp.float32)] * n_cols
    for at, col in enumerate(known):
        best[col] = cols_in[0][at]
    for k, pieces in enumerate(plane):
        block = whole(pieces)
        row_keys = jnp.transpose(jnp.broadcast_to(block[rows:, :rows].astype(jnp.float32)[:1], (128, rows)))
        row_keys = jnp.concatenate([row_keys] * (rows // 128), axis=1)
        row_best = None
        for at, same in [(at, same) for one, at, same in pairs if one == k]:
            scores = lax.dot_general(
                block[:rows], cols[at][:rows, :], (((1,), (1,)), ((), ())), preferred_element_type=jnp.float32
            )
            allowed = row_keys == cols[at][rows:, :rows].astype(jnp.float32)[:1]
            if same:
                one = lax.broadcasted_iota(jnp.int32, scores.shape, 0)
                other = lax.broadcasted_iota(jnp.int32, scores.shape, 1)
                allowed = allowed & (one != other)
            masked = jnp.where(allowed, scores, -1.0)
            best[at] = jnp.maximum(best[at], jnp.max(masked, axis=0, keepdims=True))
            if at in want_rows:
                for lane in range(0, rows, 128):
                    part = masked[:, lane : lane + 128]
                    row_best = part if row_best is None else jnp.maximum(row_best, part)
        if row_best is not None:
            row_outs[k][0] = jnp.max(jnp.transpose(row_best), axis=0, keepdims=True)
    for ref, held in zip(col_outs, outs):
        for at, col in enumerate(held):
            ref[at] = best[col]


def take(refs, counts):
    groups, at = [], 0
    for count in counts:
        groups.append(refs[at : at + count])
        at += count
    return groups


def score(name, plane, cols, pairs, want_rows, outs, known=(), cols_in=()):
    length, width = cols[0].shape
    rows = length - TAIL
    counts = tuple(len(pieces) for pieces in plane)
    kernel = functools.partial(
        score_kernel, counts, len(cols), tuple(pairs), tuple(want_rows), tuple(known), tuple(outs)
    )
    shapes = [len(held) for held in outs] + [1] * (len(plane) if want_rows else 0)
    return pl.pallas_call(
        kernel,
        out_shape=[jax.ShapeDtypeStruct((count, 1, rows), jnp.float32) for count in shapes],
        compiler_params=pltpu.CompilerParams(vmem_limit_bytes=VMEM),
        cost_estimate=pl.CostEstimate(
            flops=2 * len(pairs) * rows * rows * width,
            bytes_accessed=2 * (len(plane) + len(cols)) * length * width,
            transcendentals=0,
        ),
        name=name,
    )(*[piece for pieces in plane for piece in pieces], *cols, *cols_in)


def join_kernel(n, *refs):
    for at in range(n):
        refs[n + 1 + at][...] = jnp.maximum(refs[at][...], refs[n][at])


def join(here, got):
    return pl.pallas_call(
        functools.partial(join_kernel, len(here)),
        out_shape=[jax.ShapeDtypeStruct((1, x.shape[-1]), x.dtype) for x in here],
        compiler_params=pltpu.CompilerParams(vmem_limit_bytes=VMEM_SMALL),
        name="join",
    )(*[x.reshape(1, -1) for x in here], got)


def plane_shift(x, mask):
    size = lax.axis_size("blk")
    return lax.ppermute(x, "blk", [(i, i ^ mask) for i in range(size)])


def grp_shift(x, shift, mask=0):
    groups, size = lax.axis_size("grp"), lax.axis_size("blk")
    if not mask:
        return lax.ppermute(x, "grp", [(z, (z + shift) % groups) for z in range(groups)])
    pairs = [
        (z * size + i, (z + shift) % groups * size + (i ^ mask)) for z in range(groups) for i in range(size)
    ]
    return lax.ppermute(x, ("grp", "blk"), pairs)


def fetch_plane(packed, per_group):
    half = (packed.shape[0] - TAIL) // 2
    plane = {0: (packed,)}
    halves = {}
    for mask in sorted(range(2, per_group, 2), key=lambda mask: mask.bit_count()):
        low, high = mask & -mask, 1 << (mask.bit_length() - 1)
        if low == high:
            block = plane_shift(packed, mask)
            plane[mask] = (block,)
            halves[mask] = (block[:half], block[half:])
        else:
            plane[mask] = halves[mask] = (
                plane_shift(halves[mask ^ low][0], low),
                plane_shift(halves[mask ^ high][1], high),
            )
    return plane


def body(embeddings, target, cluster):
    groups = lax.axis_size("grp")
    per_group = lax.axis_size("blk")
    packed = pack(embeddings, target, cluster, per_group)
    one_off = grp_shift(packed, 1)
    plane = fetch_plane(packed, per_group)
    own_then = lax.optimization_barrier((packed, one_off))[0]
    own_twin = plane_shift(own_then, 1)
    half_way = grp_shift(one_off, 1)
    direct = [mask for mask, pieces in plane.items() if len(pieces) == 1]
    relayed = [mask for mask, pieces in plane.items() if len(pieces) > 1]

    cols = [packed, own_twin, one_off, plane_shift(one_off, 1)]
    every = range(len(cols))
    best, *rows_direct = score(
        "compare_direct",
        [plane[mask] for mask in direct],
        cols,
        [(k, at, k == at == 0) for k in range(len(direct)) for at in every],
        (2, 3),
        [tuple(every)],
    )
    early = [plane_shift(best, mask) for best, mask in zip(rows_direct[1:], direct[1:])]
    best = lax.optimization_barrier((best, early[0]))[0]
    own, one_off_best, twins, *rows_relayed = score(
        "compare_relayed",
        [plane[mask] for mask in relayed],
        cols,
        [(k, at, False) for k in range(len(relayed)) for at in every],
        (2, 3),
        [(0,), (2,), (1, 3)],
        known=every,
        cols_in=[best],
    )
    own, one_off_best = join([own, one_off_best], plane_shift(twins, 1))
    found = [own.reshape(1, 1, -1), rows_direct[0]]
    early += [plane_shift(best, mask) for best, mask in zip(rows_relayed, relayed)]
    found.append(grp_shift(one_off_best.reshape(1, 1, -1), -1))

    blocks = list(plane.values())
    pairs = [(k, 0, False) for k in range(len(blocks))]
    half_then = lax.optimization_barrier((half_way, own, early))[0]
    for name, block, mask in (("compare_half_way", half_way, 0), ("compare_twin", plane_shift(half_then, 1), 1)):
        (half_best,) = score(name, blocks, [block], pairs, (), [(0,)])
        found.append(grp_shift(half_best, groups // 2, mask))
    return functools.reduce(jnp.maximum, found + early).reshape(-1)


def solution(mesh):
    return jax.shard_map(
        body,
        mesh=mesh,
        in_specs=(P(("grp", "blk"), None), P(("grp", "blk"), None), P(("grp", "blk"))),
        out_specs=P(("grp", "blk")),
        check_vma=False,
    )
```

time: 41.6 us -> 41.2 us (level)
    ppermute x10 -> x11, waiting for transfers between devices: 5.84 us -> 3.96 us  [plane_shift(): return lax.ppermute(x, 'blk', [(i, i ^ mask) for i in range(size)])]
    ppermute x3 -> x4, waiting for transfers between devices: 8.76 us -> 9.91 us  [grp_shift(): lax.ppermute(x, 'grp', [(z, (z + shift) % groups) for z in range(groups)])]
    ppermute x1, starting transfers between devices: 0.57 us -> 1.58 us  [grp_shift(): return lax.ppermute(x, ('grp', 'blk'), pairs)]
    ppermute x3 -> x4, starting transfers between devices: 7.69 us -> 6.94 us  [grp_shift(): lax.ppermute(x, 'grp', [(z, (z + shift) % groups) for z in range(groups)])]
    ppermute x1, waiting for transfers between devices: 1.69 us -> 2.38 us  [grp_shift(): return lax.ppermute(x, ('grp', 'blk'), pairs)]
    ppermute x1 -> x0, starting transfers between devices: 0.68 us -> none  [relay_half_way(): lax.ppermute(x, 'grp', [(z - 1, z) for z in range(groups // 2, groups)])]
    ppermute x10 -> x11, starting transfers between devices: 10 us -> 10.3 us  [plane_shift(): return lax.ppermute(x, 'blk', [(i, i ^ mask) for i in range(size)])]
  transfers between devices with their start and end apart: 15 -> 16, of which waited for: 7 -> 5; matrix products, arithmetic and copies ran while one was open for 0% -> 0% of each run, Pallas kernels for 7% -> 8%
where the time goes in v2:
time: 41.2 us; the launch traced here: 41 us
  starting transfers between devices  18.8 us (46%)
  waiting for transfers between devices  16.2 us (39%)
  Pallas kernels  3.62 us (9%)
  local copies, waits for them, and re-layouts  1.72 us (4%)
  other arithmetic  0.57 us (1%)
    ppermute x11, starting transfers between devices, plane_shift(): return lax.ppermute(x, 'blk', [(i, i ^ mask) for i in range(size)])  10.3 us
    ppermute x4, waiting for transfers between devices, grp_shift(): lax.ppermute(x, 'grp', [(z, (z + shift) % groups) for z in range(groups)])  9.91 us
    ppermute x4, starting transfers between devices, grp_shift(): lax.ppermute(x, 'grp', [(z, (z + shift) % groups) for z in range(groups)])  6.94 us
    ppermute x11, waiting for transfers between devices, plane_shift(): return lax.ppermute(x, 'blk', [(i, i ^ mask) for i in range(size)])  3.96 us
    pallas_call x4, Pallas kernels, score(): pl.pallas_call(kernel, out_shape=[jax.ShapeDtypeStruct((count, 1, rows),...  3.45 us
    ppermute x1, waiting for transfers between devices, grp_shift(): return lax.ppermute(x, ('grp', 'blk'), pairs)  2.38 us
    unnamed x6, local copies, waits for them, and re-layouts  1.69 us
    ppermute x1, starting transfers between devices, grp_shift(): return lax.ppermute(x, ('grp', 'blk'), pairs)  1.58 us
  transfers between devices with their start and end apart: 16, of which 5 were waited for; matrix products, arithmetic and copies ran while one was open for 0% of the time, Pallas kernels for 8%

profile of v2, /device:TPU:0, one launch (start us, length us, event | category | flops | bytes accessed | tf_op | source)
XLA Modules:
  0.0 41.0 jit_solution(14164518243199673445)
XLA Ops:
  0.0 0.7 %copy-done.2 = s32[256]{0:T(256)S(1)} copy-done((s32[256]{0:T(256)S(1)}, s32[256]{0:T(256)}, u32[]{:S(2)}) %copy-start.2) | copy-done | bytes 1048
  0.7 0.0 copy-done.1
  0.7 1.0 %copy-done = bf16[256,768]{1,0:T(8,128)(2,1)S(1)} copy-done((bf16[256,768]{1,0:T(8,128)(2,1)S(1)}, bf16[256,768]{1,0:T(8,128)(2,1)}, u32[]{:S(2)}) %copy-start) | copy-done | bytes 393240
  1.7 0.2 pack.1.refs_0_.refs_3_.refs_2_
  1.9 3.1 %collective-permute-start.4 = (bf16[272,768]{1,0:T(8,128)(2,1)S(1)}, bf16[272,768]{1,0:T(8,128)(2,1)S(1)}, u32[]{:S(2)}, u32[]{:S(2)}) collective-permute-start(bf16[272,768]{1,0:T(8,128)(2,1)S(1)} %pack.1.refs_0_.refs_3_.refs_2_), channel_id=1, source_target_pairs={{0,8},{8,16},{16,24},{24,0},{1,9},{9,17},{17,25},{25,1},{2,10},{10... | collective-permute-start | bytes 1253384 | tf_op jit(solution)/shard_map/ppermute | solution.py:126
  4.9 1.5 %collective-permute-start.2 = (bf16[272,768]{1,0:T(8,128)(2,1)S(1)}, bf16[272,768]{1,0:T(8,128)(2,1)S(1)}, u32[]{:S(2)}, u32[]{:S(2)}) collective-permute-start(bf16[272,768]{1,0:T(8,128)(2,1)S(1)} %pack.1.refs_0_.refs_3_.refs_2_), channel_id=1, source_target_pairs={{0,2},{1,3},{2,0},{3,1},{4,6},{5,7},{6,4},{7,5},{8,10},{9,11},{10,... | collective-permute-start | bytes 1253384 | tf_op jit(solution)/shard_map/ppermute | solution.py:120
  6.4 1.5 %collective-permute-start = (bf16[272,768]{1,0:T(8,128)(2,1)S(1)}, bf16[272,768]{1,0:T(8,128)(2,1)S(1)}, u32[]{:S(2)}, u32[]{:S(2)}) collective-permute-start(bf16[272,768]{1,0:T(8,128)(2,1)S(1)} %pack.1.refs_0_.refs_3_.refs_2_), channel_id=1, source_target_pairs={{0,4},{1,5},{2,6},{3,7},{4,0},{5,1},{6,2},{7,3},{8,12},{9,13},{10,... | collective-permute-start | bytes 1253384 | tf_op jit(solution)/shard_map/ppermute | solution.py:120
  7.9 8.7 %collective-permute-done.4.refs_5_.refs_4_ = bf16[272,768]{1,0:T(8,128)(2,1)S(1)} collective-permute-done((bf16[272,768]{1,0:T(8,128)(2,1)S(1)}, bf16[272,768]{1,0:T(8,128)(2,1)S(1)}, u32[]{:S(2)}, u32[]{:S(2)}) %collective-permute-start.4) | collective-permute-done | bytes 417824 | tf_op jit(solution)/shard_map/ppermute | solution.py:126
  16.6 0.0 collective-permute-start.5
  16.6 0.5 %collective-permute-start.6 = (bf16[272,768]{1,0:T(8,128)(2,1)S(1)}, bf16[272,768]{1,0:T(8,128)(2,1)S(1)}, u32[]{:S(2)}, u32[]{:S(2)}) collective-permute-start(bf16[272,768]{1,0:T(8,128)(2,1)S(1)} %collective-permute-done.4.refs_5_.refs_4_), channel_id=1, source_target_pairs={{0,1},{1,0},{2,3},{3,2},{4,5},{5,4},{6,7},{7,6},{8,9},{9,8},{10,11... | collective-permute-start | bytes 1253384 | tf_op jit(solution)/shard_map/ppermute | solution.py:120
  17.1 1.6 %collective-permute-start.3 = (bf16[144,768]{1,0:T(8,128)(2,1)S(1)}, bf16[144,768]{1,0:T(8,128)(2,1)S(1)}, u32[]{:S(2)}, u32[]{:S(2)}) collective-permute-start(bf16[144,768]{1,0:T(8,128)(2,1)S(1)} %slice.9), channel_id=1, source_target_pairs={{0,4},{1,5},{2,6},{3,7},{4,0},{5,1},{6,2},{7,3},{8,12},{9,13},{10,... | collective-permute-start | bytes 663560 | tf_op jit(solution)/shard_map/ppermute | solution.py:120
  18.7 1.6 %collective-permute-start.1 = (bf16[128,768]{1,0:T(8,128)(2,1)S(1)}, bf16[128,768]{1,0:T(8,128)(2,1)S(1)}, u32[]{:S(2)}, u32[]{:S(2)}) collective-permute-start(bf16[128,768]{1,0:T(8,128)(2,1)S(1)} %slice.8), channel_id=1, source_target_pairs={{0,2},{1,3},{2,0},{3,1},{4,6},{5,7},{6,4},{7,5},{8,10},{9,11},{10,... | collective-permute-start | bytes 589832 | tf_op jit(solution)/shard_map/ppermute | solution.py:120
  20.3 0.0 collective-permute-done.5.refs_4_.refs_3_
  20.3 0.0 collective-permute-done.6.refs_6_.refs_5_
  20.3 1.5 %compare_direct.1 = (f32[4,1,256]{2,1,0:T(1,128)S(1)}, f32[1,1,256]{2,1,0:T(1,128)S(1)}, f32[1,1,256]{2,1,0:T(1,128)S(1)}, f32[1,1,256]{2,1,0:T(1,128)S(1)}) custom-call(bf16[272,768]{1,0:T(8,128)(2,1)S(1)} %pack.1.refs_0_.refs_3_.refs_2_, bf16[272,768]{1,0:T(8,128)(2,1)S(1)} %collective-permute-done.2.refs_1_, ...), custom_call_target="tpu_custom_call" | custom-call | flops 1207959552 | bytes 2924544 | tf_op jit(solution)/shard_map/compare_direct/pallas_call | solution.py:91
  21.8 0.6 %collective-permute-start.7 = (f32[1,1,256]{2,1,0:T(1,128)S(1)}, f32[1,1,256]{2,1,0:T(1,128)S(1)}, u32[]{:S(2)}, u32[]{:S(2)}) collective-permute-start(f32[1,1,256]{2,1,0:T(1,128)S(1)} %get-tuple-element.20), channel_id=1, source_target_pairs={{0,2},{1,3},{2,0},{3,1},{4,6},{5,7},{6,4},{7,5},{8,10},{9,11},{10,... | collective-permute-start | bytes 3080 | tf_op jit(solution)/shard_map/ppermute | solution.py:120
  22.4 3.0 %collective-permute-done.7 = f32[1,1,256]{2,1,0:T(1,128)S(1)} collective-permute-done((f32[1,1,256]{2,1,0:T(1,128)S(1)}, f32[1,1,256]{2,1,0:T(1,128)S(1)}, u32[]{:S(2)}, u32[]{:S(2)}) %collective-permute-start.7) | collective-permute-done | bytes 1056 | tf_op jit(solution)/shard_map/ppermute | solution.py:120
  25.5 0.7 %compare_relayed.1 = (f32[1,1,256]{2,1,0:T(1,128)S(1)}, f32[1,1,256]{2,1,0:T(1,128)S(1)}, f32[2,1,256]{2,1,0:T(1,128)S(1)}, f32[1,1,256]{2,1,0:T(1,128)S(1)}) custom-call(bf16[128,768]{1,0:T(8,128)(2,1)S(1)} %collective-permute-done.1.refs_0_.refs_3_, bf16[144,768]{1,0:T(8,128)(2,1)S(1)} %collective-permute-done.3.refs_1_.refs_4_, ...), custom_call_target="tpu_custom_call" | custom-call | flops 402653184 | bytes 2088960 | tf_op jit(solution)/shard_map/compare_relayed/pallas_call | solution.py:91
  26.2 0.1 collective-permute-start.8
  26.2 0.7 %collective-permute-start.12 = (f32[1,1,256]{2,1,0:T(1,128)S(1)}, f32[1,1,256]{2,1,0:T(1,128)S(1)}, u32[]{:S(2)}, u32[]{:S(2)}) collective-permute-start(f32[1,1,256]{2,1,0:T(1,128)S(1)} %get-tuple-element.28), channel_id=1, source_target_pairs={{0,4},{1,5},{2,6},{3,7},{4,0},{5,1},{6,2},{7,3},{8,12},{9,13},{10,... | collective-permute-start | bytes 3080 | tf_op jit(solution)/shard_map/ppermute | solution.py:120
  26.9 2.3 %collective-permute-start.13 = (f32[1,1,256]{2,1,0:T(1,128)S(1)}, f32[1,1,256]{2,1,0:T(1,128)S(1)}, u32[]{:S(2)}, u32[]{:S(2)}) collective-permute-start(f32[1,1,256]{2,1,0:T(1,128)S(1)} %get-tuple-element.29), channel_id=1, source_target_pairs={{0,6},{1,7},{2,4},{3,5},{4,2},{5,3},{6,0},{7,1},{8,14},{9,15},{10,... | collective-permute-start | bytes 3080 | tf_op jit(solution)/shard_map/ppermute | solution.py:120
  29.2 1.2 %collective-permute-done.10.refs_5_ = bf16[272,768]{1,0:T(8,128)(2,1)S(1)} collective-permute-done((bf16[272,768]{1,0:T(8,128)(2,1)S(1)}, bf16[272,768]{1,0:T(8,128)(2,1)S(1)}, u32[]{:S(2)}, u32[]{:S(2)}) %collective-permute-start.10) | collective-permute-done | bytes 417824 | tf_op jit(solution)/shard_map/ppermute | solution.py:126
  30.5 0.9 %collective-permute-done.13 = f32[1,1,256]{2,1,0:T(1,128)S(1)} collective-permute-done((f32[1,1,256]{2,1,0:T(1,128)S(1)}, f32[1,1,256]{2,1,0:T(1,128)S(1)}, u32[]{:S(2)}, u32[]{:S(2)}) %collective-permute-start.13) | collective-permute-done | bytes 1056 | tf_op jit(solution)/shard_map/ppermute | solution.py:120
  31.4 0.0 collective-permute-start.14
  31.4 0.6 %compare_half_way.1 = f32[1,1,256]{2,1,0:T(1,128)S(1)} custom-call(bf16[272,768]{1,0:T(8,128)(2,1)S(1)} %pack.1.refs_0_.refs_3_.refs_2_, bf16[272,768]{1,0:T(8,128)(2,1)S(1)} %collective-permute-done.2.refs_1_, bf16[272,768]{1,0:T(8,128)(2,1)S(1)} %collective-permute-done.refs_2_, bf16[128,768]{1,0:T(8,128)(2,1)S(1)} %collective-permute-done.1.refs_0_.refs_3_, ...), custom_call_target="tpu_custom_call" | custom-call | flops 402653184 | bytes 2088960 | tf_op jit(solution)/shard_map/compare_half_way/pallas_call | solution.py:91
  32.0 2.3 %collective-permute-start.11 = (f32[1,1,256]{2,1,0:T(1,128)S(1)}, f32[1,1,256]{2,1,0:T(1,128)S(1)}, u32[]{:S(2)}, u32[]{:S(2)}) collective-permute-start(f32[1,1,256]{2,1,0:T(1,128)S(1)} %compare_half_way.1), channel_id=1, source_target_pairs={{0,16},{8,24},{16,0},{24,8},{1,17},{9,25},{17,1},{25,9},{2,18},{10... | collective-permute-start | bytes 3080 | tf_op jit(solution)/shard_map/ppermute | solution.py:126
  34.3 1.6 %collective-permute-start.9 = (f32[1,1,256]{2,1,0:T(1,128)S(1)}, f32[1,1,256]{2,1,0:T(1,128)S(1)}, u32[]{:S(2)}, u32[]{:S(2)}) collective-permute-start(f32[1,1,256]{2,1,0:T(1,128)S(1)} %bitcast.20), channel_id=1, source_target_pairs={{0,24},{8,0},{16,8},{24,16},{1,25},{9,1},{17,9},{25,17},{2,26},{10... | collective-permute-start | bytes 3080 | tf_op jit(solution)/shard_map/ppermute | solution.py:126
  35.9 0.6 %compare_twin.1 = f32[1,1,256]{2,1,0:T(1,128)S(1)} custom-call(bf16[272,768]{1,0:T(8,128)(2,1)S(1)} %pack.1.refs_0_.refs_3_.refs_2_, bf16[272,768]{1,0:T(8,128)(2,1)S(1)} %collective-permute-done.2.refs_1_, bf16[272,768]{1,0:T(8,128)(2,1)S(1)} %collective-permute-done.refs_2_, bf16[128,768]{1,0:T(8,128)(2,1)S(1)} %collective-permute-done.1.refs_0_.refs_3_, ...), custom_call_target="tpu_custom_call" | custom-call | flops 402653184 | bytes 2088960 | tf_op jit(solution)/shard_map/compare_twin/pallas_call | solution.py:91
  36.5 1.6 %collective-permute-start.15 = (f32[1,1,256]{2,1,0:T(1,128)S(1)}, f32[1,1,256]{2,1,0:T(1,128)S(1)}, u32[]{:S(2)}, u32[]{:S(2)}) collective-permute-start(f32[1,1,256]{2,1,0:T(1,128)S(1)} %compare_twin.1), channel_id=1, source_target_pairs={{0,17},{1,16},{2,19},{3,18},{4,21},{5,20},{6,23},{7,22},{8,25},{9,... | collective-permute-start | bytes 3080 | tf_op jit(solution)/shard_map/ppermute | solution.py:130
  38.1 0.0 collective-permute-done.11
  38.1 2.4 %collective-permute-done.15 = f32[1,1,256]{2,1,0:T(1,128)S(1)} collective-permute-done((f32[1,1,256]{2,1,0:T(1,128)S(1)}, f32[1,1,256]{2,1,0:T(1,128)S(1)}, u32[]{:S(2)}, u32[]{:S(2)}) %collective-permute-start.15) | collective-permute-done | bytes 1056 | tf_op jit(solution)/shard_map/ppermute | solution.py:130
  40.4 0.6 %maximum_maximum_fusion = f32[1,1,256]{2,1,0:T(1,128)} fusion(f32[1,1,256]{2,1,0:T(1,128)S(1)} %collective-permute-done.13, f32[1,1,256]{2,1,0:T(1,128)S(1)} %collective-permute-done.12, f32[1,1,256]{2,1,0:T(1,128)S(1)} %collective-permute-done.7, f32[1,1,256]{2,1,0:T(1,128)S(1)} %collective-permute-done.15, f32[1,1,256]{2,1,0:T(1,128)S(1)} %collective-permute-done.11, ...), kind=kLoop, calls=%fused_computation.4 | loop fusion | flops 1792 | bytes 9216 | tf_op jit(solution)/shard_map/max | solution.py:196
  (15 shorter events, 0.1 us)
Async XLA Ops:
  0.0 0.7 %copy-start.2 = (s32[256]{0:T(256)S(1)}, s32[256]{0:T(256)}, u32[]{:S(2)}) copy-start(s32[256]{0:T(256)} %param.5) | copy-start | bytes 3076
  0.0 0.7 %copy-start.1 = (s32[256,1]{0,1:T(1,128)S(1)}, s32[256,1]{0,1:T(1,128)}, u32[]{:S(2)}) copy-start(s32[256,1]{0,1:T(1,128)} %param.4) | copy-start | bytes 3076
  0.7 1.0 %copy-start = (bf16[256,768]{1,0:T(8,128)(2,1)S(1)}, bf16[256,768]{1,0:T(8,128)(2,1)}, u32[]{:S(2)}) copy-start(bf16[256,768]{1,0:T(8,128)(2,1)} %emb_ref.1) | copy-start | bytes 1179652
  1.9 14.7 %collective-permute-start.4 = (bf16[272,768]{1,0:T(8,128)(2,1)S(1)}, bf16[272,768]{1,0:T(8,128)(2,1)S(1)}, u32[]{:S(2)}, u32[]{:S(2)}) collective-permute-start(bf16[272,768]{1,0:T(8,128)(2,1)S(1)} %pack.1.refs_0_.refs_3_.refs_2_), channel_id=1, source_target_pairs={{0,8},{8,16},{16,24},{24,0},{1,9},{9,17},{17,25},{25,1},{2,10},{10... | collective-permute-start | bytes 1253384 | tf_op jit(solution)/shard_map/ppermute | solution.py:126
  4.9 12.2 %collective-permute-start.2 = (bf16[272,768]{1,0:T(8,128)(2,1)S(1)}, bf16[272,768]{1,0:T(8,128)(2,1)S(1)}, u32[]{:S(2)}, u32[]{:S(2)}) collective-permute-start(bf16[272,768]{1,0:T(8,128)(2,1)S(1)} %pack.1.refs_0_.refs_3_.refs_2_), channel_id=1, source_target_pairs={{0,2},{1,3},{2,0},{3,1},{4,6},{5,7},{6,4},{7,5},{8,10},{9,11},{10,... | collective-permute-start | bytes 1253384 | tf_op jit(solution)/shard_map/ppermute | solution.py:120
  6.4 12.3 %collective-permute-start = (bf16[272,768]{1,0:T(8,128)(2,1)S(1)}, bf16[272,768]{1,0:T(8,128)(2,1)S(1)}, u32[]{:S(2)}, u32[]{:S(2)}) collective-permute-start(bf16[272,768]{1,0:T(8,128)(2,1)S(1)} %pack.1.refs_0_.refs_3_.refs_2_), channel_id=1, source_target_pairs={{0,4},{1,5},{2,6},{3,7},{4,0},{5,1},{6,2},{7,3},{8,12},{9,13},{10,... | collective-permute-start | bytes 1253384 | tf_op jit(solution)/shard_map/ppermute | solution.py:120
  16.6 3.7 %collective-permute-start.5 = (bf16[272,768]{1,0:T(8,128)(2,1)S(1)}, bf16[272,768]{1,0:T(8,128)(2,1)S(1)}, u32[]{:S(2)}, u32[]{:S(2)}) collective-permute-start(bf16[272,768]{1,0:T(8,128)(2,1)S(1)} %pack.1.refs_0_.refs_3_.refs_2_), channel_id=1, source_target_pairs={{0,1},{1,0},{2,3},{3,2},{4,5},{5,4},{6,7},{7,6},{8,9},{9,8},{10,11... | collective-permute-start | bytes 1253384 | tf_op jit(solution)/shard_map/ppermute | solution.py:120
  16.6 3.7 %collective-permute-start.6 = (bf16[272,768]{1,0:T(8,128)(2,1)S(1)}, bf16[272,768]{1,0:T(8,128)(2,1)S(1)}, u32[]{:S(2)}, u32[]{:S(2)}) collective-permute-start(bf16[272,768]{1,0:T(8,128)(2,1)S(1)} %collective-permute-done.4.refs_5_.refs_4_), channel_id=1, source_target_pairs={{0,1},{1,0},{2,3},{3,2},{4,5},{5,4},{6,7},{7,6},{8,9},{9,8},{10,11... | collective-permute-start | bytes 1253384 | tf_op jit(solution)/shard_map/ppermute | solution.py:120
  17.1 13.3 %collective-permute-start.10 = (bf16[272,768]{1,0:T(8,128)(2,1)S(1)}, bf16[272,768]{1,0:T(8,128)(2,1)S(1)}, u32[]{:S(2)}, u32[]{:S(2)}) collective-permute-start(bf16[272,768]{1,0:T(8,128)(2,1)S(1)} %collective-permute-done.4.refs_5_.refs_4_), channel_id=1, source_target_pairs={{0,8},{8,16},{16,24},{24,0},{1,9},{9,17},{17,25},{25,1},{2,10},{10... | collective-permute-start | bytes 1253384 | tf_op jit(solution)/shard_map/ppermute | solution.py:126
  17.1 8.3 %collective-permute-start.3 = (bf16[144,768]{1,0:T(8,128)(2,1)S(1)}, bf16[144,768]{1,0:T(8,128)(2,1)S(1)}, u32[]{:S(2)}, u32[]{:S(2)}) collective-permute-start(bf16[144,768]{1,0:T(8,128)(2,1)S(1)} %slice.9), channel_id=1, source_target_pairs={{0,4},{1,5},{2,6},{3,7},{4,0},{5,1},{6,2},{7,3},{8,12},{9,13},{10,... | collective-permute-start | bytes 663560 | tf_op jit(solution)/shard_map/ppermute | solution.py:120
  18.7 6.7 %collective-permute-start.1 = (bf16[128,768]{1,0:T(8,128)(2,1)S(1)}, bf16[128,768]{1,0:T(8,128)(2,1)S(1)}, u32[]{:S(2)}, u32[]{:S(2)}) collective-permute-start(bf16[128,768]{1,0:T(8,128)(2,1)S(1)} %slice.8), channel_id=1, source_target_pairs={{0,2},{1,3},{2,0},{3,1},{4,6},{5,7},{6,4},{7,5},{8,10},{9,11},{10,... | collective-permute-start | bytes 589832 | tf_op jit(solution)/shard_map/ppermute | solution.py:120
  21.8 3.6 %collective-permute-start.7 = (f32[1,1,256]{2,1,0:T(1,128)S(1)}, f32[1,1,256]{2,1,0:T(1,128)S(1)}, u32[]{:S(2)}, u32[]{:S(2)}) collective-permute-start(f32[1,1,256]{2,1,0:T(1,128)S(1)} %get-tuple-element.20), channel_id=1, source_target_pairs={{0,2},{1,3},{2,0},{3,1},{4,6},{5,7},{6,4},{7,5},{8,10},{9,11},{10,... | collective-permute-start | bytes 3080 | tf_op jit(solution)/shard_map/ppermute | solution.py:120
  26.2 3.0 %collective-permute-start.8 = (f32[2,1,256]{2,1,0:T(1,128)S(1)}, f32[2,1,256]{2,1,0:T(1,128)S(1)}, u32[]{:S(2)}, u32[]{:S(2)}) collective-permute-start(f32[2,1,256]{2,1,0:T(1,128)S(1)} %get-tuple-element.24), channel_id=1, source_target_pairs={{0,1},{1,0},{2,3},{3,2},{4,5},{5,4},{6,7},{7,6},{8,9},{9,8},{10,11... | collective-permute-start | bytes 6152 | tf_op jit(solution)/shard_map/ppermute | solution.py:120
  26.2 4.2 %collective-permute-start.12 = (f32[1,1,256]{2,1,0:T(1,128)S(1)}, f32[1,1,256]{2,1,0:T(1,128)S(1)}, u32[]{:S(2)}, u32[]{:S(2)}) collective-permute-start(f32[1,1,256]{2,1,0:T(1,128)S(1)} %get-tuple-element.28), channel_id=1, source_target_pairs={{0,4},{1,5},{2,6},{3,7},{4,0},{5,1},{6,2},{7,3},{8,12},{9,13},{10,... | collective-permute-start | bytes 3080 | tf_op jit(solution)/shard_map/ppermute | solution.py:120
  26.9 4.5 %collective-permute-start.13 = (f32[1,1,256]{2,1,0:T(1,128)S(1)}, f32[1,1,256]{2,1,0:T(1,128)S(1)}, u32[]{:S(2)}, u32[]{:S(2)}) collective-permute-start(f32[1,1,256]{2,1,0:T(1,128)S(1)} %get-tuple-element.29), channel_id=1, source_target_pairs={{0,6},{1,7},{2,4},{3,5},{4,2},{5,3},{6,0},{7,1},{8,14},{9,15},{10,... | collective-permute-start | bytes 3080 | tf_op jit(solution)/shard_map/ppermute | solution.py:120
  31.4 4.5 %collective-permute-start.14 = (bf16[272,768]{1,0:T(8,128)(2,1)S(1)}, bf16[272,768]{1,0:T(8,128)(2,1)S(1)}, u32[]{:S(2)}, u32[]{:S(2)}) collective-permute-start(bf16[272,768]{1,0:T(8,128)(2,1)S(1)} %collective-permute-done.10.refs_5_), channel_id=1, source_target_pairs={{0,1},{1,0},{2,3},{3,2},{4,5},{5,4},{6,7},{7,6},{8,9},{9,8},{10,11... | collective-permute-start | bytes 1253384 | tf_op jit(solution)/shard_map/ppermute | solution.py:120
  32.0 6.1 %collective-permute-start.11 = (f32[1,1,256]{2,1,0:T(1,128)S(1)}, f32[1,1,256]{2,1,0:T(1,128)S(1)}, u32[]{:S(2)}, u32[]{:S(2)}) collective-permute-start(f32[1,1,256]{2,1,0:T(1,128)S(1)} %compare_half_way.1), channel_id=1, source_target_pairs={{0,16},{8,24},{16,0},{24,8},{1,17},{9,25},{17,1},{25,9},{2,18},{10... | collective-permute-start | bytes 3080 | tf_op jit(solution)/shard_map/ppermute | solution.py:126
  34.3 3.8 %collective-permute-start.9 = (f32[1,1,256]{2,1,0:T(1,128)S(1)}, f32[1,1,256]{2,1,0:T(1,128)S(1)}, u32[]{:S(2)}, u32[]{:S(2)}) collective-permute-start(f32[1,1,256]{2,1,0:T(1,128)S(1)} %bitcast.20), channel_id=1, source_target_pairs={{0,24},{8,0},{16,8},{24,16},{1,25},{9,1},{17,9},{25,17},{2,26},{10... | collective-permute-start | bytes 3080 | tf_op jit(solution)/shard_map/ppermute | solution.py:126
  36.5 4.0 %collective-permute-start.15 = (f32[1,1,256]{2,1,0:T(1,128)S(1)}, f32[1,1,256]{2,1,0:T(1,128)S(1)}, u32[]{:S(2)}, u32[]{:S(2)}) collective-permute-start(f32[1,1,256]{2,1,0:T(1,128)S(1)} %compare_twin.1), channel_id=1, source_target_pairs={{0,17},{1,16},{2,19},{3,18},{4,21},{5,20},{6,23},{7,22},{8,25},{9,... | collective-permute-start | bytes 3080 | tf_op jit(solution)/shard_map/ppermute | solution.py:130

commit v3 on v2

--- a/solution.py
+++ b/solution.py
@@ -171,7 +171,7 @@
         [tuple(every)],
     )
     early = [plane_shift(best, mask) for best, mask in zip(rows_direct[1:], direct[1:])]
-    best = lax.optimization_barrier((best, early[0]))[0]
+    best = lax.optimization_barrier((best, early))[0]
     own, one_off_best, twins, *rows_relayed = score(
         "compare_relayed",
         [plane[mask] for mask in relayed],
@@ -189,8 +189,9 @@
 
     blocks = list(plane.values())
     pairs = [(k, 0, False) for k in range(len(blocks))]
-    half_then = lax.optimization_barrier((half_way, own, early))[0]
-    for name, block, mask in (("compare_half_way", half_way, 0), ("compare_twin", plane_shift(half_then, 1), 1)):
+    half_then = lax.optimization_barrier((half_way, own))[0]
+    half_twin = lax.optimization_barrier((plane_shift(half_then, 1), early))[0]
+    for name, block, mask in (("compare_half_way", half_way, 0), ("compare_twin", half_twin, 1)):
         (half_best,) = score(name, blocks, [block], pairs, (), [(0,)])
         found.append(grp_shift(half_best, groups // 2, mask))
     return functools.reduce(jnp.maximum, found + early).reshape(-1)

time: 41.2 us -> 40.3 us (0.978)
  starting transfers between devices: 18.8 us -> 16.1 us
  waiting for transfers between devices: 16.2 us -> 18 us
    ppermute x4, starting transfers between devices: 6.94 us -> 3.98 us  [grp_shift(): lax.ppermute(x, 'grp', [(z, (z + shift) % groups) for z in range(groups)])]
    ppermute x4, waiting for transfers between devices: 9.91 us -> 12.5 us  [grp_shift(): lax.ppermute(x, 'grp', [(z, (z + shift) % groups) for z in range(groups)])]
    ppermute x1, waiting for transfers between devices: 2.38 us -> 1.44 us  [grp_shift(): return lax.ppermute(x, ('grp', 'blk'), pairs)]
    ppermute x11, starting transfers between devices: 10.3 us -> 10.9 us  [plane_shift(): return lax.ppermute(x, 'blk', [(i, i ^ mask) for i in range(size)])]
  transfers between devices with their start and end apart: 16 -> 16, of which waited for: 5 -> 8; matrix products, arithmetic and copies ran while one was open for 0% -> 0% of each run, Pallas kernels for 8% -> 9%
where the time goes in v3:
time: 40.3 us; the launch traced here: 40.1 us
  waiting for transfers between devices  18 us (45%)
  starting transfers between devices  16.1 us (40%)
  Pallas kernels  3.61 us (9%)
  local copies, waits for them, and re-layouts  1.72 us (4%)
  other arithmetic  0.57 us (1%)
    ppermute x4, waiting for transfers between devices, grp_shift(): lax.ppermute(x, 'grp', [(z, (z + shift) % groups) for z in range(groups)])  12.5 us
    ppermute x11, starting transfers between devices, plane_shift(): return lax.ppermute(x, 'blk', [(i, i ^ mask) for i in range(size)])  10.9 us
    ppermute x11, waiting for transfers between devices, plane_shift(): return lax.ppermute(x, 'blk', [(i, i ^ mask) for i in range(size)])  4.09 us
    ppermute x4, starting transfers between devices, grp_shift(): lax.ppermute(x, 'grp', [(z, (z + shift) % groups) for z in range(groups)])  3.98 us
    pallas_call x4, Pallas kernels, score(): pl.pallas_call(kernel, out_shape=[jax.ShapeDtypeStruct((count, 1, rows),...  3.45 us
    unnamed x6, local copies, waits for them, and re-layouts  1.69 us
    ppermute x1, waiting for transfers between devices, grp_shift(): return lax.ppermute(x, ('grp', 'blk'), pairs)  1.44 us
    ppermute x1, starting transfers between devices, grp_shift(): return lax.ppermute(x, ('grp', 'blk'), pairs)  1.23 us
  transfers between devices with their start and end apart: 16, of which 8 were waited for; matrix products, arithmetic and copies ran while one was open for 0% of the time, Pallas kernels for 9%

profile of v3, /device:TPU:0, one launch (start us, length us, event | category | flops | bytes accessed | tf_op | source)
XLA Modules:
  0.0 40.1 jit_solution(11041850642267521354)
XLA Ops:
  0.0 0.7 %copy-done.2 = s32[256]{0:T(256)S(1)} copy-done((s32[256]{0:T(256)S(1)}, s32[256]{0:T(256)}, u32[]{:S(2)}) %copy-start.2) | copy-done | bytes 1048
  0.7 0.0 copy-done.1
  0.7 1.0 %copy-done = bf16[256,768]{1,0:T(8,128)(2,1)S(1)} copy-done((bf16[256,768]{1,0:T(8,128)(2,1)S(1)}, bf16[256,768]{1,0:T(8,128)(2,1)}, u32[]{:S(2)}) %copy-start) | copy-done | bytes 393240
  1.7 0.2 pack.1.refs_0_.refs_3_.refs_2_
  1.9 3.1 %collective-permute-start.4 = (bf16[272,768]{1,0:T(8,128)(2,1)S(1)}, bf16[272,768]{1,0:T(8,128)(2,1)S(1)}, u32[]{:S(2)}, u32[]{:S(2)}) collective-permute-start(bf16[272,768]{1,0:T(8,128)(2,1)S(1)} %pack.1.refs_0_.refs_3_.refs_2_), channel_id=1, source_target_pairs={{0,8},{8,16},{16,24},{24,0},{1,9},{9,17},{17,25},{25,1},{2,10},{10... | collective-permute-start | bytes 1253384 | tf_op jit(solution)/shard_map/ppermute | solution.py:126
  4.9 1.5 %collective-permute-start.2 = (bf16[272,768]{1,0:T(8,128)(2,1)S(1)}, bf16[272,768]{1,0:T(8,128)(2,1)S(1)}, u32[]{:S(2)}, u32[]{:S(2)}) collective-permute-start(bf16[272,768]{1,0:T(8,128)(2,1)S(1)} %pack.1.refs_0_.refs_3_.refs_2_), channel_id=1, source_target_pairs={{0,2},{1,3},{2,0},{3,1},{4,6},{5,7},{6,4},{7,5},{8,10},{9,11},{10,... | collective-permute-start | bytes 1253384 | tf_op jit(solution)/shard_map/ppermute | solution.py:120
  6.4 1.5 %collective-permute-start = (bf16[272,768]{1,0:T(8,128)(2,1)S(1)}, bf16[272,768]{1,0:T(8,128)(2,1)S(1)}, u32[]{:S(2)}, u32[]{:S(2)}) collective-permute-start(bf16[272,768]{1,0:T(8,128)(2,1)S(1)} %pack.1.refs_0_.refs_3_.refs_2_), channel_id=1, source_target_pairs={{0,4},{1,5},{2,6},{3,7},{4,0},{5,1},{6,2},{7,3},{8,12},{9,13},{10,... | collective-permute-start | bytes 1253384 | tf_op jit(solution)/shard_map/ppermute | solution.py:120
  7.9 8.7 %collective-permute-done.4.refs_5_.refs_4_ = bf16[272,768]{1,0:T(8,128)(2,1)S(1)} collective-permute-done((bf16[272,768]{1,0:T(8,128)(2,1)S(1)}, bf16[272,768]{1,0:T(8,128)(2,1)S(1)}, u32[]{:S(2)}, u32[]{:S(2)}) %collective-permute-start.4) | collective-permute-done | bytes 417824 | tf_op jit(solution)/shard_map/ppermute | solution.py:126
  16.6 0.5 %collective-permute-start.6 = (bf16[272,768]{1,0:T(8,128)(2,1)S(1)}, bf16[272,768]{1,0:T(8,128)(2,1)S(1)}, u32[]{:S(2)}, u32[]{:S(2)}) collective-permute-start(bf16[272,768]{1,0:T(8,128)(2,1)S(1)} %collective-permute-done.4.refs_5_.refs_4_), channel_id=1, source_target_pairs={{0,1},{1,0},{2,3},{3,2},{4,5},{5,4},{6,7},{7,6},{8,9},{9,8},{10,11... | collective-permute-start | bytes 1253384 | tf_op jit(solution)/shard_map/ppermute | solution.py:120
  17.1 0.0 collective-permute-start.11
  17.1 0.0 collective-permute-done.2.refs_1_
  17.1 1.6 %collective-permute-start.3 = (bf16[144,768]{1,0:T(8,128)(2,1)S(1)}, bf16[144,768]{1,0:T(8,128)(2,1)S(1)}, u32[]{:S(2)}, u32[]{:S(2)}) collective-permute-start(bf16[144,768]{1,0:T(8,128)(2,1)S(1)} %slice.9), channel_id=1, source_target_pairs={{0,4},{1,5},{2,6},{3,7},{4,0},{5,1},{6,2},{7,3},{8,12},{9,13},{10,... | collective-permute-start | bytes 663560 | tf_op jit(solution)/shard_map/ppermute | solution.py:120
  18.7 1.6 %collective-permute-start.1 = (bf16[128,768]{1,0:T(8,128)(2,1)S(1)}, bf16[128,768]{1,0:T(8,128)(2,1)S(1)}, u32[]{:S(2)}, u32[]{:S(2)}) collective-permute-start(bf16[128,768]{1,0:T(8,128)(2,1)S(1)} %slice.8), channel_id=1, source_target_pairs={{0,2},{1,3},{2,0},{3,1},{4,6},{5,7},{6,4},{7,5},{8,10},{9,11},{10,... | collective-permute-start | bytes 589832 | tf_op jit(solution)/shard_map/ppermute | solution.py:120
  20.3 1.5 %compare_direct.1 = (f32[4,1,256]{2,1,0:T(1,128)S(1)}, f32[1,1,256]{2,1,0:T(1,128)S(1)}, f32[1,1,256]{2,1,0:T(1,128)S(1)}, f32[1,1,256]{2,1,0:T(1,128)S(1)}) custom-call(bf16[272,768]{1,0:T(8,128)(2,1)S(1)} %pack.1.refs_0_.refs_3_.refs_2_, bf16[272,768]{1,0:T(8,128)(2,1)S(1)} %collective-permute-done.2.refs_1_, ...), custom_call_target="tpu_custom_call" | custom-call | flops 1207959552 | bytes 2924544 | tf_op jit(solution)/shard_map/compare_direct/pallas_call | solution.py:91
  21.8 0.6 %collective-permute-start.7 = (f32[1,1,256]{2,1,0:T(1,128)S(1)}, f32[1,1,256]{2,1,0:T(1,128)S(1)}, u32[]{:S(2)}, u32[]{:S(2)}) collective-permute-start(f32[1,1,256]{2,1,0:T(1,128)S(1)} %get-tuple-element.21), channel_id=1, source_target_pairs={{0,2},{1,3},{2,0},{3,1},{4,6},{5,7},{6,4},{7,5},{8,10},{9,11},{10,... | collective-permute-start | bytes 3080 | tf_op jit(solution)/shard_map/ppermute | solution.py:120
  22.4 1.1 %collective-permute-start.8 = (f32[1,1,256]{2,1,0:T(1,128)S(1)}, f32[1,1,256]{2,1,0:T(1,128)S(1)}, u32[]{:S(2)}, u32[]{:S(2)}) collective-permute-start(f32[1,1,256]{2,1,0:T(1,128)S(1)} %get-tuple-element.22), channel_id=1, source_target_pairs={{0,4},{1,5},{2,6},{3,7},{4,0},{5,1},{6,2},{7,3},{8,12},{9,13},{10,... | collective-permute-start | bytes 3080 | tf_op jit(solution)/shard_map/ppermute | solution.py:120
  23.6 1.9 %collective-permute-done.7 = f32[1,1,256]{2,1,0:T(1,128)S(1)} collective-permute-done((f32[1,1,256]{2,1,0:T(1,128)S(1)}, f32[1,1,256]{2,1,0:T(1,128)S(1)}, u32[]{:S(2)}, u32[]{:S(2)}) %collective-permute-start.7) | collective-permute-done | bytes 1056 | tf_op jit(solution)/shard_map/ppermute | solution.py:120
  25.5 0.5 %collective-permute-done.8 = f32[1,1,256]{2,1,0:T(1,128)S(1)} collective-permute-done((f32[1,1,256]{2,1,0:T(1,128)S(1)}, f32[1,1,256]{2,1,0:T(1,128)S(1)}, u32[]{:S(2)}, u32[]{:S(2)}) %collective-permute-start.8) | collective-permute-done | bytes 1056 | tf_op jit(solution)/shard_map/ppermute | solution.py:120
  26.0 0.7 %compare_relayed.1 = (f32[1,1,256]{2,1,0:T(1,128)S(1)}, f32[1,1,256]{2,1,0:T(1,128)S(1)}, f32[2,1,256]{2,1,0:T(1,128)S(1)}, f32[1,1,256]{2,1,0:T(1,128)S(1)}) custom-call(bf16[128,768]{1,0:T(8,128)(2,1)S(1)} %collective-permute-done.1.refs_0_.refs_3_, bf16[144,768]{1,0:T(8,128)(2,1)S(1)} %collective-permute-done.3.refs_1_.refs_4_, ...), custom_call_target="tpu_custom_call" | custom-call | flops 402653184 | bytes 2088960 | tf_op jit(solution)/shard_map/compare_relayed/pallas_call | solution.py:91
  26.7 0.1 collective-permute-start.9
  26.8 1.1 %collective-permute-done.9.refs_2_ = f32[2,1,256]{2,1,0:T(1,128)S(1)} collective-permute-done((f32[2,1,256]{2,1,0:T(1,128)S(1)}, f32[2,1,256]{2,1,0:T(1,128)S(1)}, u32[]{:S(2)}, u32[]{:S(2)}) %collective-permute-start.9) | collective-permute-done | bytes 2080 | tf_op jit(solution)/shard_map/ppermute | solution.py:120
  27.9 2.5 %collective-permute-done.11.refs_5_ = bf16[272,768]{1,0:T(8,128)(2,1)S(1)} collective-permute-done((bf16[272,768]{1,0:T(8,128)(2,1)S(1)}, bf16[272,768]{1,0:T(8,128)(2,1)S(1)}, u32[]{:S(2)}, u32[]{:S(2)}) %collective-permute-start.11) | collective-permute-done | bytes 417824 | tf_op jit(solution)/shard_map/ppermute | solution.py:126
  30.5 2.4 %collective-permute-start.14 = (f32[1,1,256]{2,1,0:T(1,128)S(1)}, f32[1,1,256]{2,1,0:T(1,128)S(1)}, u32[]{:S(2)}, u32[]{:S(2)}) collective-permute-start(f32[1,1,256]{2,1,0:T(1,128)S(1)} %get-tuple-element.31), channel_id=1, source_target_pairs={{0,6},{1,7},{2,4},{3,5},{4,2},{5,3},{6,0},{7,1},{8,14},{9,15},{10,... | collective-permute-start | bytes 3080 | tf_op jit(solution)/shard_map/ppermute | solution.py:120
  32.9 0.6 %compare_half_way.1 = f32[1,1,256]{2,1,0:T(1,128)S(1)} custom-call(bf16[272,768]{1,0:T(8,128)(2,1)S(1)} %pack.1.refs_0_.refs_3_.refs_2_, bf16[272,768]{1,0:T(8,128)(2,1)S(1)} %collective-permute-done.2.refs_1_, bf16[272,768]{1,0:T(8,128)(2,1)S(1)} %collective-permute-done.refs_2_, bf16[128,768]{1,0:T(8,128)(2,1)S(1)} %collective-permute-done.1.refs_0_.refs_3_, ...), custom_call_target="tpu_custom_call" | custom-call | flops 402653184 | bytes 2088960 | tf_op jit(solution)/shard_map/compare_half_way/pallas_call | solution.py:91
  33.5 0.1 collective-permute-start.12
  33.6 0.8 %collective-permute-start.10 = (f32[1,1,256]{2,1,0:T(1,128)S(1)}, f32[1,1,256]{2,1,0:T(1,128)S(1)}, u32[]{:S(2)}, u32[]{:S(2)}) collective-permute-start(f32[1,1,256]{2,1,0:T(1,128)S(1)} %bitcast.20), channel_id=1, source_target_pairs={{0,24},{8,0},{16,8},{24,16},{1,25},{9,1},{17,9},{25,17},{2,26},{10... | collective-permute-start | bytes 3080 | tf_op jit(solution)/shard_map/ppermute | solution.py:126
  34.4 0.5 %collective-permute-done.14 = f32[1,1,256]{2,1,0:T(1,128)S(1)} collective-permute-done((f32[1,1,256]{2,1,0:T(1,128)S(1)}, f32[1,1,256]{2,1,0:T(1,128)S(1)}, u32[]{:S(2)}, u32[]{:S(2)}) %collective-permute-start.14) | collective-permute-done | bytes 1056 | tf_op jit(solution)/shard_map/ppermute | solution.py:120
  34.9 0.6 %compare_twin.1 = f32[1,1,256]{2,1,0:T(1,128)S(1)} custom-call(bf16[272,768]{1,0:T(8,128)(2,1)S(1)} %pack.1.refs_0_.refs_3_.refs_2_, bf16[272,768]{1,0:T(8,128)(2,1)S(1)} %collective-permute-done.2.refs_1_, bf16[272,768]{1,0:T(8,128)(2,1)S(1)} %collective-permute-done.refs_2_, bf16[128,768]{1,0:T(8,128)(2,1)S(1)} %collective-permute-done.1.refs_0_.refs_3_, ...), custom_call_target="tpu_custom_call" | custom-call | flops 402653184 | bytes 2088960 | tf_op jit(solution)/shard_map/compare_twin/pallas_call | solution.py:91
  35.6 1.2 %collective-permute-start.15 = (f32[1,1,256]{2,1,0:T(1,128)S(1)}, f32[1,1,256]{2,1,0:T(1,128)S(1)}, u32[]{:S(2)}, u32[]{:S(2)}) collective-permute-start(f32[1,1,256]{2,1,0:T(1,128)S(1)} %compare_twin.1), channel_id=1, source_target_pairs={{0,17},{1,16},{2,19},{3,18},{4,21},{5,20},{6,23},{7,22},{8,25},{9,... | collective-permute-start | bytes 3080 | tf_op jit(solution)/shard_map/ppermute | solution.py:130
  36.8 1.3 %collective-permute-done.12 = f32[1,1,256]{2,1,0:T(1,128)S(1)} collective-permute-done((f32[1,1,256]{2,1,0:T(1,128)S(1)}, f32[1,1,256]{2,1,0:T(1,128)S(1)}, u32[]{:S(2)}, u32[]{:S(2)}) %collective-permute-start.12) | collective-permute-done | bytes 1056 | tf_op jit(solution)/shard_map/ppermute | solution.py:126
  38.1 1.4 %collective-permute-done.15 = f32[1,1,256]{2,1,0:T(1,128)S(1)} collective-permute-done((f32[1,1,256]{2,1,0:T(1,128)S(1)}, f32[1,1,256]{2,1,0:T(1,128)S(1)}, u32[]{:S(2)}, u32[]{:S(2)}) %collective-permute-start.15) | collective-permute-done | bytes 1056 | tf_op jit(solution)/shard_map/ppermute | solution.py:130
  39.5 0.6 %maximum_maximum_fusion = f32[1,1,256]{2,1,0:T(1,128)} fusion(f32[1,1,256]{2,1,0:T(1,128)S(1)} %collective-permute-done.14, f32[1,1,256]{2,1,0:T(1,128)S(1)} %collective-permute-done.8, f32[1,1,256]{2,1,0:T(1,128)S(1)} %collective-permute-done.7, f32[1,1,256]{2,1,0:T(1,128)S(1)} %collective-permute-done.15, f32[1,1,256]{2,1,0:T(1,128)S(1)} %collective-permute-done.12, ...), kind=kLoop, calls=%fused_computation.4 | loop fusion | flops 1792 | bytes 9216 | tf_op jit(solution)/shard_map/max | solution.py:197
  (15 shorter events, 0.1 us)
Async XLA Ops:
  0.0 0.7 %copy-start.2 = (s32[256]{0:T(256)S(1)}, s32[256]{0:T(256)}, u32[]{:S(2)}) copy-start(s32[256]{0:T(256)} %param.5) | copy-start | bytes 3076
  0.0 0.7 %copy-start.1 = (s32[256,1]{0,1:T(1,128)S(1)}, s32[256,1]{0,1:T(1,128)}, u32[]{:S(2)}) copy-start(s32[256,1]{0,1:T(1,128)} %param.4) | copy-start | bytes 3076
  0.7 1.0 %copy-start = (bf16[256,768]{1,0:T(8,128)(2,1)S(1)}, bf16[256,768]{1,0:T(8,128)(2,1)}, u32[]{:S(2)}) copy-start(bf16[256,768]{1,0:T(8,128)(2,1)} %emb_ref.1) | copy-start | bytes 1179652
  1.9 14.7 %collective-permute-start.4 = (bf16[272,768]{1,0:T(8,128)(2,1)S(1)}, bf16[272,768]{1,0:T(8,128)(2,1)S(1)}, u32[]{:S(2)}, u32[]{:S(2)}) collective-permute-start(bf16[272,768]{1,0:T(8,128)(2,1)S(1)} %pack.1.refs_0_.refs_3_.refs_2_), channel_id=1, source_target_pairs={{0,8},{8,16},{16,24},{24,0},{1,9},{9,17},{17,25},{25,1},{2,10},{10... | collective-permute-start | bytes 1253384 | tf_op jit(solution)/shard_map/ppermute | solution.py:126
  4.9 12.2 %collective-permute-start.2 = (bf16[272,768]{1,0:T(8,128)(2,1)S(1)}, bf16[272,768]{1,0:T(8,128)(2,1)S(1)}, u32[]{:S(2)}, u32[]{:S(2)}) collective-permute-start(bf16[272,768]{1,0:T(8,128)(2,1)S(1)} %pack.1.refs_0_.refs_3_.refs_2_), channel_id=1, source_target_pairs={{0,2},{1,3},{2,0},{3,1},{4,6},{5,7},{6,4},{7,5},{8,10},{9,11},{10,... | collective-permute-start | bytes 1253384 | tf_op jit(solution)/shard_map/ppermute | solution.py:120
  6.4 12.3 %collective-permute-start = (bf16[272,768]{1,0:T(8,128)(2,1)S(1)}, bf16[272,768]{1,0:T(8,128)(2,1)S(1)}, u32[]{:S(2)}, u32[]{:S(2)}) collective-permute-start(bf16[272,768]{1,0:T(8,128)(2,1)S(1)} %pack.1.refs_0_.refs_3_.refs_2_), channel_id=1, source_target_pairs={{0,4},{1,5},{2,6},{3,7},{4,0},{5,1},{6,2},{7,3},{8,12},{9,13},{10,... | collective-permute-start | bytes 1253384 | tf_op jit(solution)/shard_map/ppermute | solution.py:120
  16.6 3.7 %collective-permute-start.5 = (bf16[272,768]{1,0:T(8,128)(2,1)S(1)}, bf16[272,768]{1,0:T(8,128)(2,1)S(1)}, u32[]{:S(2)}, u32[]{:S(2)}) collective-permute-start(bf16[272,768]{1,0:T(8,128)(2,1)S(1)} %pack.1.refs_0_.refs_3_.refs_2_), channel_id=1, source_target_pairs={{0,1},{1,0},{2,3},{3,2},{4,5},{5,4},{6,7},{7,6},{8,9},{9,8},{10,11... | collective-permute-start | bytes 1253384 | tf_op jit(solution)/shard_map/ppermute | solution.py:120
  16.6 3.7 %collective-permute-start.6 = (bf16[272,768]{1,0:T(8,128)(2,1)S(1)}, bf16[272,768]{1,0:T(8,128)(2,1)S(1)}, u32[]{:S(2)}, u32[]{:S(2)}) collective-permute-start(bf16[272,768]{1,0:T(8,128)(2,1)S(1)} %collective-permute-done.4.refs_5_.refs_4_), channel_id=1, source_target_pairs={{0,1},{1,0},{2,3},{3,2},{4,5},{5,4},{6,7},{7,6},{8,9},{9,8},{10,11... | collective-permute-start | bytes 1253384 | tf_op jit(solution)/shard_map/ppermute | solution.py:120
  17.1 13.3 %collective-permute-start.11 = (bf16[272,768]{1,0:T(8,128)(2,1)S(1)}, bf16[272,768]{1,0:T(8,128)(2,1)S(1)}, u32[]{:S(2)}, u32[]{:S(2)}) collective-permute-start(bf16[272,768]{1,0:T(8,128)(2,1)S(1)} %collective-permute-done.4.refs_5_.refs_4_), channel_id=1, source_target_pairs={{0,8},{8,16},{16,24},{24,0},{1,9},{9,17},{17,25},{25,1},{2,10},{10... | collective-permute-start | bytes 1253384 | tf_op jit(solution)/shard_map/ppermute | solution.py:126
  17.1 8.9 %collective-permute-start.3 = (bf16[144,768]{1,0:T(8,128)(2,1)S(1)}, bf16[144,768]{1,0:T(8,128)(2,1)S(1)}, u32[]{:S(2)}, u32[]{:S(2)}) collective-permute-start(bf16[144,768]{1,0:T(8,128)(2,1)S(1)} %slice.9), channel_id=1, source_target_pairs={{0,4},{1,5},{2,6},{3,7},{4,0},{5,1},{6,2},{7,3},{8,12},{9,13},{10,... | collective-permute-start | bytes 663560 | tf_op jit(solution)/shard_map/ppermute | solution.py:120
  18.7 7.3 %collective-permute-start.1 = (bf16[128,768]{1,0:T(8,128)(2,1)S(1)}, bf16[128,768]{1,0:T(8,128)(2,1)S(1)}, u32[]{:S(2)}, u32[]{:S(2)}) collective-permute-start(bf16[128,768]{1,0:T(8,128)(2,1)S(1)} %slice.8), channel_id=1, source_target_pairs={{0,2},{1,3},{2,0},{3,1},{4,6},{5,7},{6,4},{7,5},{8,10},{9,11},{10,... | collective-permute-start | bytes 589832 | tf_op jit(solution)/shard_map/ppermute | solution.py:120
  21.8 3.6 %collective-permute-start.7 = (f32[1,1,256]{2,1,0:T(1,128)S(1)}, f32[1,1,256]{2,1,0:T(1,128)S(1)}, u32[]{:S(2)}, u32[]{:S(2)}) collective-permute-start(f32[1,1,256]{2,1,0:T(1,128)S(1)} %get-tuple-element.21), channel_id=1, source_target_pairs={{0,2},{1,3},{2,0},{3,1},{4,6},{5,7},{6,4},{7,5},{8,10},{9,11},{10,... | collective-permute-start | bytes 3080 | tf_op jit(solution)/shard_map/ppermute | solution.py:120
  22.4 3.6 %collective-permute-start.8 = (f32[1,1,256]{2,1,0:T(1,128)S(1)}, f32[1,1,256]{2,1,0:T(1,128)S(1)}, u32[]{:S(2)}, u32[]{:S(2)}) collective-permute-start(f32[1,1,256]{2,1,0:T(1,128)S(1)} %get-tuple-element.22), channel_id=1, source_target_pairs={{0,4},{1,5},{2,6},{3,7},{4,0},{5,1},{6,2},{7,3},{8,12},{9,13},{10,... | collective-permute-start | bytes 3080 | tf_op jit(solution)/shard_map/ppermute | solution.py:120
  26.7 1.2 %collective-permute-start.9 = (f32[2,1,256]{2,1,0:T(1,128)S(1)}, f32[2,1,256]{2,1,0:T(1,128)S(1)}, u32[]{:S(2)}, u32[]{:S(2)}) collective-permute-start(f32[2,1,256]{2,1,0:T(1,128)S(1)} %get-tuple-element.26), channel_id=1, source_target_pairs={{0,1},{1,0},{2,3},{3,2},{4,5},{5,4},{6,7},{7,6},{8,9},{9,8},{10,11... | collective-permute-start | bytes 6152 | tf_op jit(solution)/shard_map/ppermute | solution.py:120
  30.5 4.5 %collective-permute-start.13 = (bf16[272,768]{1,0:T(8,128)(2,1)S(1)}, bf16[272,768]{1,0:T(8,128)(2,1)S(1)}, u32[]{:S(2)}, u32[]{:S(2)}) collective-permute-start(bf16[272,768]{1,0:T(8,128)(2,1)S(1)} %collective-permute-done.11.refs_5_), channel_id=1, source_target_pairs={{0,1},{1,0},{2,3},{3,2},{4,5},{5,4},{6,7},{7,6},{8,9},{9,8},{10,11... | collective-permute-start | bytes 1253384 | tf_op jit(solution)/shard_map/ppermute | solution.py:120
  30.5 4.5 %collective-permute-start.14 = (f32[1,1,256]{2,1,0:T(1,128)S(1)}, f32[1,1,256]{2,1,0:T(1,128)S(1)}, u32[]{:S(2)}, u32[]{:S(2)}) collective-permute-start(f32[1,1,256]{2,1,0:T(1,128)S(1)} %get-tuple-element.31), channel_id=1, source_target_pairs={{0,6},{1,7},{2,4},{3,5},{4,2},{5,3},{6,0},{7,1},{8,14},{9,15},{10,... | collective-permute-start | bytes 3080 | tf_op jit(solution)/shard_map/ppermute | solution.py:120
  33.5 4.5 %collective-permute-start.12 = (f32[1,1,256]{2,1,0:T(1,128)S(1)}, f32[1,1,256]{2,1,0:T(1,128)S(1)}, u32[]{:S(2)}, u32[]{:S(2)}) collective-permute-start(f32[1,1,256]{2,1,0:T(1,128)S(1)} %compare_half_way.1), channel_id=1, source_target_pairs={{0,16},{8,24},{16,0},{24,8},{1,17},{9,25},{17,1},{25,9},{2,18},{10... | collective-permute-start | bytes 3080 | tf_op jit(solution)/shard_map/ppermute | solution.py:126
  33.6 4.5 %collective-permute-start.10 = (f32[1,1,256]{2,1,0:T(1,128)S(1)}, f32[1,1,256]{2,1,0:T(1,128)S(1)}, u32[]{:S(2)}, u32[]{:S(2)}) collective-permute-start(f32[1,1,256]{2,1,0:T(1,128)S(1)} %bitcast.20), channel_id=1, source_target_pairs={{0,24},{8,0},{16,8},{24,16},{1,25},{9,1},{17,9},{25,17},{2,26},{10... | collective-permute-start | bytes 3080 | tf_op jit(solution)/shard_map/ppermute | solution.py:126
  35.6 4.0 %collective-permute-start.15 = (f32[1,1,256]{2,1,0:T(1,128)S(1)}, f32[1,1,256]{2,1,0:T(1,128)S(1)}, u32[]{:S(2)}, u32[]{:S(2)}) collective-permute-start(f32[1,1,256]{2,1,0:T(1,128)S(1)} %compare_twin.1), channel_id=1, source_target_pairs={{0,17},{1,16},{2,19},{3,18},{4,21},{5,20},{6,23},{7,22},{8,25},{9,... | collective-permute-start | bytes 3080 | tf_op jit(solution)/shard_map/ppermute | solution.py:130

commit v4 on v3

--- a/solution.py
+++ b/solution.py
@@ -8,6 +8,7 @@
 from jax.sharding import PartitionSpec as P
 
 CLUSTERS = 64
+LANES = 128
 TAIL = 16
 VMEM = 24 << 20
 VMEM_SMALL = 8 << 20
@@ -17,25 +18,30 @@
     rows, width = emb_ref.shape
     x = emb_ref[...].astype(jnp.float32)
     scale = lax.rsqrt(jnp.sum(x * x, axis=1, keepdims=True) + 1e-06)
-    out_ref[:rows, :] = (x * scale).astype(jnp.bfloat16)
-    key = target_ref[...] // per_group * CLUSTERS + cluster_ref[...] + 1
-    key = jnp.concatenate([key, jnp.zeros((1, width - rows), jnp.int32)], axis=1)
-    key = jnp.broadcast_to(key.astype(jnp.float32), (TAIL, width))
-    out_ref[rows:, :] = key.astype(jnp.bfloat16)
+    normed = (x * scale).astype(jnp.bfloat16)
+    for at in range(width // LANES):
+        out_ref[at * rows : (at + 1) * rows, :] = normed[:, at * LANES : (at + 1) * LANES]
+    key = (target_ref[...] // per_group * CLUSTERS + cluster_ref[...] + 1).astype(jnp.float32)
+    tail = [key[:, at : at + LANES] for at in range(0, rows, LANES)]
+    tail.append(jnp.zeros((TAIL - len(tail), LANES), jnp.float32))
+    out_ref[out_ref.shape[0] - TAIL :, :] = jnp.concatenate(tail, axis=0).astype(jnp.bfloat16)
 
 
 def pack(embeddings, target, cluster, per_group):
     rows, width = embeddings.shape
     return pl.pallas_call(
         functools.partial(pack_kernel, per_group),
-        out_shape=jax.ShapeDtypeStruct((rows + TAIL, width), jnp.bfloat16),
+        out_shape=jax.ShapeDtypeStruct((rows * width // LANES + TAIL, LANES), jnp.bfloat16),
         compiler_params=pltpu.CompilerParams(vmem_limit_bytes=VMEM_SMALL),
         name="pack",
     )(embeddings, target.reshape(1, rows), cluster.reshape(1, rows))
 
 
-def whole(pieces):
-    return pieces[0][...] if len(pieces) == 1 else jnp.concatenate([ref[...] for ref in pieces], axis=0)
+def unpack(pieces, rows):
+    panels = [ref[at : at + rows, :] for ref in pieces for at in range(0, ref.shape[0] - rows + 1, rows)]
+    tail = pieces[-1][pieces[-1].shape[0] - TAIL :, :].astype(jnp.float32)
+    keys = [tail[at : at + 1, :] for at in range(rows // LANES)]
+    return jnp.concatenate(panels, axis=1), jnp.concatenate(keys, axis=1)
 
 
 def score_kernel(counts, n_cols, pairs, want_rows, known, outs, *refs):
@@ -45,16 +51,18 @@
     best = [jnp.full((1, rows), -1.0, jnp.float32)] * n_cols
     for at, col in enumerate(known):
         best[col] = cols_in[0][at]
+    cols = [unpack([ref], rows) for ref in cols]
     for k, pieces in enumerate(plane):
-        block = whole(pieces)
-        row_keys = jnp.transpose(jnp.broadcast_to(block[rows:, :rows].astype(jnp.float32)[:1], (128, rows)))
-        row_keys = jnp.concatenate([row_keys] * (rows // 128), axis=1)
+        block, keys = unpack(pieces, rows)
+        row_keys = jnp.transpose(jnp.broadcast_to(keys, (LANES, rows)))
+        row_keys = jnp.concatenate([row_keys] * (rows // LANES), axis=1)
         row_best = None
         for at, same in [(at, same) for one, at, same in pairs if one == k]:
+            col, col_keys = cols[at]
             scores = lax.dot_general(
-                block[:rows], cols[at][:rows, :], (((1,), (1,)), ((), ())), preferred_element_type=jnp.float32
+                block, col, (((1,), (1,)), ((), ())), preferred_element_type=jnp.float32
             )
-            allowed = row_keys == cols[at][rows:, :rows].astype(jnp.float32)[:1]
+            allowed = row_keys == col_keys
             if same:
                 one = lax.broadcasted_iota(jnp.int32, scores.shape, 0)
                 other = lax.broadcasted_iota(jnp.int32, scores.shape, 1)
@@ -62,8 +70,8 @@
             masked = jnp.where(allowed, scores, -1.0)
             best[at] = jnp.maximum(best[at], jnp.max(masked, axis=0, keepdims=True))
             if at in want_rows:
-                for lane in range(0, rows, 128):
-                    part = masked[:, lane : lane + 128]
+                for lane in range(0, rows, LANES):
+                    part = masked[:, lane : lane + LANES]
                     row_best = part if row_best is None else jnp.maximum(row_best, part)
         if row_best is not None:
             row_outs[k][0] = jnp.max(jnp.transpose(row_best), axis=0, keepdims=True)
@@ -80,9 +88,8 @@
     return groups
 
 
-def score(name, plane, cols, pairs, want_rows, outs, known=(), cols_in=()):
-    length, width = cols[0].shape
-    rows = length - TAIL
+def score(name, rows, plane, cols, pairs, want_rows, outs, known=(), cols_in=()):
+    size = cols[0].size
     counts = tuple(len(pieces) for pieces in plane)
     kernel = functools.partial(
         score_kernel, counts, len(cols), tuple(pairs), tuple(want_rows), tuple(known), tuple(outs)
@@ -93,8 +100,8 @@
         out_shape=[jax.ShapeDtypeStruct((count, 1, rows), jnp.float32) for count in shapes],
         compiler_params=pltpu.CompilerParams(vmem_limit_bytes=VMEM),
         cost_estimate=pl.CostEstimate(
-            flops=2 * len(pairs) * rows * rows * width,
-            bytes_accessed=2 * (len(plane) + len(cols)) * length * width,
+            flops=2 * len(pairs) * rows * size,
+            bytes_accessed=2 * (len(plane) + len(cols)) * size,
             transcendentals=0,
         ),
         name=name,
@@ -130,8 +137,8 @@
     return lax.ppermute(x, ("grp", "blk"), pairs)
 
 
-def fetch_plane(packed, per_group):
-    half = (packed.shape[0] - TAIL) // 2
+def fetch_plane(packed, rows, per_group):
+    half = packed.shape[0] // rows // 2 * rows
     plane = {0: (packed,)}
     halves = {}
     for mask in sorted(range(2, per_group, 2), key=lambda mask: mask.bit_count()):
@@ -151,9 +158,10 @@
 def body(embeddings, target, cluster):
     groups = lax.axis_size("grp")
     per_group = lax.axis_size("blk")
+    rows = embeddings.shape[0]
     packed = pack(embeddings, target, cluster, per_group)
     one_off = grp_shift(packed, 1)
-    plane = fetch_plane(packed, per_group)
+    plane = fetch_plane(packed, rows, per_group)
     own_then = lax.optimization_barrier((packed, one_off))[0]
     own_twin = plane_shift(own_then, 1)
     half_way = grp_shift(one_off, 1)
@@ -164,6 +172,7 @@
     every = range(len(cols))
     best, *rows_direct = score(
         "compare_direct",
+        rows,
         [plane[mask] for mask in direct],
         cols,
         [(k, at, k == at == 0) for k in range(len(direct)) for at in every],
@@ -174,6 +183,7 @@
     best = lax.optimization_barrier((best, early))[0]
     own, one_off_best, twins, *rows_relayed = score(
         "compare_relayed",
+        rows,
         [plane[mask] for mask in relayed],
         cols,
         [(k, at, False) for k in range(len(relayed)) for at in every],
@@ -192,7 +202,7 @@
     half_then = lax.optimization_barrier((half_way, own))[0]
     half_twin = lax.optimization_barrier((plane_shift(half_then, 1), early))[0]
     for name, block, mask in (("compare_half_way", half_way, 0), ("compare_twin", half_twin, 1)):
-        (half_best,) = score(name, blocks, [block], pairs, (), [(0,)])
+        (half_best,) = score(name, rows, blocks, [block], pairs, (), [(0,)])
         found.append(grp_shift(half_best, groups // 2, mask))
     return functools.reduce(jnp.maximum, found + early).reshape(-1)
 

time: 40.3 us -> 39.4 us (0.978)
  waiting for transfers between devices: 18 us -> 17 us
    ppermute x4, waiting for transfers between devices: 12.5 us -> 11.6 us  [grp_shift(): lax.ppermute(x, 'grp', [(z, (z + shift) % groups) for z in range(groups)])]
where the time goes in v4:
time: 39.4 us; the launch traced here: 39.2 us
  waiting for transfers between devices  17 us (43%)
  starting transfers between devices  16.2 us (41%)
  Pallas kernels  3.65 us (9%)
  local copies, waits for them, and re-layouts  1.72 us (4%)
  other arithmetic  0.57 us (1%)
    ppermute x4, waiting for transfers between devices, grp_shift(): lax.ppermute(x, 'grp', [(z, (z + shift) % groups) for z in range(groups)])  11.6 us
    ppermute x11, starting transfers between devices, plane_shift(): return lax.ppermute(x, 'blk', [(i, i ^ mask) for i in range(size)])  10.8 us
    ppermute x4, starting transfers between devices, grp_shift(): lax.ppermute(x, 'grp', [(z, (z + shift) % groups) for z in range(groups)])  4.13 us
    ppermute x11, waiting for transfers between devices, plane_shift(): return lax.ppermute(x, 'blk', [(i, i ^ mask) for i in range(size)])  3.98 us
    pallas_call x4, Pallas kernels, score(): pl.pallas_call(kernel, out_shape=[jax.ShapeDtypeStruct((count, 1, rows),...  3.48 us
    unnamed x6, local copies, waits for them, and re-layouts  1.69 us
    ppermute x1, waiting for transfers between devices, grp_shift(): return lax.ppermute(x, ('grp', 'blk'), pairs)  1.45 us
    ppermute x1, starting transfers between devices, grp_shift(): return lax.ppermute(x, ('grp', 'blk'), pairs)  1.23 us
  transfers between devices with their start and end apart: 16, of which 8 were waited for; matrix products, arithmetic and copies ran while one was open for 0% of the time, Pallas kernels for 9%

profile of v4, /device:TPU:0, one launch (start us, length us, event | category | flops | bytes accessed | tf_op | source)
XLA Modules:
  0.0 39.2 jit_solution(13487238427531976194)
XLA Ops:
  0.0 0.7 %copy-done.2 = s32[256]{0:T(256)S(1)} copy-done((s32[256]{0:T(256)S(1)}, s32[256]{0:T(256)}, u32[]{:S(2)}) %copy-start.2) | copy-done | bytes 1048
  0.7 0.0 copy-done.1
  0.7 1.0 %copy-done = bf16[256,768]{1,0:T(8,128)(2,1)S(1)} copy-done((bf16[256,768]{1,0:T(8,128)(2,1)S(1)}, bf16[256,768]{1,0:T(8,128)(2,1)}, u32[]{:S(2)}) %copy-start) | copy-done | bytes 393240
  1.7 0.2 pack.1.refs_0_.refs_3_.refs_2_
  1.9 3.1 %collective-permute-start.4 = (bf16[1552,128]{1,0:T(8,128)(2,1)S(1)}, bf16[1552,128]{1,0:T(8,128)(2,1)S(1)}, u32[]{:S(2)}, u32[]{:S(2)}) collective-permute-start(bf16[1552,128]{1,0:T(8,128)(2,1)S(1)} %pack.1.refs_0_.refs_3_.refs_2_), channel_id=1, source_target_pairs={{0,8},{8,16},{16,24},{24,0},{1,9},{9,17},{17,25},{25,1},{2,10},{10... | collective-permute-start | bytes 1191944 | tf_op jit(solution)/shard_map/ppermute | solution.py:133
  4.9 1.5 %collective-permute-start.2 = (bf16[1552,128]{1,0:T(8,128)(2,1)S(1)}, bf16[1552,128]{1,0:T(8,128)(2,1)S(1)}, u32[]{:S(2)}, u32[]{:S(2)}) collective-permute-start(bf16[1552,128]{1,0:T(8,128)(2,1)S(1)} %pack.1.refs_0_.refs_3_.refs_2_), channel_id=1, source_target_pairs={{0,2},{1,3},{2,0},{3,1},{4,6},{5,7},{6,4},{7,5},{8,10},{9,11},{10,... | collective-permute-start | bytes 1191944 | tf_op jit(solution)/shard_map/ppermute | solution.py:127
  6.4 1.5 %collective-permute-start = (bf16[1552,128]{1,0:T(8,128)(2,1)S(1)}, bf16[1552,128]{1,0:T(8,128)(2,1)S(1)}, u32[]{:S(2)}, u32[]{:S(2)}) collective-permute-start(bf16[1552,128]{1,0:T(8,128)(2,1)S(1)} %pack.1.refs_0_.refs_3_.refs_2_), channel_id=1, source_target_pairs={{0,4},{1,5},{2,6},{3,7},{4,0},{5,1},{6,2},{7,3},{8,12},{9,13},{10,... | collective-permute-start | bytes 1191944 | tf_op jit(solution)/shard_map/ppermute | solution.py:127
  7.9 8.2 %collective-permute-done.4.refs_5_.refs_4_ = bf16[1552,128]{1,0:T(8,128)(2,1)S(1)} collective-permute-done((bf16[1552,128]{1,0:T(8,128)(2,1)S(1)}, bf16[1552,128]{1,0:T(8,128)(2,1)S(1)}, u32[]{:S(2)}, u32[]{:S(2)}) %collective-permute-start.4) | collective-permute-done | bytes 397344 | tf_op jit(solution)/shard_map/ppermute | solution.py:133
  16.2 0.5 %collective-permute-start.6 = (bf16[1552,128]{1,0:T(8,128)(2,1)S(1)}, bf16[1552,128]{1,0:T(8,128)(2,1)S(1)}, u32[]{:S(2)}, u32[]{:S(2)}) collective-permute-start(bf16[1552,128]{1,0:T(8,128)(2,1)S(1)} %collective-permute-done.4.refs_5_.refs_4_), channel_id=1, source_target_pairs={{0,1},{1,0},{2,3},{3,2},{4,5},{5,4},{6,7},{7,6},{8,9},{9,8},{10,11... | collective-permute-start | bytes 1191944 | tf_op jit(solution)/shard_map/ppermute | solution.py:127
  16.7 0.0 collective-permute-start.11
  16.7 0.0 collective-permute-done.2.refs_1_
  16.7 1.6 %collective-permute-start.3 = (bf16[784,128]{1,0:T(8,128)(2,1)S(1)}, bf16[784,128]{1,0:T(8,128)(2,1)S(1)}, u32[]{:S(2)}, u32[]{:S(2)}) collective-permute-start(bf16[784,128]{1,0:T(8,128)(2,1)S(1)} %slice.9), channel_id=1, source_target_pairs={{0,4},{1,5},{2,6},{3,7},{4,0},{5,1},{6,2},{7,3},{8,12},{9,13},{10,... | collective-permute-start | bytes 602120 | tf_op jit(solution)/shard_map/ppermute | solution.py:127
  18.3 1.6 %collective-permute-start.1 = (bf16[768,128]{1,0:T(8,128)(2,1)S(1)}, bf16[768,128]{1,0:T(8,128)(2,1)S(1)}, u32[]{:S(2)}, u32[]{:S(2)}) collective-permute-start(bf16[768,128]{1,0:T(8,128)(2,1)S(1)} %slice.8), channel_id=1, source_target_pairs={{0,2},{1,3},{2,0},{3,1},{4,6},{5,7},{6,4},{7,5},{8,10},{9,11},{10,... | collective-permute-start | bytes 589832 | tf_op jit(solution)/shard_map/ppermute | solution.py:127
  19.9 1.5 %compare_direct.1 = (f32[4,1,256]{2,1,0:T(1,128)S(1)}, f32[1,1,256]{2,1,0:T(1,128)S(1)}, f32[1,1,256]{2,1,0:T(1,128)S(1)}, f32[1,1,256]{2,1,0:T(1,128)S(1)}) custom-call(bf16[1552,128]{1,0:T(8,128)(2,1)S(1)} %pack.1.refs_0_.refs_3_.refs_2_, bf16[1552,128]{1,0:T(8,128)(2,1)S(1)} %collective-permute-done.2.refs_1_, ...), custom_call_target="tpu_custom_call" | custom-call | flops 1220542464 | bytes 2781184 | tf_op jit(solution)/shard_map/compare_direct/pallas_call | solution.py:98
  21.4 0.6 %collective-permute-start.7 = (f32[1,1,256]{2,1,0:T(1,128)S(1)}, f32[1,1,256]{2,1,0:T(1,128)S(1)}, u32[]{:S(2)}, u32[]{:S(2)}) collective-permute-start(f32[1,1,256]{2,1,0:T(1,128)S(1)} %get-tuple-element.21), channel_id=1, source_target_pairs={{0,2},{1,3},{2,0},{3,1},{4,6},{5,7},{6,4},{7,5},{8,10},{9,11},{10,... | collective-permute-start | bytes 3080 | tf_op jit(solution)/shard_map/ppermute | solution.py:127
  22.0 1.1 %collective-permute-start.8 = (f32[1,1,256]{2,1,0:T(1,128)S(1)}, f32[1,1,256]{2,1,0:T(1,128)S(1)}, u32[]{:S(2)}, u32[]{:S(2)}) collective-permute-start(f32[1,1,256]{2,1,0:T(1,128)S(1)} %get-tuple-element.22), channel_id=1, source_target_pairs={{0,4},{1,5},{2,6},{3,7},{4,0},{5,1},{6,2},{7,3},{8,12},{9,13},{10,... | collective-permute-start | bytes 3080 | tf_op jit(solution)/shard_map/ppermute | solution.py:127
  23.1 2.0 %collective-permute-done.7 = f32[1,1,256]{2,1,0:T(1,128)S(1)} collective-permute-done((f32[1,1,256]{2,1,0:T(1,128)S(1)}, f32[1,1,256]{2,1,0:T(1,128)S(1)}, u32[]{:S(2)}, u32[]{:S(2)}) %collective-permute-start.7) | collective-permute-done | bytes 1056 | tf_op jit(solution)/shard_map/ppermute | solution.py:127
  25.0 0.5 %collective-permute-done.8 = f32[1,1,256]{2,1,0:T(1,128)S(1)} collective-permute-done((f32[1,1,256]{2,1,0:T(1,128)S(1)}, f32[1,1,256]{2,1,0:T(1,128)S(1)}, u32[]{:S(2)}, u32[]{:S(2)}) %collective-permute-start.8) | collective-permute-done | bytes 1056 | tf_op jit(solution)/shard_map/ppermute | solution.py:127
  25.6 0.7 %compare_relayed.1 = (f32[1,1,256]{2,1,0:T(1,128)S(1)}, f32[1,1,256]{2,1,0:T(1,128)S(1)}, f32[2,1,256]{2,1,0:T(1,128)S(1)}, f32[1,1,256]{2,1,0:T(1,128)S(1)}) custom-call(bf16[768,128]{1,0:T(8,128)(2,1)S(1)} %collective-permute-done.1.refs_0_.refs_3_, bf16[784,128]{1,0:T(8,128)(2,1)S(1)} %collective-permute-done.3.refs_1_.refs_4_, ...), custom_call_target="tpu_custom_call" | custom-call | flops 406847488 | bytes 1986560 | tf_op jit(solution)/shard_map/compare_relayed/pallas_call | solution.py:98
  26.3 0.1 collective-permute-start.9
  26.3 1.1 %collective-permute-done.9.refs_2_ = f32[2,1,256]{2,1,0:T(1,128)S(1)} collective-permute-done((f32[2,1,256]{2,1,0:T(1,128)S(1)}, f32[2,1,256]{2,1,0:T(1,128)S(1)}, u32[]{:S(2)}, u32[]{:S(2)}) %collective-permute-start.9) | collective-permute-done | bytes 2080 | tf_op jit(solution)/shard_map/ppermute | solution.py:127
  27.5 2.1 %collective-permute-done.11.refs_5_ = bf16[1552,128]{1,0:T(8,128)(2,1)S(1)} collective-permute-done((bf16[1552,128]{1,0:T(8,128)(2,1)S(1)}, bf16[1552,128]{1,0:T(8,128)(2,1)S(1)}, u32[]{:S(2)}, u32[]{:S(2)}) %collective-permute-start.11) | collective-permute-done | bytes 397344 | tf_op jit(solution)/shard_map/ppermute | solution.py:133
  29.6 2.4 %collective-permute-start.14 = (f32[1,1,256]{2,1,0:T(1,128)S(1)}, f32[1,1,256]{2,1,0:T(1,128)S(1)}, u32[]{:S(2)}, u32[]{:S(2)}) collective-permute-start(f32[1,1,256]{2,1,0:T(1,128)S(1)} %get-tuple-element.31), channel_id=1, source_target_pairs={{0,6},{1,7},{2,4},{3,5},{4,2},{5,3},{6,0},{7,1},{8,14},{9,15},{10,... | collective-permute-start | bytes 3080 | tf_op jit(solution)/shard_map/ppermute | solution.py:127
  32.0 0.6 %compare_half_way.1 = f32[1,1,256]{2,1,0:T(1,128)S(1)} custom-call(bf16[1552,128]{1,0:T(8,128)(2,1)S(1)} %pack.1.refs_0_.refs_3_.refs_2_, bf16[1552,128]{1,0:T(8,128)(2,1)S(1)} %collective-permute-done.2.refs_1_, bf16[1552,128]{1,0:T(8,128)(2,1)S(1)} %collective-permute-done.refs_2_, bf16[768,128]{1,0:T(8,128)(2,1)S(1)} %collective-permute-done.1.refs_0_.refs_3_, ...), custom_call_target="tpu_custom_call" | custom-call | flops 406847488 | bytes 1986560 | tf_op jit(solution)/shard_map/compare_half_way/pallas_call | solution.py:98
  32.7 0.1 collective-permute-start.12
  32.7 1.0 %collective-permute-start.10 = (f32[1,1,256]{2,1,0:T(1,128)S(1)}, f32[1,1,256]{2,1,0:T(1,128)S(1)}, u32[]{:S(2)}, u32[]{:S(2)}) collective-permute-start(f32[1,1,256]{2,1,0:T(1,128)S(1)} %bitcast.20), channel_id=1, source_target_pairs={{0,24},{8,0},{16,8},{24,16},{1,25},{9,1},{17,9},{25,17},{2,26},{10... | collective-permute-start | bytes 3080 | tf_op jit(solution)/shard_map/ppermute | solution.py:133
  33.7 0.3 collective-permute-done.14
  34.1 0.6 %compare_twin.1 = f32[1,1,256]{2,1,0:T(1,128)S(1)} custom-call(bf16[1552,128]{1,0:T(8,128)(2,1)S(1)} %pack.1.refs_0_.refs_3_.refs_2_, bf16[1552,128]{1,0:T(8,128)(2,1)S(1)} %collective-permute-done.2.refs_1_, bf16[1552,128]{1,0:T(8,128)(2,1)S(1)} %collective-permute-done.refs_2_, bf16[768,128]{1,0:T(8,128)(2,1)S(1)} %collective-permute-done.1.refs_0_.refs_3_, ...), custom_call_target="tpu_custom_call" | custom-call | flops 406847488 | bytes 1986560 | tf_op jit(solution)/shard_map/compare_twin/pallas_call | solution.py:98
  34.7 1.2 %collective-permute-start.15 = (f32[1,1,256]{2,1,0:T(1,128)S(1)}, f32[1,1,256]{2,1,0:T(1,128)S(1)}, u32[]{:S(2)}, u32[]{:S(2)}) collective-permute-start(f32[1,1,256]{2,1,0:T(1,128)S(1)} %compare_twin.1), channel_id=1, source_target_pairs={{0,17},{1,16},{2,19},{3,18},{4,21},{5,20},{6,23},{7,22},{8,25},{9,... | collective-permute-start | bytes 3080 | tf_op jit(solution)/shard_map/ppermute | solution.py:137
  35.9 1.3 %collective-permute-done.12 = f32[1,1,256]{2,1,0:T(1,128)S(1)} collective-permute-done((f32[1,1,256]{2,1,0:T(1,128)S(1)}, f32[1,1,256]{2,1,0:T(1,128)S(1)}, u32[]{:S(2)}, u32[]{:S(2)}) %collective-permute-start.12) | collective-permute-done | bytes 1056 | tf_op jit(solution)/shard_map/ppermute | solution.py:133
  37.2 1.4 %collective-permute-done.15 = f32[1,1,256]{2,1,0:T(1,128)S(1)} collective-permute-done((f32[1,1,256]{2,1,0:T(1,128)S(1)}, f32[1,1,256]{2,1,0:T(1,128)S(1)}, u32[]{:S(2)}, u32[]{:S(2)}) %collective-permute-start.15) | collective-permute-done | bytes 1056 | tf_op jit(solution)/shard_map/ppermute | solution.py:137
  38.6 0.6 %maximum_maximum_fusion = f32[1,1,256]{2,1,0:T(1,128)} fusion(f32[1,1,256]{2,1,0:T(1,128)S(1)} %collective-permute-done.14, f32[1,1,256]{2,1,0:T(1,128)S(1)} %collective-permute-done.8, f32[1,1,256]{2,1,0:T(1,128)S(1)} %collective-permute-done.7, f32[1,1,256]{2,1,0:T(1,128)S(1)} %collective-permute-done.15, f32[1,1,256]{2,1,0:T(1,128)S(1)} %collective-permute-done.12, ...), kind=kLoop, calls=%fused_computation.4 | loop fusion | flops 1792 | bytes 9216 | tf_op jit(solution)/shard_map/max | solution.py:207
  (15 shorter events, 0.1 us)
Async XLA Ops:
  0.0 0.7 %copy-start.2 = (s32[256]{0:T(256)S(1)}, s32[256]{0:T(256)}, u32[]{:S(2)}) copy-start(s32[256]{0:T(256)} %param.5) | copy-start | bytes 3076
  0.0 0.7 %copy-start.1 = (s32[256,1]{0,1:T(1,128)S(1)}, s32[256,1]{0,1:T(1,128)}, u32[]{:S(2)}) copy-start(s32[256,1]{0,1:T(1,128)} %param.4) | copy-start | bytes 3076
  0.7 1.0 %copy-start = (bf16[256,768]{1,0:T(8,128)(2,1)S(1)}, bf16[256,768]{1,0:T(8,128)(2,1)}, u32[]{:S(2)}) copy-start(bf16[256,768]{1,0:T(8,128)(2,1)} %emb_ref.1) | copy-start | bytes 1179652
  1.9 14.3 %collective-permute-start.4 = (bf16[1552,128]{1,0:T(8,128)(2,1)S(1)}, bf16[1552,128]{1,0:T(8,128)(2,1)S(1)}, u32[]{:S(2)}, u32[]{:S(2)}) collective-permute-start(bf16[1552,128]{1,0:T(8,128)(2,1)S(1)} %pack.1.refs_0_.refs_3_.refs_2_), channel_id=1, source_target_pairs={{0,8},{8,16},{16,24},{24,0},{1,9},{9,17},{17,25},{25,1},{2,10},{10... | collective-permute-start | bytes 1191944 | tf_op jit(solution)/shard_map/ppermute | solution.py:133
  4.9 11.7 %collective-permute-start.2 = (bf16[1552,128]{1,0:T(8,128)(2,1)S(1)}, bf16[1552,128]{1,0:T(8,128)(2,1)S(1)}, u32[]{:S(2)}, u32[]{:S(2)}) collective-permute-start(bf16[1552,128]{1,0:T(8,128)(2,1)S(1)} %pack.1.refs_0_.refs_3_.refs_2_), channel_id=1, source_target_pairs={{0,2},{1,3},{2,0},{3,1},{4,6},{5,7},{6,4},{7,5},{8,10},{9,11},{10,... | collective-permute-start | bytes 1191944 | tf_op jit(solution)/shard_map/ppermute | solution.py:127
  6.4 11.9 %collective-permute-start = (bf16[1552,128]{1,0:T(8,128)(2,1)S(1)}, bf16[1552,128]{1,0:T(8,128)(2,1)S(1)}, u32[]{:S(2)}, u32[]{:S(2)}) collective-permute-start(bf16[1552,128]{1,0:T(8,128)(2,1)S(1)} %pack.1.refs_0_.refs_3_.refs_2_), channel_id=1, source_target_pairs={{0,4},{1,5},{2,6},{3,7},{4,0},{5,1},{6,2},{7,3},{8,12},{9,13},{10,... | collective-permute-start | bytes 1191944 | tf_op jit(solution)/shard_map/ppermute | solution.py:127
  16.2 3.7 %collective-permute-start.5 = (bf16[1552,128]{1,0:T(8,128)(2,1)S(1)}, bf16[1552,128]{1,0:T(8,128)(2,1)S(1)}, u32[]{:S(2)}, u32[]{:S(2)}) collective-permute-start(bf16[1552,128]{1,0:T(8,128)(2,1)S(1)} %pack.1.refs_0_.refs_3_.refs_2_), channel_id=1, source_target_pairs={{0,1},{1,0},{2,3},{3,2},{4,5},{5,4},{6,7},{7,6},{8,9},{9,8},{10,11... | collective-permute-start | bytes 1191944 | tf_op jit(solution)/shard_map/ppermute | solution.py:127
  16.2 3.7 %collective-permute-start.6 = (bf16[1552,128]{1,0:T(8,128)(2,1)S(1)}, bf16[1552,128]{1,0:T(8,128)(2,1)S(1)}, u32[]{:S(2)}, u32[]{:S(2)}) collective-permute-start(bf16[1552,128]{1,0:T(8,128)(2,1)S(1)} %collective-permute-done.4.refs_5_.refs_4_), channel_id=1, source_target_pairs={{0,1},{1,0},{2,3},{3,2},{4,5},{5,4},{6,7},{7,6},{8,9},{9,8},{10,11... | collective-permute-start | bytes 1191944 | tf_op jit(solution)/shard_map/ppermute | solution.py:127
  16.7 12.9 %collective-permute-start.11 = (bf16[1552,128]{1,0:T(8,128)(2,1)S(1)}, bf16[1552,128]{1,0:T(8,128)(2,1)S(1)}, u32[]{:S(2)}, u32[]{:S(2)}) collective-permute-start(bf16[1552,128]{1,0:T(8,128)(2,1)S(1)} %collective-permute-done.4.refs_5_.refs_4_), channel_id=1, source_target_pairs={{0,8},{8,16},{16,24},{24,0},{1,9},{9,17},{17,25},{25,1},{2,10},{10... | collective-permute-start | bytes 1191944 | tf_op jit(solution)/shard_map/ppermute | solution.py:133
  16.7 8.9 %collective-permute-start.3 = (bf16[784,128]{1,0:T(8,128)(2,1)S(1)}, bf16[784,128]{1,0:T(8,128)(2,1)S(1)}, u32[]{:S(2)}, u32[]{:S(2)}) collective-permute-start(bf16[784,128]{1,0:T(8,128)(2,1)S(1)} %slice.9), channel_id=1, source_target_pairs={{0,4},{1,5},{2,6},{3,7},{4,0},{5,1},{6,2},{7,3},{8,12},{9,13},{10,... | collective-permute-start | bytes 602120 | tf_op jit(solution)/shard_map/ppermute | solution.py:127
  18.3 7.3 %collective-permute-start.1 = (bf16[768,128]{1,0:T(8,128)(2,1)S(1)}, bf16[768,128]{1,0:T(8,128)(2,1)S(1)}, u32[]{:S(2)}, u32[]{:S(2)}) collective-permute-start(bf16[768,128]{1,0:T(8,128)(2,1)S(1)} %slice.8), channel_id=1, source_target_pairs={{0,2},{1,3},{2,0},{3,1},{4,6},{5,7},{6,4},{7,5},{8,10},{9,11},{10,... | collective-permute-start | bytes 589832 | tf_op jit(solution)/shard_map/ppermute | solution.py:127
  21.4 3.6 %collective-permute-start.7 = (f32[1,1,256]{2,1,0:T(1,128)S(1)}, f32[1,1,256]{2,1,0:T(1,128)S(1)}, u32[]{:S(2)}, u32[]{:S(2)}) collective-permute-start(f32[1,1,256]{2,1,0:T(1,128)S(1)} %get-tuple-element.21), channel_id=1, source_target_pairs={{0,2},{1,3},{2,0},{3,1},{4,6},{5,7},{6,4},{7,5},{8,10},{9,11},{10,... | collective-permute-start | bytes 3080 | tf_op jit(solution)/shard_map/ppermute | solution.py:127
  22.0 3.6 %collective-permute-start.8 = (f32[1,1,256]{2,1,0:T(1,128)S(1)}, f32[1,1,256]{2,1,0:T(1,128)S(1)}, u32[]{:S(2)}, u32[]{:S(2)}) collective-permute-start(f32[1,1,256]{2,1,0:T(1,128)S(1)} %get-tuple-element.22), channel_id=1, source_target_pairs={{0,4},{1,5},{2,6},{3,7},{4,0},{5,1},{6,2},{7,3},{8,12},{9,13},{10,... | collective-permute-start | bytes 3080 | tf_op jit(solution)/shard_map/ppermute | solution.py:127
  26.3 1.2 %collective-permute-start.9 = (f32[2,1,256]{2,1,0:T(1,128)S(1)}, f32[2,1,256]{2,1,0:T(1,128)S(1)}, u32[]{:S(2)}, u32[]{:S(2)}) collective-permute-start(f32[2,1,256]{2,1,0:T(1,128)S(1)} %get-tuple-element.26), channel_id=1, source_target_pairs={{0,1},{1,0},{2,3},{3,2},{4,5},{5,4},{6,7},{7,6},{8,9},{9,8},{10,11... | collective-permute-start | bytes 6152 | tf_op jit(solution)/shard_map/ppermute | solution.py:127
  29.6 4.5 %collective-permute-start.13 = (bf16[1552,128]{1,0:T(8,128)(2,1)S(1)}, bf16[1552,128]{1,0:T(8,128)(2,1)S(1)}, u32[]{:S(2)}, u32[]{:S(2)}) collective-permute-start(bf16[1552,128]{1,0:T(8,128)(2,1)S(1)} %collective-permute-done.11.refs_5_), channel_id=1, source_target_pairs={{0,1},{1,0},{2,3},{3,2},{4,5},{5,4},{6,7},{7,6},{8,9},{9,8},{10,11... | collective-permute-start | bytes 1191944 | tf_op jit(solution)/shard_map/ppermute | solution.py:127
  29.6 4.5 %collective-permute-start.14 = (f32[1,1,256]{2,1,0:T(1,128)S(1)}, f32[1,1,256]{2,1,0:T(1,128)S(1)}, u32[]{:S(2)}, u32[]{:S(2)}) collective-permute-start(f32[1,1,256]{2,1,0:T(1,128)S(1)} %get-tuple-element.31), channel_id=1, source_target_pairs={{0,6},{1,7},{2,4},{3,5},{4,2},{5,3},{6,0},{7,1},{8,14},{9,15},{10,... | collective-permute-start | bytes 3080 | tf_op jit(solution)/shard_map/ppermute | solution.py:127
  32.7 4.5 %collective-permute-start.12 = (f32[1,1,256]{2,1,0:T(1,128)S(1)}, f32[1,1,256]{2,1,0:T(1,128)S(1)}, u32[]{:S(2)}, u32[]{:S(2)}) collective-permute-start(f32[1,1,256]{2,1,0:T(1,128)S(1)} %compare_half_way.1), channel_id=1, source_target_pairs={{0,16},{8,24},{16,0},{24,8},{1,17},{9,25},{17,1},{25,9},{2,18},{10... | collective-permute-start | bytes 3080 | tf_op jit(solution)/shard_map/ppermute | solution.py:133
  32.7 4.5 %collective-permute-start.10 = (f32[1,1,256]{2,1,0:T(1,128)S(1)}, f32[1,1,256]{2,1,0:T(1,128)S(1)}, u32[]{:S(2)}, u32[]{:S(2)}) collective-permute-start(f32[1,1,256]{2,1,0:T(1,128)S(1)} %bitcast.20), channel_id=1, source_target_pairs={{0,24},{8,0},{16,8},{24,16},{1,25},{9,1},{17,9},{25,17},{2,26},{10... | collective-permute-start | bytes 3080 | tf_op jit(solution)/shard_map/ppermute | solution.py:133
  34.7 4.0 %collective-permute-start.15 = (f32[1,1,256]{2,1,0:T(1,128)S(1)}, f32[1,1,256]{2,1,0:T(1,128)S(1)}, u32[]{:S(2)}, u32[]{:S(2)}) collective-permute-start(f32[1,1,256]{2,1,0:T(1,128)S(1)} %compare_twin.1), channel_id=1, source_target_pairs={{0,17},{1,16},{2,19},{3,18},{4,21},{5,20},{6,23},{7,22},{8,25},{9,... | collective-permute-start | bytes 3080 | tf_op jit(solution)/shard_map/ppermute | solution.py:137

commit v5 on v4

--- a/solution.py
+++ b/solution.py
@@ -199,8 +199,8 @@
 
     blocks = list(plane.values())
     pairs = [(k, 0, False) for k in range(len(blocks))]
-    half_then = lax.optimization_barrier((half_way, own))[0]
-    half_twin = lax.optimization_barrier((plane_shift(half_then, 1), early))[0]
+    half_then = lax.optimization_barrier((half_way, own, early))[0]
+    half_twin = plane_shift(half_then, 1)
     for name, block, mask in (("compare_half_way", half_way, 0), ("compare_twin", half_twin, 1)):
         (half_best,) = score(name, rows, blocks, [block], pairs, (), [(0,)])
         found.append(grp_shift(half_best, groups // 2, mask))

time: 39.4 us -> 40.8 us (1.036)
  starting transfers between devices: 16.2 us -> 18.5 us
  waiting for transfers between devices: 17 us -> 16.1 us
    ppermute x4, starting transfers between devices: 4.13 us -> 7.03 us  [grp_shift(): lax.ppermute(x, 'grp', [(z, (z + shift) % groups) for z in range(groups)])]
    ppermute x4, waiting for transfers between devices: 11.6 us -> 9.95 us  [grp_shift(): lax.ppermute(x, 'grp', [(z, (z + shift) % groups) for z in range(groups)])]
    ppermute x11, starting transfers between devices: 10.8 us -> 9.9 us  [plane_shift(): return lax.ppermute(x, 'blk', [(i, i ^ mask) for i in range(size)])]
    ppermute x1, waiting for transfers between devices: 1.45 us -> 2.37 us  [grp_shift(): return lax.ppermute(x, ('grp', 'blk'), pairs)]
  transfers between devices with their start and end apart: 16 -> 16, of which waited for: 8 -> 6; matrix products, arithmetic and copies ran while one was open for 0% -> 0% of each run, Pallas kernels for 9% -> 9%
where the time goes in v5:
time: 40.8 us; the launch traced here: 40.6 us
  starting transfers between devices  18.5 us (45%)
  waiting for transfers between devices  16.1 us (39%)
  Pallas kernels  3.65 us (9%)
  local copies, waits for them, and re-layouts  1.72 us (4%)
  other arithmetic  0.57 us (1%)
    ppermute x4, waiting for transfers between devices, grp_shift(): lax.ppermute(x, 'grp', [(z, (z + shift) % groups) for z in range(groups)])  9.95 us
    ppermute x11, starting transfers between devices, plane_shift(): return lax.ppermute(x, 'blk', [(i, i ^ mask) for i in range(size)])  9.9 us
    ppermute x4, starting transfers between devices, grp_shift(): lax.ppermute(x, 'grp', [(z, (z + shift) % groups) for z in range(groups)])  7.03 us
    ppermute x11, waiting for transfers between devices, plane_shift(): return lax.ppermute(x, 'blk', [(i, i ^ mask) for i in range(size)])  3.81 us
    pallas_call x4, Pallas kernels, score(): pl.pallas_call(kernel, out_shape=[jax.ShapeDtypeStruct((count, 1, rows),...  3.48 us
    ppermute x1, waiting for transfers between devices, grp_shift(): return lax.ppermute(x, ('grp', 'blk'), pairs)  2.37 us
    unnamed x6, local copies, waits for them, and re-layouts  1.69 us
    ppermute x1, starting transfers between devices, grp_shift(): return lax.ppermute(x, ('grp', 'blk'), pairs)  1.58 us
  transfers between devices with their start and end apart: 16, of which 6 were waited for; matrix products, arithmetic and copies ran while one was open for 0% of the time, Pallas kernels for 9%

profile of v5, /device:TPU:0, one launch (start us, length us, event | category | flops | bytes accessed | tf_op | source)
XLA Modules:
  0.0 40.6 jit_solution(12061981526404694555)
XLA Ops:
  0.0 0.7 %copy-done.2 = s32[256]{0:T(256)S(1)} copy-done((s32[256]{0:T(256)S(1)}, s32[256]{0:T(256)}, u32[]{:S(2)}) %copy-start.2) | copy-done | bytes 1048
  0.7 0.0 copy-done.1
  0.7 1.0 %copy-done = bf16[256,768]{1,0:T(8,128)(2,1)S(1)} copy-done((bf16[256,768]{1,0:T(8,128)(2,1)S(1)}, bf16[256,768]{1,0:T(8,128)(2,1)}, u32[]{:S(2)}) %copy-start) | copy-done | bytes 393240
  1.7 0.2 pack.1.refs_0_.refs_3_.refs_2_
  1.9 3.1 %collective-permute-start.4 = (bf16[1552,128]{1,0:T(8,128)(2,1)S(1)}, bf16[1552,128]{1,0:T(8,128)(2,1)S(1)}, u32[]{:S(2)}, u32[]{:S(2)}) collective-permute-start(bf16[1552,128]{1,0:T(8,128)(2,1)S(1)} %pack.1.refs_0_.refs_3_.refs_2_), channel_id=1, source_target_pairs={{0,8},{8,16},{16,24},{24,0},{1,9},{9,17},{17,25},{25,1},{2,10},{10... | collective-permute-start | bytes 1191944 | tf_op jit(solution)/shard_map/ppermute | solution.py:133
  4.9 1.5 %collective-permute-start.2 = (bf16[1552,128]{1,0:T(8,128)(2,1)S(1)}, bf16[1552,128]{1,0:T(8,128)(2,1)S(1)}, u32[]{:S(2)}, u32[]{:S(2)}) collective-permute-start(bf16[1552,128]{1,0:T(8,128)(2,1)S(1)} %pack.1.refs_0_.refs_3_.refs_2_), channel_id=1, source_target_pairs={{0,2},{1,3},{2,0},{3,1},{4,6},{5,7},{6,4},{7,5},{8,10},{9,11},{10,... | collective-permute-start | bytes 1191944 | tf_op jit(solution)/shard_map/ppermute | solution.py:127
  6.4 1.5 %collective-permute-start = (bf16[1552,128]{1,0:T(8,128)(2,1)S(1)}, bf16[1552,128]{1,0:T(8,128)(2,1)S(1)}, u32[]{:S(2)}, u32[]{:S(2)}) collective-permute-start(bf16[1552,128]{1,0:T(8,128)(2,1)S(1)} %pack.1.refs_0_.refs_3_.refs_2_), channel_id=1, source_target_pairs={{0,4},{1,5},{2,6},{3,7},{4,0},{5,1},{6,2},{7,3},{8,12},{9,13},{10,... | collective-permute-start | bytes 1191944 | tf_op jit(solution)/shard_map/ppermute | solution.py:127
  7.9 8.2 %collective-permute-done.4.refs_5_.refs_4_ = bf16[1552,128]{1,0:T(8,128)(2,1)S(1)} collective-permute-done((bf16[1552,128]{1,0:T(8,128)(2,1)S(1)}, bf16[1552,128]{1,0:T(8,128)(2,1)S(1)}, u32[]{:S(2)}, u32[]{:S(2)}) %collective-permute-start.4) | collective-permute-done | bytes 397344 | tf_op jit(solution)/shard_map/ppermute | solution.py:133
  16.2 0.0 collective-permute-start.5
  16.2 0.5 %collective-permute-start.6 = (bf16[1552,128]{1,0:T(8,128)(2,1)S(1)}, bf16[1552,128]{1,0:T(8,128)(2,1)S(1)}, u32[]{:S(2)}, u32[]{:S(2)}) collective-permute-start(bf16[1552,128]{1,0:T(8,128)(2,1)S(1)} %collective-permute-done.4.refs_5_.refs_4_), channel_id=1, source_target_pairs={{0,1},{1,0},{2,3},{3,2},{4,5},{5,4},{6,7},{7,6},{8,9},{9,8},{10,11... | collective-permute-start | bytes 1191944 | tf_op jit(solution)/shard_map/ppermute | solution.py:127
  16.7 0.0 collective-permute-start.11
  16.7 0.0 collective-permute-done.2.refs_1_
  16.7 1.6 %collective-permute-start.3 = (bf16[784,128]{1,0:T(8,128)(2,1)S(1)}, bf16[784,128]{1,0:T(8,128)(2,1)S(1)}, u32[]{:S(2)}, u32[]{:S(2)}) collective-permute-start(bf16[784,128]{1,0:T(8,128)(2,1)S(1)} %slice.9), channel_id=1, source_target_pairs={{0,4},{1,5},{2,6},{3,7},{4,0},{5,1},{6,2},{7,3},{8,12},{9,13},{10,... | collective-permute-start | bytes 602120 | tf_op jit(solution)/shard_map/ppermute | solution.py:127
  18.3 0.0 collective-permute-done.refs_2_
  18.3 1.6 %collective-permute-start.1 = (bf16[768,128]{1,0:T(8,128)(2,1)S(1)}, bf16[768,128]{1,0:T(8,128)(2,1)S(1)}, u32[]{:S(2)}, u32[]{:S(2)}) collective-permute-start(bf16[768,128]{1,0:T(8,128)(2,1)S(1)} %slice.8), channel_id=1, source_target_pairs={{0,2},{1,3},{2,0},{3,1},{4,6},{5,7},{6,4},{7,5},{8,10},{9,11},{10,... | collective-permute-start | bytes 589832 | tf_op jit(solution)/shard_map/ppermute | solution.py:127
  19.9 1.5 %compare_direct.1 = (f32[4,1,256]{2,1,0:T(1,128)S(1)}, f32[1,1,256]{2,1,0:T(1,128)S(1)}, f32[1,1,256]{2,1,0:T(1,128)S(1)}, f32[1,1,256]{2,1,0:T(1,128)S(1)}) custom-call(bf16[1552,128]{1,0:T(8,128)(2,1)S(1)} %pack.1.refs_0_.refs_3_.refs_2_, bf16[1552,128]{1,0:T(8,128)(2,1)S(1)} %collective-permute-done.2.refs_1_, ...), custom_call_target="tpu_custom_call" | custom-call | flops 1220542464 | bytes 2781184 | tf_op jit(solution)/shard_map/compare_direct/pallas_call | solution.py:98
  21.4 0.6 %collective-permute-start.7 = (f32[1,1,256]{2,1,0:T(1,128)S(1)}, f32[1,1,256]{2,1,0:T(1,128)S(1)}, u32[]{:S(2)}, u32[]{:S(2)}) collective-permute-start(f32[1,1,256]{2,1,0:T(1,128)S(1)} %get-tuple-element.20), channel_id=1, source_target_pairs={{0,2},{1,3},{2,0},{3,1},{4,6},{5,7},{6,4},{7,5},{8,10},{9,11},{10,... | collective-permute-start | bytes 3080 | tf_op jit(solution)/shard_map/ppermute | solution.py:127
  22.0 1.1 %collective-permute-start.8 = (f32[1,1,256]{2,1,0:T(1,128)S(1)}, f32[1,1,256]{2,1,0:T(1,128)S(1)}, u32[]{:S(2)}, u32[]{:S(2)}) collective-permute-start(f32[1,1,256]{2,1,0:T(1,128)S(1)} %get-tuple-element.21), channel_id=1, source_target_pairs={{0,4},{1,5},{2,6},{3,7},{4,0},{5,1},{6,2},{7,3},{8,12},{9,13},{10,... | collective-permute-start | bytes 3080 | tf_op jit(solution)/shard_map/ppermute | solution.py:127
  23.1 2.0 %collective-permute-done.7 = f32[1,1,256]{2,1,0:T(1,128)S(1)} collective-permute-done((f32[1,1,256]{2,1,0:T(1,128)S(1)}, f32[1,1,256]{2,1,0:T(1,128)S(1)}, u32[]{:S(2)}, u32[]{:S(2)}) %collective-permute-start.7) | collective-permute-done | bytes 1056 | tf_op jit(solution)/shard_map/ppermute | solution.py:127
  25.0 0.5 %collective-permute-done.8 = f32[1,1,256]{2,1,0:T(1,128)S(1)} collective-permute-done((f32[1,1,256]{2,1,0:T(1,128)S(1)}, f32[1,1,256]{2,1,0:T(1,128)S(1)}, u32[]{:S(2)}, u32[]{:S(2)}) %collective-permute-start.8) | collective-permute-done | bytes 1056 | tf_op jit(solution)/shard_map/ppermute | solution.py:127
  25.6 0.7 %compare_relayed.1 = (f32[1,1,256]{2,1,0:T(1,128)S(1)}, f32[1,1,256]{2,1,0:T(1,128)S(1)}, f32[2,1,256]{2,1,0:T(1,128)S(1)}, f32[1,1,256]{2,1,0:T(1,128)S(1)}) custom-call(bf16[768,128]{1,0:T(8,128)(2,1)S(1)} %collective-permute-done.1.refs_0_.refs_3_, bf16[784,128]{1,0:T(8,128)(2,1)S(1)} %collective-permute-done.3.refs_1_.refs_4_, ...), custom_call_target="tpu_custom_call" | custom-call | flops 406847488 | bytes 1986560 | tf_op jit(solution)/shard_map/compare_relayed/pallas_call | solution.py:98
  26.3 0.1 collective-permute-start.9
  26.3 1.5 %collective-permute-start.13 = (f32[1,1,256]{2,1,0:T(1,128)S(1)}, f32[1,1,256]{2,1,0:T(1,128)S(1)}, u32[]{:S(2)}, u32[]{:S(2)}) collective-permute-start(f32[1,1,256]{2,1,0:T(1,128)S(1)} %get-tuple-element.29), channel_id=1, source_target_pairs={{0,6},{1,7},{2,4},{3,5},{4,2},{5,3},{6,0},{7,1},{8,14},{9,15},{10,... | collective-permute-start | bytes 3080 | tf_op jit(solution)/shard_map/ppermute | solution.py:127
  27.8 1.7 %collective-permute-done.11.refs_5_ = bf16[1552,128]{1,0:T(8,128)(2,1)S(1)} collective-permute-done((bf16[1552,128]{1,0:T(8,128)(2,1)S(1)}, bf16[1552,128]{1,0:T(8,128)(2,1)S(1)}, u32[]{:S(2)}, u32[]{:S(2)}) %collective-permute-start.11) | collective-permute-done | bytes 397344 | tf_op jit(solution)/shard_map/ppermute | solution.py:133
  29.6 1.3 %collective-permute-done.13 = f32[1,1,256]{2,1,0:T(1,128)S(1)} collective-permute-done((f32[1,1,256]{2,1,0:T(1,128)S(1)}, f32[1,1,256]{2,1,0:T(1,128)S(1)}, u32[]{:S(2)}, u32[]{:S(2)}) %collective-permute-start.13) | collective-permute-done | bytes 1056 | tf_op jit(solution)/shard_map/ppermute | solution.py:127
  30.9 0.6 %compare_half_way.1 = f32[1,1,256]{2,1,0:T(1,128)S(1)} custom-call(bf16[1552,128]{1,0:T(8,128)(2,1)S(1)} %pack.1.refs_0_.refs_3_.refs_2_, bf16[1552,128]{1,0:T(8,128)(2,1)S(1)} %collective-permute-done.2.refs_1_, bf16[1552,128]{1,0:T(8,128)(2,1)S(1)} %collective-permute-done.refs_2_, bf16[768,128]{1,0:T(8,128)(2,1)S(1)} %collective-permute-done.1.refs_0_.refs_3_, ...), custom_call_target="tpu_custom_call" | custom-call | flops 406847488 | bytes 1986560 | tf_op jit(solution)/shard_map/compare_half_way/pallas_call | solution.py:98
  31.5 2.4 %collective-permute-start.12 = (f32[1,1,256]{2,1,0:T(1,128)S(1)}, f32[1,1,256]{2,1,0:T(1,128)S(1)}, u32[]{:S(2)}, u32[]{:S(2)}) collective-permute-start(f32[1,1,256]{2,1,0:T(1,128)S(1)} %compare_half_way.1), channel_id=1, source_target_pairs={{0,16},{8,24},{16,0},{24,8},{1,17},{9,25},{17,1},{25,9},{2,18},{10... | collective-permute-start | bytes 3080 | tf_op jit(solution)/shard_map/ppermute | solution.py:133
  33.9 1.6 %collective-permute-start.10 = (f32[1,1,256]{2,1,0:T(1,128)S(1)}, f32[1,1,256]{2,1,0:T(1,128)S(1)}, u32[]{:S(2)}, u32[]{:S(2)}) collective-permute-start(f32[1,1,256]{2,1,0:T(1,128)S(1)} %bitcast.20), channel_id=1, source_target_pairs={{0,24},{8,0},{16,8},{24,16},{1,25},{9,1},{17,9},{25,17},{2,26},{10... | collective-permute-start | bytes 3080 | tf_op jit(solution)/shard_map/ppermute | solution.py:133
  35.5 0.6 %compare_twin.1 = f32[1,1,256]{2,1,0:T(1,128)S(1)} custom-call(bf16[1552,128]{1,0:T(8,128)(2,1)S(1)} %pack.1.refs_0_.refs_3_.refs_2_, bf16[1552,128]{1,0:T(8,128)(2,1)S(1)} %collective-permute-done.2.refs_1_, bf16[1552,128]{1,0:T(8,128)(2,1)S(1)} %collective-permute-done.refs_2_, bf16[768,128]{1,0:T(8,128)(2,1)S(1)} %collective-permute-done.1.refs_0_.refs_3_, ...), custom_call_target="tpu_custom_call" | custom-call | flops 406847488 | bytes 1986560 | tf_op jit(solution)/shard_map/compare_twin/pallas_call | solution.py:98
  36.1 1.6 %collective-permute-start.15 = (f32[1,1,256]{2,1,0:T(1,128)S(1)}, f32[1,1,256]{2,1,0:T(1,128)S(1)}, u32[]{:S(2)}, u32[]{:S(2)}) collective-permute-start(f32[1,1,256]{2,1,0:T(1,128)S(1)} %compare_twin.1), channel_id=1, source_target_pairs={{0,17},{1,16},{2,19},{3,18},{4,21},{5,20},{6,23},{7,22},{8,25},{9,... | collective-permute-start | bytes 3080 | tf_op jit(solution)/shard_map/ppermute | solution.py:137
  37.7 2.4 %collective-permute-done.15 = f32[1,1,256]{2,1,0:T(1,128)S(1)} collective-permute-done((f32[1,1,256]{2,1,0:T(1,128)S(1)}, f32[1,1,256]{2,1,0:T(1,128)S(1)}, u32[]{:S(2)}, u32[]{:S(2)}) %collective-permute-start.15) | collective-permute-done | bytes 1056 | tf_op jit(solution)/shard_map/ppermute | solution.py:137
  40.1 0.6 %maximum_maximum_fusion = f32[1,1,256]{2,1,0:T(1,128)} fusion(f32[1,1,256]{2,1,0:T(1,128)S(1)} %collective-permute-done.13, f32[1,1,256]{2,1,0:T(1,128)S(1)} %collective-permute-done.8, f32[1,1,256]{2,1,0:T(1,128)S(1)} %collective-permute-done.7, f32[1,1,256]{2,1,0:T(1,128)S(1)} %collective-permute-done.15, f32[1,1,256]{2,1,0:T(1,128)S(1)} %collective-permute-done.12, ...), kind=kLoop, calls=%fused_computation.4 | loop fusion | flops 1792 | bytes 9216 | tf_op jit(solution)/shard_map/max | solution.py:207
  (15 shorter events, 0.1 us)
Async XLA Ops:
  0.0 0.7 %copy-start.2 = (s32[256]{0:T(256)S(1)}, s32[256]{0:T(256)}, u32[]{:S(2)}) copy-start(s32[256]{0:T(256)} %param.5) | copy-start | bytes 3076
  0.0 0.7 %copy-start.1 = (s32[256,1]{0,1:T(1,128)S(1)}, s32[256,1]{0,1:T(1,128)}, u32[]{:S(2)}) copy-start(s32[256,1]{0,1:T(1,128)} %param.4) | copy-start | bytes 3076
  0.7 1.0 %copy-start = (bf16[256,768]{1,0:T(8,128)(2,1)S(1)}, bf16[256,768]{1,0:T(8,128)(2,1)}, u32[]{:S(2)}) copy-start(bf16[256,768]{1,0:T(8,128)(2,1)} %emb_ref.1) | copy-start | bytes 1179652
  1.9 14.3 %collective-permute-start.4 = (bf16[1552,128]{1,0:T(8,128)(2,1)S(1)}, bf16[1552,128]{1,0:T(8,128)(2,1)S(1)}, u32[]{:S(2)}, u32[]{:S(2)}) collective-permute-start(bf16[1552,128]{1,0:T(8,128)(2,1)S(1)} %pack.1.refs_0_.refs_3_.refs_2_), channel_id=1, source_target_pairs={{0,8},{8,16},{16,24},{24,0},{1,9},{9,17},{17,25},{25,1},{2,10},{10... | collective-permute-start | bytes 1191944 | tf_op jit(solution)/shard_map/ppermute | solution.py:133
  4.9 11.7 %collective-permute-start.2 = (bf16[1552,128]{1,0:T(8,128)(2,1)S(1)}, bf16[1552,128]{1,0:T(8,128)(2,1)S(1)}, u32[]{:S(2)}, u32[]{:S(2)}) collective-permute-start(bf16[1552,128]{1,0:T(8,128)(2,1)S(1)} %pack.1.refs_0_.refs_3_.refs_2_), channel_id=1, source_target_pairs={{0,2},{1,3},{2,0},{3,1},{4,6},{5,7},{6,4},{7,5},{8,10},{9,11},{10,... | collective-permute-start | bytes 1191944 | tf_op jit(solution)/shard_map/ppermute | solution.py:127
  6.4 11.9 %collective-permute-start = (bf16[1552,128]{1,0:T(8,128)(2,1)S(1)}, bf16[1552,128]{1,0:T(8,128)(2,1)S(1)}, u32[]{:S(2)}, u32[]{:S(2)}) collective-permute-start(bf16[1552,128]{1,0:T(8,128)(2,1)S(1)} %pack.1.refs_0_.refs_3_.refs_2_), channel_id=1, source_target_pairs={{0,4},{1,5},{2,6},{3,7},{4,0},{5,1},{6,2},{7,3},{8,12},{9,13},{10,... | collective-permute-start | bytes 1191944 | tf_op jit(solution)/shard_map/ppermute | solution.py:127
  16.2 3.7 %collective-permute-start.5 = (bf16[1552,128]{1,0:T(8,128)(2,1)S(1)}, bf16[1552,128]{1,0:T(8,128)(2,1)S(1)}, u32[]{:S(2)}, u32[]{:S(2)}) collective-permute-start(bf16[1552,128]{1,0:T(8,128)(2,1)S(1)} %pack.1.refs_0_.refs_3_.refs_2_), channel_id=1, source_target_pairs={{0,1},{1,0},{2,3},{3,2},{4,5},{5,4},{6,7},{7,6},{8,9},{9,8},{10,11... | collective-permute-start | bytes 1191944 | tf_op jit(solution)/shard_map/ppermute | solution.py:127
  16.2 3.7 %collective-permute-start.6 = (bf16[1552,128]{1,0:T(8,128)(2,1)S(1)}, bf16[1552,128]{1,0:T(8,128)(2,1)S(1)}, u32[]{:S(2)}, u32[]{:S(2)}) collective-permute-start(bf16[1552,128]{1,0:T(8,128)(2,1)S(1)} %collective-permute-done.4.refs_5_.refs_4_), channel_id=1, source_target_pairs={{0,1},{1,0},{2,3},{3,2},{4,5},{5,4},{6,7},{7,6},{8,9},{9,8},{10,11... | collective-permute-start | bytes 1191944 | tf_op jit(solution)/shard_map/ppermute | solution.py:127
  16.7 12.9 %collective-permute-start.11 = (bf16[1552,128]{1,0:T(8,128)(2,1)S(1)}, bf16[1552,128]{1,0:T(8,128)(2,1)S(1)}, u32[]{:S(2)}, u32[]{:S(2)}) collective-permute-start(bf16[1552,128]{1,0:T(8,128)(2,1)S(1)} %collective-permute-done.4.refs_5_.refs_4_), channel_id=1, source_target_pairs={{0,8},{8,16},{16,24},{24,0},{1,9},{9,17},{17,25},{25,1},{2,10},{10... | collective-permute-start | bytes 1191944 | tf_op jit(solution)/shard_map/ppermute | solution.py:133
  16.7 8.9 %collective-permute-start.3 = (bf16[784,128]{1,0:T(8,128)(2,1)S(1)}, bf16[784,128]{1,0:T(8,128)(2,1)S(1)}, u32[]{:S(2)}, u32[]{:S(2)}) collective-permute-start(bf16[784,128]{1,0:T(8,128)(2,1)S(1)} %slice.9), channel_id=1, source_target_pairs={{0,4},{1,5},{2,6},{3,7},{4,0},{5,1},{6,2},{7,3},{8,12},{9,13},{10,... | collective-permute-start | bytes 602120 | tf_op jit(solution)/shard_map/ppermute | solution.py:127
  18.3 7.3 %collective-permute-start.1 = (bf16[768,128]{1,0:T(8,128)(2,1)S(1)}, bf16[768,128]{1,0:T(8,128)(2,1)S(1)}, u32[]{:S(2)}, u32[]{:S(2)}) collective-permute-start(bf16[768,128]{1,0:T(8,128)(2,1)S(1)} %slice.8), channel_id=1, source_target_pairs={{0,2},{1,3},{2,0},{3,1},{4,6},{5,7},{6,4},{7,5},{8,10},{9,11},{10,... | collective-permute-start | bytes 589832 | tf_op jit(solution)/shard_map/ppermute | solution.py:127
  21.4 3.6 %collective-permute-start.7 = (f32[1,1,256]{2,1,0:T(1,128)S(1)}, f32[1,1,256]{2,1,0:T(1,128)S(1)}, u32[]{:S(2)}, u32[]{:S(2)}) collective-permute-start(f32[1,1,256]{2,1,0:T(1,128)S(1)} %get-tuple-element.20), channel_id=1, source_target_pairs={{0,2},{1,3},{2,0},{3,1},{4,6},{5,7},{6,4},{7,5},{8,10},{9,11},{10,... | collective-permute-start | bytes 3080 | tf_op jit(solution)/shard_map/ppermute | solution.py:127
  22.0 3.6 %collective-permute-start.8 = (f32[1,1,256]{2,1,0:T(1,128)S(1)}, f32[1,1,256]{2,1,0:T(1,128)S(1)}, u32[]{:S(2)}, u32[]{:S(2)}) collective-permute-start(f32[1,1,256]{2,1,0:T(1,128)S(1)} %get-tuple-element.21), channel_id=1, source_target_pairs={{0,4},{1,5},{2,6},{3,7},{4,0},{5,1},{6,2},{7,3},{8,12},{9,13},{10,... | collective-permute-start | bytes 3080 | tf_op jit(solution)/shard_map/ppermute | solution.py:127
  26.3 1.6 %collective-permute-start.9 = (f32[2,1,256]{2,1,0:T(1,128)S(1)}, f32[2,1,256]{2,1,0:T(1,128)S(1)}, u32[]{:S(2)}, u32[]{:S(2)}) collective-permute-start(f32[2,1,256]{2,1,0:T(1,128)S(1)} %get-tuple-element.25), channel_id=1, source_target_pairs={{0,1},{1,0},{2,3},{3,2},{4,5},{5,4},{6,7},{7,6},{8,9},{9,8},{10,11... | collective-permute-start | bytes 6152 | tf_op jit(solution)/shard_map/ppermute | solution.py:127
  26.3 4.5 %collective-permute-start.13 = (f32[1,1,256]{2,1,0:T(1,128)S(1)}, f32[1,1,256]{2,1,0:T(1,128)S(1)}, u32[]{:S(2)}, u32[]{:S(2)}) collective-permute-start(f32[1,1,256]{2,1,0:T(1,128)S(1)} %get-tuple-element.29), channel_id=1, source_target_pairs={{0,6},{1,7},{2,4},{3,5},{4,2},{5,3},{6,0},{7,1},{8,14},{9,15},{10,... | collective-permute-start | bytes 3080 | tf_op jit(solution)/shard_map/ppermute | solution.py:127
  30.9 4.6 %collective-permute-start.14 = (bf16[1552,128]{1,0:T(8,128)(2,1)S(1)}, bf16[1552,128]{1,0:T(8,128)(2,1)S(1)}, u32[]{:S(2)}, u32[]{:S(2)}) collective-permute-start(bf16[1552,128]{1,0:T(8,128)(2,1)S(1)} %collective-permute-done.11.refs_5_), channel_id=1, source_target_pairs={{0,1},{1,0},{2,3},{3,2},{4,5},{5,4},{6,7},{7,6},{8,9},{9,8},{10,11... | collective-permute-start | bytes 1191944 | tf_op jit(solution)/shard_map/ppermute | solution.py:127
  31.5 6.2 %collective-permute-start.12 = (f32[1,1,256]{2,1,0:T(1,128)S(1)}, f32[1,1,256]{2,1,0:T(1,128)S(1)}, u32[]{:S(2)}, u32[]{:S(2)}) collective-permute-start(f32[1,1,256]{2,1,0:T(1,128)S(1)} %compare_half_way.1), channel_id=1, source_target_pairs={{0,16},{8,24},{16,0},{24,8},{1,17},{9,25},{17,1},{25,9},{2,18},{10... | collective-permute-start | bytes 3080 | tf_op jit(solution)/shard_map/ppermute | solution.py:133
  33.9 3.8 %collective-permute-start.10 = (f32[1,1,256]{2,1,0:T(1,128)S(1)}, f32[1,1,256]{2,1,0:T(1,128)S(1)}, u32[]{:S(2)}, u32[]{:S(2)}) collective-permute-start(f32[1,1,256]{2,1,0:T(1,128)S(1)} %bitcast.20), channel_id=1, source_target_pairs={{0,24},{8,0},{16,8},{24,16},{1,25},{9,1},{17,9},{25,17},{2,26},{10... | collective-permute-start | bytes 3080 | tf_op jit(solution)/shard_map/ppermute | solution.py:133
  36.1 4.0 %collective-permute-start.15 = (f32[1,1,256]{2,1,0:T(1,128)S(1)}, f32[1,1,256]{2,1,0:T(1,128)S(1)}, u32[]{:S(2)}, u32[]{:S(2)}) collective-permute-start(f32[1,1,256]{2,1,0:T(1,128)S(1)} %compare_twin.1), channel_id=1, source_target_pairs={{0,17},{1,16},{2,19},{3,18},{4,21},{5,20},{6,23},{7,22},{8,25},{9,... | collective-permute-start | bytes 3080 | tf_op jit(solution)/shard_map/ppermute | solution.py:137

commit v6 on v4

--- a/solution.py
+++ b/solution.py
@@ -14,27 +14,49 @@
 VMEM_SMALL = 8 << 20
 
 
-def pack_kernel(per_group, emb_ref, target_ref, cluster_ref, out_ref):
-    rows, width = emb_ref.shape
-    x = emb_ref[...].astype(jnp.float32)
+def put_block(x, key, out_ref):
+    rows, width = x.shape
+    x = x.astype(jnp.float32)
     scale = lax.rsqrt(jnp.sum(x * x, axis=1, keepdims=True) + 1e-06)
     normed = (x * scale).astype(jnp.bfloat16)
     for at in range(width // LANES):
         out_ref[at * rows : (at + 1) * rows, :] = normed[:, at * LANES : (at + 1) * LANES]
-    key = (target_ref[...] // per_group * CLUSTERS + cluster_ref[...] + 1).astype(jnp.float32)
     tail = [key[:, at : at + LANES] for at in range(0, rows, LANES)]
     tail.append(jnp.zeros((TAIL - len(tail), LANES), jnp.float32))
     out_ref[out_ref.shape[0] - TAIL :, :] = jnp.concatenate(tail, axis=0).astype(jnp.bfloat16)
 
 
-def pack(embeddings, target, cluster, per_group):
-    rows, width = embeddings.shape
-    return pl.pallas_call(
-        functools.partial(pack_kernel, per_group),
-        out_shape=jax.ShapeDtypeStruct((rows * width // LANES + TAIL, LANES), jnp.bfloat16),
+def pack_own_kernel(per_group, emb_ref, target_ref, cluster_ref, out_ref, key_ref):
+    key = (target_ref[...] // per_group * CLUSTERS + cluster_ref[...] + 1).astype(jnp.float32)
+    key_ref[...] = key
+    put_block(emb_ref[...], key, out_ref)
+
+
+def pack_kernel(emb_ref, key_ref, out_ref):
+    put_block(emb_ref[...], key_ref[...], out_ref)
+
+
+def block_shape(embeddings):
+    return jax.ShapeDtypeStruct((embeddings.size // LANES + TAIL, LANES), jnp.bfloat16)
+
+
+def pack_own(embeddings, target, cluster, per_group):
+    rows = embeddings.shape[0]
+    return pl.pallas_call(
+        functools.partial(pack_own_kernel, per_group),
+        out_shape=[block_shape(embeddings), jax.ShapeDtypeStruct((1, rows), jnp.float32)],
+        compiler_params=pltpu.CompilerParams(vmem_limit_bytes=VMEM_SMALL),
+        name="pack_own",
+    )(embeddings, target.reshape(1, rows), cluster.reshape(1, rows))
+
+
+def pack(embeddings, keys):
+    return pl.pallas_call(
+        pack_kernel,
+        out_shape=block_shape(embeddings),
         compiler_params=pltpu.CompilerParams(vmem_limit_bytes=VMEM_SMALL),
         name="pack",
-    )(embeddings, target.reshape(1, rows), cluster.reshape(1, rows))
+    )(embeddings, keys)
 
 
 def unpack(pieces, rows):
@@ -159,12 +181,15 @@
     groups = lax.axis_size("grp")
     per_group = lax.axis_size("blk")
     rows = embeddings.shape[0]
-    packed = pack(embeddings, target, cluster, per_group)
-    one_off = grp_shift(packed, 1)
+    one_off_raw = grp_shift(embeddings, 1)
+    half_way_raw = grp_shift(one_off_raw, 1)
+    packed, keys = pack_own(embeddings, target, cluster, per_group)
     plane = fetch_plane(packed, rows, per_group)
-    own_then = lax.optimization_barrier((packed, one_off))[0]
+    one_off_keys, half_way_keys = lax.optimization_barrier((grp_shift(keys, 1), grp_shift(keys, 2)))
+    one_off = pack(one_off_raw, one_off_keys)
+    half_way = pack(half_way_raw, half_way_keys)
+    own_then = lax.optimization_barrier((packed, one_off_raw))[0]
     own_twin = plane_shift(own_then, 1)
-    half_way = grp_shift(one_off, 1)
     direct = [mask for mask, pieces in plane.items() if len(pieces) == 1]
     relayed = [mask for mask, pieces in plane.items() if len(pieces) > 1]
 

time: 39.4 us -> 38.2 us (0.970)
  waiting for transfers between devices: 17 us -> 11.9 us
  starting transfers between devices: 16.2 us -> 19.8 us
    ppermute x4 -> x6, starting transfers between devices: 4.13 us -> 8.11 us  [grp_shift(): lax.ppermute(x, 'grp', [(z, (z + shift) % groups) for z in range(groups)])]
    ppermute x4 -> x6, waiting for transfers between devices: 11.6 us -> 7.7 us  [grp_shift(): lax.ppermute(x, 'grp', [(z, (z + shift) % groups) for z in range(groups)])]
    ppermute x11, waiting for transfers between devices: 3.98 us -> 2.71 us  [plane_shift(): return lax.ppermute(x, 'blk', [(i, i ^ mask) for i in range(size)])]
  transfers between devices with their start and end apart: 16 -> 18, of which waited for: 8 -> 7; matrix products, arithmetic and copies ran while one was open for 0% -> 0% of each run, Pallas kernels for 9% -> 10%
where the time goes in v6:
time: 38.2 us; the launch traced here: 38.1 us
  starting transfers between devices  19.8 us (52%)
  waiting for transfers between devices  11.9 us (31%)
  Pallas kernels  4 us (10%)
  local copies, waits for them, and re-layouts  1.72 us (5%)
  other arithmetic  0.57 us (1%)
    ppermute x11, starting transfers between devices, plane_shift(): return lax.ppermute(x, 'blk', [(i, i ^ mask) for i in range(size)])  10.5 us
    ppermute x6, starting transfers between devices, grp_shift(): lax.ppermute(x, 'grp', [(z, (z + shift) % groups) for z in range(groups)])  8.11 us
    ppermute x6, waiting for transfers between devices, grp_shift(): lax.ppermute(x, 'grp', [(z, (z + shift) % groups) for z in range(groups)])  7.7 us
    pallas_call x4, Pallas kernels, score(): pl.pallas_call(kernel, out_shape=[jax.ShapeDtypeStruct((count, 1, rows),...  3.51 us
    ppermute x11, waiting for transfers between devices, plane_shift(): return lax.ppermute(x, 'blk', [(i, i ^ mask) for i in range(size)])  2.71 us
    unnamed x6, local copies, waits for them, and re-layouts  1.69 us
    ppermute x1, waiting for transfers between devices, grp_shift(): return lax.ppermute(x, ('grp', 'blk'), pairs)  1.44 us
    ppermute x1, starting transfers between devices, grp_shift(): return lax.ppermute(x, ('grp', 'blk'), pairs)  1.17 us
  transfers between devices with their start and end apart: 18, of which 7 were waited for; matrix products, arithmetic and copies ran while one was open for 0% of the time, Pallas kernels for 10%

profile of v6, /device:TPU:0, one launch (start us, length us, event | category | flops | bytes accessed | tf_op | source)
XLA Modules:
  0.0 38.1 jit_solution(8023535641630741800)
XLA Ops:
  0.0 3.0 %collective-permute-start.4 = (bf16[256,768]{1,0:T(8,128)(2,1)}, bf16[256,768]{1,0:T(8,128)(2,1)S(1)}, u32[]{:S(2)}, u32[]{:S(2)}) collective-permute-start(bf16[256,768]{1,0:T(8,128)(2,1)} %emb_ref.1), channel_id=1, source_target_pairs={{0,8},{8,16},{16,24},{24,0},{1,9},{9,17},{17,25},{25,1},{2,10},{10... | collective-permute-start | bytes 1179656 | tf_op jit(solution)/shard_map/ppermute | solution.py:155
  3.0 0.7 %copy-done.2 = s32[256]{0:T(256)S(1)} copy-done((s32[256]{0:T(256)S(1)}, s32[256]{0:T(256)}, u32[]{:S(2)}) %copy-start.2) | copy-done | bytes 1048
  3.7 1.0 %copy-done = bf16[256,768]{1,0:T(8,128)(2,1)S(1)} copy-done((bf16[256,768]{1,0:T(8,128)(2,1)S(1)}, bf16[256,768]{1,0:T(8,128)(2,1)}, u32[]{:S(2)}) %copy-start) | copy-done | bytes 393240
  4.7 0.2 pack_own.1
  4.9 1.6 %collective-permute-start.2 = (bf16[1552,128]{1,0:T(8,128)(2,1)S(1)}, bf16[1552,128]{1,0:T(8,128)(2,1)S(1)}, u32[]{:S(2)}, u32[]{:S(2)}) collective-permute-start(bf16[1552,128]{1,0:T(8,128)(2,1)S(1)} %get-tuple-element.24.refs_0_.refs_3_.refs_2_), channel_id=1, source_target_pairs={{0,2},{1,3},{2,0},{3,1},{4,6},{5,7},{6,4},{7,5},{8,10},{9,11},{10,... | collective-permute-start | bytes 1191944 | tf_op jit(solution)/shard_map/ppermute | solution.py:149
  6.4 1.5 %collective-permute-start = (bf16[1552,128]{1,0:T(8,128)(2,1)S(1)}, bf16[1552,128]{1,0:T(8,128)(2,1)S(1)}, u32[]{:S(2)}, u32[]{:S(2)}) collective-permute-start(bf16[1552,128]{1,0:T(8,128)(2,1)S(1)} %get-tuple-element.24.refs_0_.refs_3_.refs_2_), channel_id=1, source_target_pairs={{0,4},{1,5},{2,6},{3,7},{4,0},{5,1},{6,2},{7,3},{8,12},{9,13},{10,... | collective-permute-start | bytes 1191944 | tf_op jit(solution)/shard_map/ppermute | solution.py:149
  8.0 1.6 %collective-permute-start.6 = (f32[1,256]{1,0:T(1,128)S(1)}, f32[1,256]{1,0:T(1,128)S(1)}, u32[]{:S(2)}, u32[]{:S(2)}) collective-permute-start(f32[1,256]{1,0:T(1,128)S(1)} %get-tuple-element.25), channel_id=1, source_target_pairs={{0,8},{8,16},{16,24},{24,0},{1,9},{9,17},{17,25},{25,1},{2,10},{10... | collective-permute-start | bytes 3080 | tf_op jit(solution)/shard_map/ppermute | solution.py:155
  9.5 1.2 %collective-permute-start.7 = (f32[1,256]{1,0:T(1,128)S(1)}, f32[1,256]{1,0:T(1,128)S(1)}, u32[]{:S(2)}, u32[]{:S(2)}) collective-permute-start(f32[1,256]{1,0:T(1,128)S(1)} %get-tuple-element.25), channel_id=1, source_target_pairs={{0,16},{8,24},{16,0},{24,8},{1,17},{9,25},{17,1},{25,9},{2,18},{10... | collective-permute-start | bytes 3080 | tf_op jit(solution)/shard_map/ppermute | solution.py:155
  10.8 3.7 %collective-permute-done.6.key_ref = f32[1,256]{1,0:T(1,128)S(1)} collective-permute-done((f32[1,256]{1,0:T(1,128)S(1)}, f32[1,256]{1,0:T(1,128)S(1)}, u32[]{:S(2)}, u32[]{:S(2)}) %collective-permute-start.6) | collective-permute-done | bytes 1056 | tf_op jit(solution)/shard_map/ppermute | solution.py:155
  14.5 0.2 pack.2.refs_5_.refs_4_
  14.6 0.6 %collective-permute-start.8 = (bf16[1552,128]{1,0:T(8,128)(2,1)S(1)}, bf16[1552,128]{1,0:T(8,128)(2,1)S(1)}, u32[]{:S(2)}, u32[]{:S(2)}) collective-permute-start(bf16[1552,128]{1,0:T(8,128)(2,1)S(1)} %pack.2.refs_5_.refs_4_), channel_id=1, source_target_pairs={{0,1},{1,0},{2,3},{3,2},{4,5},{5,4},{6,7},{7,6},{8,9},{9,8},{10,11... | collective-permute-start | bytes 1191944 | tf_op jit(solution)/shard_map/ppermute | solution.py:149
  15.2 1.1 %collective-permute-start.13 = (bf16[256,768]{1,0:T(8,128)(2,1)S(1)}, bf16[256,768]{1,0:T(8,128)(2,1)S(1)}, u32[]{:S(2)}, u32[]{:S(2)}) collective-permute-start(bf16[256,768]{1,0:T(8,128)(2,1)S(1)} %collective-permute-done.4.emb_ref), channel_id=1, source_target_pairs={{0,8},{8,16},{16,24},{24,0},{1,9},{9,17},{17,25},{25,1},{2,10},{10... | collective-permute-start | bytes 1179656 | tf_op jit(solution)/shard_map/ppermute | solution.py:155
  16.3 1.0 %collective-permute-start.3 = (bf16[784,128]{1,0:T(8,128)(2,1)S(1)}, bf16[784,128]{1,0:T(8,128)(2,1)S(1)}, u32[]{:S(2)}, u32[]{:S(2)}) collective-permute-start(bf16[784,128]{1,0:T(8,128)(2,1)S(1)} %slice.9), channel_id=1, source_target_pairs={{0,4},{1,5},{2,6},{3,7},{4,0},{5,1},{6,2},{7,3},{8,12},{9,13},{10,... | collective-permute-start | bytes 602120 | tf_op jit(solution)/shard_map/ppermute | solution.py:149
  17.4 1.6 %collective-permute-start.1 = (bf16[768,128]{1,0:T(8,128)(2,1)S(1)}, bf16[768,128]{1,0:T(8,128)(2,1)S(1)}, u32[]{:S(2)}, u32[]{:S(2)}) collective-permute-start(bf16[768,128]{1,0:T(8,128)(2,1)S(1)} %slice.8), channel_id=1, source_target_pairs={{0,2},{1,3},{2,0},{3,1},{4,6},{5,7},{6,4},{7,5},{8,10},{9,11},{10,... | collective-permute-start | bytes 589832 | tf_op jit(solution)/shard_map/ppermute | solution.py:149
  18.9 1.6 %compare_direct.1 = (f32[4,1,256]{2,1,0:T(1,128)S(1)}, f32[1,1,256]{2,1,0:T(1,128)S(1)}, f32[1,1,256]{2,1,0:T(1,128)S(1)}, f32[1,1,256]{2,1,0:T(1,128)S(1)}) custom-call(bf16[1552,128]{1,0:T(8,128)(2,1)S(1)} %get-tuple-element.24.refs_0_.refs_3_.refs_2_, bf16[1552,128]{1,0:T(8,128)(2,1)S(1)} %collective-permute-done.2.refs_1_, ...), custom_call_target="tpu_custom_call" | custom-call | flops 1220542464 | bytes 2781184 | tf_op jit(solution)/shard_map/compare_direct/pallas_call | solution.py:120
  20.5 0.6 %collective-permute-start.9 = (f32[1,1,256]{2,1,0:T(1,128)S(1)}, f32[1,1,256]{2,1,0:T(1,128)S(1)}, u32[]{:S(2)}, u32[]{:S(2)}) collective-permute-start(f32[1,1,256]{2,1,0:T(1,128)S(1)} %get-tuple-element.28), channel_id=1, source_target_pairs={{0,2},{1,3},{2,0},{3,1},{4,6},{5,7},{6,4},{7,5},{8,10},{9,11},{10,... | collective-permute-start | bytes 3080 | tf_op jit(solution)/shard_map/ppermute | solution.py:149
  21.1 1.1 %collective-permute-start.10 = (f32[1,1,256]{2,1,0:T(1,128)S(1)}, f32[1,1,256]{2,1,0:T(1,128)S(1)}, u32[]{:S(2)}, u32[]{:S(2)}) collective-permute-start(f32[1,1,256]{2,1,0:T(1,128)S(1)} %get-tuple-element.29), channel_id=1, source_target_pairs={{0,4},{1,5},{2,6},{3,7},{4,0},{5,1},{6,2},{7,3},{8,12},{9,13},{10,... | collective-permute-start | bytes 3080 | tf_op jit(solution)/shard_map/ppermute | solution.py:149
  22.2 1.9 %collective-permute-done.9 = f32[1,1,256]{2,1,0:T(1,128)S(1)} collective-permute-done((f32[1,1,256]{2,1,0:T(1,128)S(1)}, f32[1,1,256]{2,1,0:T(1,128)S(1)}, u32[]{:S(2)}, u32[]{:S(2)}) %collective-permute-start.9) | collective-permute-done | bytes 1056 | tf_op jit(solution)/shard_map/ppermute | solution.py:149
  24.1 0.5 %collective-permute-done.10 = f32[1,1,256]{2,1,0:T(1,128)S(1)} collective-permute-done((f32[1,1,256]{2,1,0:T(1,128)S(1)}, f32[1,1,256]{2,1,0:T(1,128)S(1)}, u32[]{:S(2)}, u32[]{:S(2)}) %collective-permute-start.10) | collective-permute-done | bytes 1056 | tf_op jit(solution)/shard_map/ppermute | solution.py:149
  24.7 0.7 %compare_relayed.1 = (f32[1,1,256]{2,1,0:T(1,128)S(1)}, f32[1,1,256]{2,1,0:T(1,128)S(1)}, f32[2,1,256]{2,1,0:T(1,128)S(1)}, f32[1,1,256]{2,1,0:T(1,128)S(1)}) custom-call(bf16[768,128]{1,0:T(8,128)(2,1)S(1)} %collective-permute-done.1.refs_0_.refs_3_, bf16[784,128]{1,0:T(8,128)(2,1)S(1)} %collective-permute-done.3.refs_1_.refs_4_, ...), custom_call_target="tpu_custom_call" | custom-call | flops 406847488 | bytes 1986560 | tf_op jit(solution)/shard_map/compare_relayed/pallas_call | solution.py:120
  25.4 0.1 collective-permute-start.11
  25.4 2.7 %collective-permute-done.13.emb_ref = bf16[256,768]{1,0:T(8,128)(2,1)S(1)} collective-permute-done((bf16[256,768]{1,0:T(8,128)(2,1)S(1)}, bf16[256,768]{1,0:T(8,128)(2,1)S(1)}, u32[]{:S(2)}, u32[]{:S(2)}) %collective-permute-start.13) | collective-permute-done | bytes 393248 | tf_op jit(solution)/shard_map/ppermute | solution.py:155
  28.1 0.2 pack.3.refs_5_
  28.4 2.5 %collective-permute-start.16 = (f32[1,1,256]{2,1,0:T(1,128)S(1)}, f32[1,1,256]{2,1,0:T(1,128)S(1)}, u32[]{:S(2)}, u32[]{:S(2)}) collective-permute-start(f32[1,1,256]{2,1,0:T(1,128)S(1)} %get-tuple-element.39), channel_id=1, source_target_pairs={{0,6},{1,7},{2,4},{3,5},{4,2},{5,3},{6,0},{7,1},{8,14},{9,15},{10,... | collective-permute-start | bytes 3080 | tf_op jit(solution)/shard_map/ppermute | solution.py:149
  30.9 0.6 %compare_half_way.1 = f32[1,1,256]{2,1,0:T(1,128)S(1)} custom-call(bf16[1552,128]{1,0:T(8,128)(2,1)S(1)} %get-tuple-element.24.refs_0_.refs_3_.refs_2_, bf16[1552,128]{1,0:T(8,128)(2,1)S(1)} %collective-permute-done.2.refs_1_, bf16[1552,128]{1,0:T(8,128)(2,1)S(1)} %collective-permute-done.refs_2_, ...), custom_call_target="tpu_custom_call" | custom-call | flops 406847488 | bytes 1986560 | tf_op jit(solution)/shard_map/compare_half_way/pallas_call | solution.py:120
  31.6 1.1 %collective-permute-start.12 = (f32[1,1,256]{2,1,0:T(1,128)S(1)}, f32[1,1,256]{2,1,0:T(1,128)S(1)}, u32[]{:S(2)}, u32[]{:S(2)}) collective-permute-start(f32[1,1,256]{2,1,0:T(1,128)S(1)} %bitcast.20), channel_id=1, source_target_pairs={{0,24},{8,0},{16,8},{24,16},{1,25},{9,1},{17,9},{25,17},{2,26},{10... | collective-permute-start | bytes 3080 | tf_op jit(solution)/shard_map/ppermute | solution.py:155
  32.7 0.2 collective-permute-done.16
  32.9 0.6 %compare_twin.1 = f32[1,1,256]{2,1,0:T(1,128)S(1)} custom-call(bf16[1552,128]{1,0:T(8,128)(2,1)S(1)} %get-tuple-element.24.refs_0_.refs_3_.refs_2_, bf16[1552,128]{1,0:T(8,128)(2,1)S(1)} %collective-permute-done.2.refs_1_, bf16[1552,128]{1,0:T(8,128)(2,1)S(1)} %collective-permute-done.refs_2_, bf16[768,128]{1,0:T(8,128)(2,1)S(1)} %collective-permute-done.1.refs_0_.refs_3_, ...), custom_call_target="tpu_custom_call" | custom-call | flops 406847488 | bytes 1986560 | tf_op jit(solution)/shard_map/compare_twin/pallas_call | solution.py:120
  33.5 1.2 %collective-permute-start.17 = (f32[1,1,256]{2,1,0:T(1,128)S(1)}, f32[1,1,256]{2,1,0:T(1,128)S(1)}, u32[]{:S(2)}, u32[]{:S(2)}) collective-permute-start(f32[1,1,256]{2,1,0:T(1,128)S(1)} %compare_twin.1), channel_id=1, source_target_pairs={{0,17},{1,16},{2,19},{3,18},{4,21},{5,20},{6,23},{7,22},{8,25},{9,... | collective-permute-start | bytes 3080 | tf_op jit(solution)/shard_map/ppermute | solution.py:159
  34.7 1.3 %collective-permute-done.14 = f32[1,1,256]{2,1,0:T(1,128)S(1)} collective-permute-done((f32[1,1,256]{2,1,0:T(1,128)S(1)}, f32[1,1,256]{2,1,0:T(1,128)S(1)}, u32[]{:S(2)}, u32[]{:S(2)}) %collective-permute-start.14) | collective-permute-done | bytes 1056 | tf_op jit(solution)/shard_map/ppermute | solution.py:155
  36.1 1.4 %collective-permute-done.17 = f32[1,1,256]{2,1,0:T(1,128)S(1)} collective-permute-done((f32[1,1,256]{2,1,0:T(1,128)S(1)}, f32[1,1,256]{2,1,0:T(1,128)S(1)}, u32[]{:S(2)}, u32[]{:S(2)}) %collective-permute-start.17) | collective-permute-done | bytes 1056 | tf_op jit(solution)/shard_map/ppermute | solution.py:159
  37.5 0.6 %maximum_maximum_fusion = f32[1,1,256]{2,1,0:T(1,128)} fusion(f32[1,1,256]{2,1,0:T(1,128)S(1)} %collective-permute-done.16, f32[1,1,256]{2,1,0:T(1,128)S(1)} %collective-permute-done.10, f32[1,1,256]{2,1,0:T(1,128)S(1)} %collective-permute-done.9, f32[1,1,256]{2,1,0:T(1,128)S(1)} %collective-permute-done.17, f32[1,1,256]{2,1,0:T(1,128)S(1)} %collective-permute-done.14, ...), kind=kLoop, calls=%fused_computation.4 | loop fusion | flops 1792 | bytes 9216 | tf_op jit(solution)/shard_map/max | solution.py:232
  (21 shorter events, 0.2 us)
Async XLA Ops:
  0.0 14.5 %collective-permute-start.4 = (bf16[256,768]{1,0:T(8,128)(2,1)}, bf16[256,768]{1,0:T(8,128)(2,1)S(1)}, u32[]{:S(2)}, u32[]{:S(2)}) collective-permute-start(bf16[256,768]{1,0:T(8,128)(2,1)} %emb_ref.1), channel_id=1, source_target_pairs={{0,8},{8,16},{16,24},{24,0},{1,9},{9,17},{17,25},{25,1},{2,10},{10... | collective-permute-start | bytes 1179656 | tf_op jit(solution)/shard_map/ppermute | solution.py:155
  3.0 0.7 %copy-start.2 = (s32[256]{0:T(256)S(1)}, s32[256]{0:T(256)}, u32[]{:S(2)}) copy-start(s32[256]{0:T(256)} %param.5) | copy-start | bytes 3076
  3.0 0.7 %copy-start.1 = (s32[256,1]{0,1:T(1,128)S(1)}, s32[256,1]{0,1:T(1,128)}, u32[]{:S(2)}) copy-start(s32[256,1]{0,1:T(1,128)} %param.4) | copy-start | bytes 3076
  3.7 1.0 %copy-start = (bf16[256,768]{1,0:T(8,128)(2,1)S(1)}, bf16[256,768]{1,0:T(8,128)(2,1)}, u32[]{:S(2)}) copy-start(bf16[256,768]{1,0:T(8,128)(2,1)} %emb_ref.1) | copy-start | bytes 1179652
  4.9 11.4 %collective-permute-start.2 = (bf16[1552,128]{1,0:T(8,128)(2,1)S(1)}, bf16[1552,128]{1,0:T(8,128)(2,1)S(1)}, u32[]{:S(2)}, u32[]{:S(2)}) collective-permute-start(bf16[1552,128]{1,0:T(8,128)(2,1)S(1)} %get-tuple-element.24.refs_0_.refs_3_.refs_2_), channel_id=1, source_target_pairs={{0,2},{1,3},{2,0},{3,1},{4,6},{5,7},{6,4},{7,5},{8,10},{9,11},{10,... | collective-permute-start | bytes 1191944 | tf_op jit(solution)/shard_map/ppermute | solution.py:149
  6.4 10.9 %collective-permute-start = (bf16[1552,128]{1,0:T(8,128)(2,1)S(1)}, bf16[1552,128]{1,0:T(8,128)(2,1)S(1)}, u32[]{:S(2)}, u32[]{:S(2)}) collective-permute-start(bf16[1552,128]{1,0:T(8,128)(2,1)S(1)} %get-tuple-element.24.refs_0_.refs_3_.refs_2_), channel_id=1, source_target_pairs={{0,4},{1,5},{2,6},{3,7},{4,0},{5,1},{6,2},{7,3},{8,12},{9,13},{10,... | collective-permute-start | bytes 1191944 | tf_op jit(solution)/shard_map/ppermute | solution.py:149
  8.0 6.5 %collective-permute-start.6 = (f32[1,256]{1,0:T(1,128)S(1)}, f32[1,256]{1,0:T(1,128)S(1)}, u32[]{:S(2)}, u32[]{:S(2)}) collective-permute-start(f32[1,256]{1,0:T(1,128)S(1)} %get-tuple-element.25), channel_id=1, source_target_pairs={{0,8},{8,16},{16,24},{24,0},{1,9},{9,17},{17,25},{25,1},{2,10},{10... | collective-permute-start | bytes 3080 | tf_op jit(solution)/shard_map/ppermute | solution.py:155
  9.5 4.9 %collective-permute-start.7 = (f32[1,256]{1,0:T(1,128)S(1)}, f32[1,256]{1,0:T(1,128)S(1)}, u32[]{:S(2)}, u32[]{:S(2)}) collective-permute-start(f32[1,256]{1,0:T(1,128)S(1)} %get-tuple-element.25), channel_id=1, source_target_pairs={{0,16},{8,24},{16,0},{24,8},{1,17},{9,25},{17,1},{25,9},{2,18},{10... | collective-permute-start | bytes 3080 | tf_op jit(solution)/shard_map/ppermute | solution.py:155
  14.5 4.5 %collective-permute-start.5 = (bf16[1552,128]{1,0:T(8,128)(2,1)S(1)}, bf16[1552,128]{1,0:T(8,128)(2,1)S(1)}, u32[]{:S(2)}, u32[]{:S(2)}) collective-permute-start(bf16[1552,128]{1,0:T(8,128)(2,1)S(1)} %get-tuple-element.24.refs_0_.refs_3_.refs_2_), channel_id=1, source_target_pairs={{0,1},{1,0},{2,3},{3,2},{4,5},{5,4},{6,7},{7,6},{8,9},{9,8},{10,11... | collective-permute-start | bytes 1191944 | tf_op jit(solution)/shard_map/ppermute | solution.py:149
  14.6 4.3 %collective-permute-start.8 = (bf16[1552,128]{1,0:T(8,128)(2,1)S(1)}, bf16[1552,128]{1,0:T(8,128)(2,1)S(1)}, u32[]{:S(2)}, u32[]{:S(2)}) collective-permute-start(bf16[1552,128]{1,0:T(8,128)(2,1)S(1)} %pack.2.refs_5_.refs_4_), channel_id=1, source_target_pairs={{0,1},{1,0},{2,3},{3,2},{4,5},{5,4},{6,7},{7,6},{8,9},{9,8},{10,11... | collective-permute-start | bytes 1191944 | tf_op jit(solution)/shard_map/ppermute | solution.py:149
  15.2 12.9 %collective-permute-start.13 = (bf16[256,768]{1,0:T(8,128)(2,1)S(1)}, bf16[256,768]{1,0:T(8,128)(2,1)S(1)}, u32[]{:S(2)}, u32[]{:S(2)}) collective-permute-start(bf16[256,768]{1,0:T(8,128)(2,1)S(1)} %collective-permute-done.4.emb_ref), channel_id=1, source_target_pairs={{0,8},{8,16},{16,24},{24,0},{1,9},{9,17},{17,25},{25,1},{2,10},{10... | collective-permute-start | bytes 1179656 | tf_op jit(solution)/shard_map/ppermute | solution.py:155
  16.3 8.3 %collective-permute-start.3 = (bf16[784,128]{1,0:T(8,128)(2,1)S(1)}, bf16[784,128]{1,0:T(8,128)(2,1)S(1)}, u32[]{:S(2)}, u32[]{:S(2)}) collective-permute-start(bf16[784,128]{1,0:T(8,128)(2,1)S(1)} %slice.9), channel_id=1, source_target_pairs={{0,4},{1,5},{2,6},{3,7},{4,0},{5,1},{6,2},{7,3},{8,12},{9,13},{10,... | collective-permute-start | bytes 602120 | tf_op jit(solution)/shard_map/ppermute | solution.py:149
  17.4 7.3 %collective-permute-start.1 = (bf16[768,128]{1,0:T(8,128)(2,1)S(1)}, bf16[768,128]{1,0:T(8,128)(2,1)S(1)}, u32[]{:S(2)}, u32[]{:S(2)}) collective-permute-start(bf16[768,128]{1,0:T(8,128)(2,1)S(1)} %slice.8), channel_id=1, source_target_pairs={{0,2},{1,3},{2,0},{3,1},{4,6},{5,7},{6,4},{7,5},{8,10},{9,11},{10,... | collective-permute-start | bytes 589832 | tf_op jit(solution)/shard_map/ppermute | solution.py:149
  20.5 3.6 %collective-permute-start.9 = (f32[1,1,256]{2,1,0:T(1,128)S(1)}, f32[1,1,256]{2,1,0:T(1,128)S(1)}, u32[]{:S(2)}, u32[]{:S(2)}) collective-permute-start(f32[1,1,256]{2,1,0:T(1,128)S(1)} %get-tuple-element.28), channel_id=1, source_target_pairs={{0,2},{1,3},{2,0},{3,1},{4,6},{5,7},{6,4},{7,5},{8,10},{9,11},{10,... | collective-permute-start | bytes 3080 | tf_op jit(solution)/shard_map/ppermute | solution.py:149
  21.1 3.6 %collective-permute-start.10 = (f32[1,1,256]{2,1,0:T(1,128)S(1)}, f32[1,1,256]{2,1,0:T(1,128)S(1)}, u32[]{:S(2)}, u32[]{:S(2)}) collective-permute-start(f32[1,1,256]{2,1,0:T(1,128)S(1)} %get-tuple-element.29), channel_id=1, source_target_pairs={{0,4},{1,5},{2,6},{3,7},{4,0},{5,1},{6,2},{7,3},{8,12},{9,13},{10,... | collective-permute-start | bytes 3080 | tf_op jit(solution)/shard_map/ppermute | solution.py:149
  25.4 2.9 %collective-permute-start.11 = (f32[2,1,256]{2,1,0:T(1,128)S(1)}, f32[2,1,256]{2,1,0:T(1,128)S(1)}, u32[]{:S(2)}, u32[]{:S(2)}) collective-permute-start(f32[2,1,256]{2,1,0:T(1,128)S(1)} %get-tuple-element.33), channel_id=1, source_target_pairs={{0,1},{1,0},{2,3},{3,2},{4,5},{5,4},{6,7},{7,6},{8,9},{9,8},{10,11... | collective-permute-start | bytes 6152 | tf_op jit(solution)/shard_map/ppermute | solution.py:149
  28.3 4.6 %collective-permute-start.15 = (bf16[1552,128]{1,0:T(8,128)(2,1)S(1)}, bf16[1552,128]{1,0:T(8,128)(2,1)S(1)}, u32[]{:S(2)}, u32[]{:S(2)}) collective-permute-start(bf16[1552,128]{1,0:T(8,128)(2,1)S(1)} %pack.3.refs_5_), channel_id=1, source_target_pairs={{0,1},{1,0},{2,3},{3,2},{4,5},{5,4},{6,7},{7,6},{8,9},{9,8},{10,11... | collective-permute-start | bytes 1191944 | tf_op jit(solution)/shard_map/ppermute | solution.py:149
  28.4 4.5 %collective-permute-start.16 = (f32[1,1,256]{2,1,0:T(1,128)S(1)}, f32[1,1,256]{2,1,0:T(1,128)S(1)}, u32[]{:S(2)}, u32[]{:S(2)}) collective-permute-start(f32[1,1,256]{2,1,0:T(1,128)S(1)} %get-tuple-element.39), channel_id=1, source_target_pairs={{0,6},{1,7},{2,4},{3,5},{4,2},{5,3},{6,0},{7,1},{8,14},{9,15},{10,... | collective-permute-start | bytes 3080 | tf_op jit(solution)/shard_map/ppermute | solution.py:149
  31.5 4.5 %collective-permute-start.14 = (f32[1,1,256]{2,1,0:T(1,128)S(1)}, f32[1,1,256]{2,1,0:T(1,128)S(1)}, u32[]{:S(2)}, u32[]{:S(2)}) collective-permute-start(f32[1,1,256]{2,1,0:T(1,128)S(1)} %compare_half_way.1), channel_id=1, source_target_pairs={{0,16},{8,24},{16,0},{24,8},{1,17},{9,25},{17,1},{25,9},{2,18},{10... | collective-permute-start | bytes 3080 | tf_op jit(solution)/shard_map/ppermute | solution.py:155
  31.6 4.5 %collective-permute-start.12 = (f32[1,1,256]{2,1,0:T(1,128)S(1)}, f32[1,1,256]{2,1,0:T(1,128)S(1)}, u32[]{:S(2)}, u32[]{:S(2)}) collective-permute-start(f32[1,1,256]{2,1,0:T(1,128)S(1)} %bitcast.20), channel_id=1, source_target_pairs={{0,24},{8,0},{16,8},{24,16},{1,25},{9,1},{17,9},{25,17},{2,26},{10... | collective-permute-start | bytes 3080 | tf_op jit(solution)/shard_map/ppermute | solution.py:155
  33.5 4.0 %collective-permute-start.17 = (f32[1,1,256]{2,1,0:T(1,128)S(1)}, f32[1,1,256]{2,1,0:T(1,128)S(1)}, u32[]{:S(2)}, u32[]{:S(2)}) collective-permute-start(f32[1,1,256]{2,1,0:T(1,128)S(1)} %compare_twin.1), channel_id=1, source_target_pairs={{0,17},{1,16},{2,19},{3,18},{4,21},{5,20},{6,23},{7,22},{8,25},{9,... | collective-permute-start | bytes 3080 | tf_op jit(solution)/shard_map/ppermute | solution.py:159

commit v7 on v6

--- a/solution.py
+++ b/solution.py
@@ -68,12 +68,13 @@
 
 def score_kernel(counts, n_cols, pairs, want_rows, known, outs, *refs):
     n_rows = len(counts) if want_rows else 0
-    *plane, cols, cols_in, col_outs, row_outs = take(refs, counts + (n_cols, bool(known), len(outs), n_rows))
+    *blocks, cols_in, col_outs, row_outs = take(refs, counts + n_cols + (bool(known), len(outs), n_rows))
+    plane, cols = blocks[: len(counts)], blocks[len(counts) :]
     rows = col_outs[0].shape[2]
-    best = [jnp.full((1, rows), -1.0, jnp.float32)] * n_cols
+    best = [jnp.full((1, rows), -1.0, jnp.float32)] * len(n_cols)
     for at, col in enumerate(known):
         best[col] = cols_in[0][at]
-    cols = [unpack([ref], rows) for ref in cols]
+    cols = [unpack(pieces, rows) for pieces in cols]
     for k, pieces in enumerate(plane):
         block, keys = unpack(pieces, rows)
         row_keys = jnp.transpose(jnp.broadcast_to(keys, (LANES, rows)))
@@ -111,10 +112,11 @@
 
 
 def score(name, rows, plane, cols, pairs, want_rows, outs, known=(), cols_in=()):
-    size = cols[0].size
+    size = sum(piece.size for piece in cols[0])
     counts = tuple(len(pieces) for pieces in plane)
+    n_cols = tuple(len(pieces) for pieces in cols)
     kernel = functools.partial(
-        score_kernel, counts, len(cols), tuple(pairs), tuple(want_rows), tuple(known), tuple(outs)
+        score_kernel, counts, n_cols, tuple(pairs), tuple(want_rows), tuple(known), tuple(outs)
     )
     shapes = [len(held) for held in outs] + [1] * (len(plane) if want_rows else 0)
     return pl.pallas_call(
@@ -127,7 +129,7 @@
             transcendentals=0,
         ),
         name=name,
-    )(*[piece for pieces in plane for piece in pieces], *cols, *cols_in)
+    )(*[piece for pieces in (*plane, *cols) for piece in pieces], *cols_in)
 
 
 def join_kernel(n, *refs):
@@ -159,8 +161,12 @@
     return lax.ppermute(x, ("grp", "blk"), pairs)
 
 
+def cut(block, rows):
+    half = block.shape[0] // rows // 2 * rows
+    return block[:half], block[half:]
+
+
 def fetch_plane(packed, rows, per_group):
-    half = packed.shape[0] // rows // 2 * rows
     plane = {0: (packed,)}
     halves = {}
     for mask in sorted(range(2, per_group, 2), key=lambda mask: mask.bit_count()):
@@ -168,7 +174,7 @@
         if low == high:
             block = plane_shift(packed, mask)
             plane[mask] = (block,)
-            halves[mask] = (block[:half], block[half:])
+            halves[mask] = cut(block, rows)
         else:
             plane[mask] = halves[mask] = (
                 plane_shift(halves[mask ^ low][0], low),
@@ -188,12 +194,12 @@
     one_off_keys, half_way_keys = lax.optimization_barrier((grp_shift(keys, 1), grp_shift(keys, 2)))
     one_off = pack(one_off_raw, one_off_keys)
     half_way = pack(half_way_raw, half_way_keys)
-    own_then = lax.optimization_barrier((packed, one_off_raw))[0]
+    own_then = lax.optimization_barrier((packed, one_off_keys))[0]
     own_twin = plane_shift(own_then, 1)
     direct = [mask for mask, pieces in plane.items() if len(pieces) == 1]
     relayed = [mask for mask, pieces in plane.items() if len(pieces) > 1]
 
-    cols = [packed, own_twin, one_off, plane_shift(one_off, 1)]
+    cols = [(packed,), (own_twin,), (one_off,), [plane_shift(piece, 1) for piece in cut(one_off, rows)]]
     every = range(len(cols))
     best, *rows_direct = score(
         "compare_direct",
@@ -227,7 +233,7 @@
     half_then = lax.optimization_barrier((half_way, own))[0]
     half_twin = lax.optimization_barrier((plane_shift(half_then, 1), early))[0]
     for name, block, mask in (("compare_half_way", half_way, 0), ("compare_twin", half_twin, 1)):
-        (half_best,) = score(name, rows, blocks, [block], pairs, (), [(0,)])
+        (half_best,) = score(name, rows, blocks, [(block,)], pairs, (), [(0,)])
         found.append(grp_shift(half_best, groups // 2, mask))
     return functools.reduce(jnp.maximum, found + early).reshape(-1)
 

time: 38.2 us -> 38 us (level)
  waiting for transfers between devices: 11.9 us -> 10.4 us
  starting transfers between devices: 19.8 us -> 21 us
    ppermute x6, waiting for transfers between devices: 7.7 us -> 5.66 us  [grp_shift(): lax.ppermute(x, 'grp', [(z, (z + shift) % groups) for z in range(groups)])]
    ppermute x11 -> x12, waiting for transfers between devices: 2.71 us -> 4.58 us  [plane_shift(): return lax.ppermute(x, 'blk', [(i, i ^ mask) for i in range(size)])]
    ppermute x1, waiting for transfers between devices: 1.44 us -> 0.16 us  [grp_shift(): return lax.ppermute(x, ('grp', 'blk'), pairs)]
    ppermute x1, starting transfers between devices: 1.17 us -> 2.07 us  [grp_shift(): return lax.ppermute(x, ('grp', 'blk'), pairs)]
    ppermute x11 -> x12, starting transfers between devices: 10.5 us -> 10.6 us  [plane_shift(): return lax.ppermute(x, 'blk', [(i, i ^ mask) for i in range(size)])]
  transfers between devices with their start and end apart: 18 -> 19, of which waited for: 7 -> 8; matrix products, arithmetic and copies ran while one was open for 0% -> 0% of each run, Pallas kernels for 10% -> 10%
where the time goes in v7:
time: 38 us; the launch traced here: 37.8 us
  starting transfers between devices  21 us (55%)
  waiting for transfers between devices  10.4 us (27%)
  Pallas kernels  3.98 us (10%)
  local copies, waits for them, and re-layouts  1.75 us (5%)
  other arithmetic  0.57 us (1%)
    ppermute x12, starting transfers between devices, plane_shift(): return lax.ppermute(x, 'blk', [(i, i ^ mask) for i in range(size)])  10.6 us
    ppermute x6, starting transfers between devices, grp_shift(): lax.ppermute(x, 'grp', [(z, (z + shift) % groups) for z in range(groups)])  8.35 us
    ppermute x6, waiting for transfers between devices, grp_shift(): lax.ppermute(x, 'grp', [(z, (z + shift) % groups) for z in range(groups)])  5.66 us
    ppermute x12, waiting for transfers between devices, plane_shift(): return lax.ppermute(x, 'blk', [(i, i ^ mask) for i in range(size)])  4.58 us
    pallas_call x4, Pallas kernels, score(): pl.pallas_call(kernel, out_shape=[jax.ShapeDtypeStruct((count, 1, rows),...  3.5 us
    ppermute x1, starting transfers between devices, grp_shift(): return lax.ppermute(x, ('grp', 'blk'), pairs)  2.07 us
    unnamed x6, local copies, waits for them, and re-layouts  1.69 us
  transfers between devices with their start and end apart: 19, of which 8 were waited for; matrix products, arithmetic and copies ran while one was open for 0% of the time, Pallas kernels for 10%

profile of v7, /device:TPU:0, one launch (start us, length us, event | category | flops | bytes accessed | tf_op | source)
XLA Modules:
  0.0 37.8 jit_solution(11311869696798279824)
XLA Ops:
  0.0 3.0 %collective-permute-start.7 = (bf16[256,768]{1,0:T(8,128)(2,1)}, bf16[256,768]{1,0:T(8,128)(2,1)S(1)}, u32[]{:S(2)}, u32[]{:S(2)}) collective-permute-start(bf16[256,768]{1,0:T(8,128)(2,1)} %emb_ref.1), channel_id=1, source_target_pairs={{0,8},{8,16},{16,24},{24,0},{1,9},{9,17},{17,25},{25,1},{2,10},{10... | collective-permute-start | bytes 1179656 | tf_op jit(solution)/shard_map/ppermute | solution.py:157
  3.0 0.7 %copy-done.2 = s32[256]{0:T(256)S(1)} copy-done((s32[256]{0:T(256)S(1)}, s32[256]{0:T(256)}, u32[]{:S(2)}) %copy-start.2) | copy-done | bytes 1048
  3.7 1.0 %copy-done = bf16[256,768]{1,0:T(8,128)(2,1)S(1)} copy-done((bf16[256,768]{1,0:T(8,128)(2,1)S(1)}, bf16[256,768]{1,0:T(8,128)(2,1)}, u32[]{:S(2)}) %copy-start) | copy-done | bytes 393240
  4.7 0.2 pack_own.1
  4.9 1.6 %collective-permute-start.2 = (bf16[1552,128]{1,0:T(8,128)(2,1)S(1)}, bf16[1552,128]{1,0:T(8,128)(2,1)S(1)}, u32[]{:S(2)}, u32[]{:S(2)}) collective-permute-start(bf16[1552,128]{1,0:T(8,128)(2,1)S(1)} %get-tuple-element.26.refs_0_.refs_3_.refs_2_), channel_id=1, source_target_pairs={{0,2},{1,3},{2,0},{3,1},{4,6},{5,7},{6,4},{7,5},{8,10},{9,11},{10,... | collective-permute-start | bytes 1191944 | tf_op jit(solution)/shard_map/ppermute | solution.py:151
  6.4 1.5 %collective-permute-start = (bf16[1552,128]{1,0:T(8,128)(2,1)S(1)}, bf16[1552,128]{1,0:T(8,128)(2,1)S(1)}, u32[]{:S(2)}, u32[]{:S(2)}) collective-permute-start(bf16[1552,128]{1,0:T(8,128)(2,1)S(1)} %get-tuple-element.26.refs_0_.refs_3_.refs_2_), channel_id=1, source_target_pairs={{0,4},{1,5},{2,6},{3,7},{4,0},{5,1},{6,2},{7,3},{8,12},{9,13},{10,... | collective-permute-start | bytes 1191944 | tf_op jit(solution)/shard_map/ppermute | solution.py:151
  8.0 1.6 %collective-permute-start.4 = (f32[1,256]{1,0:T(1,128)S(1)}, f32[1,256]{1,0:T(1,128)S(1)}, u32[]{:S(2)}, u32[]{:S(2)}) collective-permute-start(f32[1,256]{1,0:T(1,128)S(1)} %get-tuple-element.24), channel_id=1, source_target_pairs={{0,8},{8,16},{16,24},{24,0},{1,9},{9,17},{17,25},{25,1},{2,10},{10... | collective-permute-start | bytes 3080 | tf_op jit(solution)/shard_map/ppermute | solution.py:157
  9.5 1.2 %collective-permute-start.5 = (f32[1,256]{1,0:T(1,128)S(1)}, f32[1,256]{1,0:T(1,128)S(1)}, u32[]{:S(2)}, u32[]{:S(2)}) collective-permute-start(f32[1,256]{1,0:T(1,128)S(1)} %get-tuple-element.24), channel_id=1, source_target_pairs={{0,16},{8,24},{16,0},{24,8},{1,17},{9,25},{17,1},{25,9},{2,18},{10... | collective-permute-start | bytes 3080 | tf_op jit(solution)/shard_map/ppermute | solution.py:157
  10.8 3.7 %collective-permute-done.4.key_ref = f32[1,256]{1,0:T(1,128)S(1)} collective-permute-done((f32[1,256]{1,0:T(1,128)S(1)}, f32[1,256]{1,0:T(1,128)S(1)}, u32[]{:S(2)}, u32[]{:S(2)}) %collective-permute-start.4) | collective-permute-done | bytes 1056 | tf_op jit(solution)/shard_map/ppermute | solution.py:157
  14.5 1.1 %collective-permute-start.14 = (bf16[256,768]{1,0:T(8,128)(2,1)S(1)}, bf16[256,768]{1,0:T(8,128)(2,1)S(1)}, u32[]{:S(2)}, u32[]{:S(2)}) collective-permute-start(bf16[256,768]{1,0:T(8,128)(2,1)S(1)} %collective-permute-done.7.emb_ref), channel_id=1, source_target_pairs={{0,8},{8,16},{16,24},{24,0},{1,9},{9,17},{17,25},{25,1},{2,10},{10... | collective-permute-start | bytes 1179656 | tf_op jit(solution)/shard_map/ppermute | solution.py:157
  15.6 0.2 pack.2.refs_5_.refs_4_
  15.8 0.3 collective-permute-start.9
  16.1 0.3 collective-permute-start.8
  16.5 0.4 collective-permute-done.refs_2_
  16.8 1.5 %collective-permute-start.3 = (bf16[784,128]{1,0:T(8,128)(2,1)S(1)}, bf16[784,128]{1,0:T(8,128)(2,1)S(1)}, u32[]{:S(2)}, u32[]{:S(2)}) collective-permute-start(bf16[784,128]{1,0:T(8,128)(2,1)S(1)} %slice.17), channel_id=1, source_target_pairs={{0,4},{1,5},{2,6},{3,7},{4,0},{5,1},{6,2},{7,3},{8,12},{9,13},{10,... | collective-permute-start | bytes 602120 | tf_op jit(solution)/shard_map/ppermute | solution.py:151
  18.4 0.7 %collective-permute-start.1 = (bf16[768,128]{1,0:T(8,128)(2,1)S(1)}, bf16[768,128]{1,0:T(8,128)(2,1)S(1)}, u32[]{:S(2)}, u32[]{:S(2)}) collective-permute-start(bf16[768,128]{1,0:T(8,128)(2,1)S(1)} %slice.16), channel_id=1, source_target_pairs={{0,2},{1,3},{2,0},{3,1},{4,6},{5,7},{6,4},{7,5},{8,10},{9,11},{10,... | collective-permute-start | bytes 589832 | tf_op jit(solution)/shard_map/ppermute | solution.py:151
  19.1 1.5 %compare_direct.1 = (f32[4,1,256]{2,1,0:T(1,128)S(1)}, f32[1,1,256]{2,1,0:T(1,128)S(1)}, f32[1,1,256]{2,1,0:T(1,128)S(1)}, f32[1,1,256]{2,1,0:T(1,128)S(1)}) custom-call(bf16[1552,128]{1,0:T(8,128)(2,1)S(1)} %get-tuple-element.26.refs_0_.refs_3_.refs_2_, bf16[1552,128]{1,0:T(8,128)(2,1)S(1)} %collective-permute-done.2.refs_1_, ...), custom_call_target="tpu_custom_call" | custom-call | flops 1220542464 | bytes 2781184 | tf_op jit(solution)/shard_map/compare_direct/pallas_call | solution.py:122
  20.6 1.5 %collective-permute-start.10 = (f32[1,1,256]{2,1,0:T(1,128)S(1)}, f32[1,1,256]{2,1,0:T(1,128)S(1)}, u32[]{:S(2)}, u32[]{:S(2)}) collective-permute-start(f32[1,1,256]{2,1,0:T(1,128)S(1)} %get-tuple-element.28), channel_id=1, source_target_pairs={{0,2},{1,3},{2,0},{3,1},{4,6},{5,7},{6,4},{7,5},{8,10},{9,11},{10,... | collective-permute-start | bytes 3080 | tf_op jit(solution)/shard_map/ppermute | solution.py:151
  22.1 0.5 %collective-permute-start.11 = (f32[1,1,256]{2,1,0:T(1,128)S(1)}, f32[1,1,256]{2,1,0:T(1,128)S(1)}, u32[]{:S(2)}, u32[]{:S(2)}) collective-permute-start(f32[1,1,256]{2,1,0:T(1,128)S(1)} %get-tuple-element.29), channel_id=1, source_target_pairs={{0,4},{1,5},{2,6},{3,7},{4,0},{5,1},{6,2},{7,3},{8,12},{9,13},{10,... | collective-permute-start | bytes 3080 | tf_op jit(solution)/shard_map/ppermute | solution.py:151
  22.6 1.8 %collective-permute-done.10 = f32[1,1,256]{2,1,0:T(1,128)S(1)} collective-permute-done((f32[1,1,256]{2,1,0:T(1,128)S(1)}, f32[1,1,256]{2,1,0:T(1,128)S(1)}, u32[]{:S(2)}, u32[]{:S(2)}) %collective-permute-start.10) | collective-permute-done | bytes 1056 | tf_op jit(solution)/shard_map/ppermute | solution.py:151
  24.4 1.2 %collective-permute-done.11 = f32[1,1,256]{2,1,0:T(1,128)S(1)} collective-permute-done((f32[1,1,256]{2,1,0:T(1,128)S(1)}, f32[1,1,256]{2,1,0:T(1,128)S(1)}, u32[]{:S(2)}, u32[]{:S(2)}) %collective-permute-start.11) | collective-permute-done | bytes 1056 | tf_op jit(solution)/shard_map/ppermute | solution.py:151
  25.6 0.7 %compare_relayed.1 = (f32[1,1,256]{2,1,0:T(1,128)S(1)}, f32[1,1,256]{2,1,0:T(1,128)S(1)}, f32[2,1,256]{2,1,0:T(1,128)S(1)}, f32[1,1,256]{2,1,0:T(1,128)S(1)}) custom-call(bf16[768,128]{1,0:T(8,128)(2,1)S(1)} %collective-permute-done.1.refs_0_.refs_3_, bf16[784,128]{1,0:T(8,128)(2,1)S(1)} %collective-permute-done.3.refs_1_.refs_4_, ...), custom_call_target="tpu_custom_call" | custom-call | flops 406847488 | bytes 1986560 | tf_op jit(solution)/shard_map/compare_relayed/pallas_call | solution.py:122
  26.4 1.1 %collective-permute-done.12.refs_2_ = f32[2,1,256]{2,1,0:T(1,128)S(1)} collective-permute-done((f32[2,1,256]{2,1,0:T(1,128)S(1)}, f32[2,1,256]{2,1,0:T(1,128)S(1)}, u32[]{:S(2)}, u32[]{:S(2)}) %collective-permute-start.12) | collective-permute-done | bytes 2080 | tf_op jit(solution)/shard_map/ppermute | solution.py:151
  27.6 0.2 collective-permute-done.14.emb_ref
  28.0 2.5 %collective-permute-start.17 = (f32[1,1,256]{2,1,0:T(1,128)S(1)}, f32[1,1,256]{2,1,0:T(1,128)S(1)}, u32[]{:S(2)}, u32[]{:S(2)}) collective-permute-start(f32[1,1,256]{2,1,0:T(1,128)S(1)} %get-tuple-element.39), channel_id=1, source_target_pairs={{0,6},{1,7},{2,4},{3,5},{4,2},{5,3},{6,0},{7,1},{8,14},{9,15},{10,... | collective-permute-start | bytes 3080 | tf_op jit(solution)/shard_map/ppermute | solution.py:151
  30.6 1.3 %collective-permute-start.13 = (f32[1,1,256]{2,1,0:T(1,128)S(1)}, f32[1,1,256]{2,1,0:T(1,128)S(1)}, u32[]{:S(2)}, u32[]{:S(2)}) collective-permute-start(f32[1,1,256]{2,1,0:T(1,128)S(1)} %bitcast.20), channel_id=1, source_target_pairs={{0,24},{8,0},{16,8},{24,16},{1,25},{9,1},{17,9},{25,17},{2,26},{10... | collective-permute-start | bytes 3080 | tf_op jit(solution)/shard_map/ppermute | solution.py:157
  31.9 0.6 %compare_half_way.1 = f32[1,1,256]{2,1,0:T(1,128)S(1)} custom-call(bf16[1552,128]{1,0:T(8,128)(2,1)S(1)} %get-tuple-element.26.refs_0_.refs_3_.refs_2_, bf16[1552,128]{1,0:T(8,128)(2,1)S(1)} %collective-permute-done.2.refs_1_, bf16[1552,128]{1,0:T(8,128)(2,1)S(1)} %collective-permute-done.refs_2_, ...), custom_call_target="tpu_custom_call" | custom-call | flops 406847488 | bytes 1986560 | tf_op jit(solution)/shard_map/compare_half_way/pallas_call | solution.py:122
  32.6 0.6 %compare_twin.1 = f32[1,1,256]{2,1,0:T(1,128)S(1)} custom-call(bf16[1552,128]{1,0:T(8,128)(2,1)S(1)} %get-tuple-element.26.refs_0_.refs_3_.refs_2_, bf16[1552,128]{1,0:T(8,128)(2,1)S(1)} %collective-permute-done.2.refs_1_, bf16[1552,128]{1,0:T(8,128)(2,1)S(1)} %collective-permute-done.refs_2_, bf16[768,128]{1,0:T(8,128)(2,1)S(1)} %collective-permute-done.1.refs_0_.refs_3_, ...), custom_call_target="tpu_custom_call" | custom-call | flops 406847488 | bytes 1986560 | tf_op jit(solution)/shard_map/compare_twin/pallas_call | solution.py:122
  33.3 2.1 %collective-permute-start.18 = (f32[1,1,256]{2,1,0:T(1,128)S(1)}, f32[1,1,256]{2,1,0:T(1,128)S(1)}, u32[]{:S(2)}, u32[]{:S(2)}) collective-permute-start(f32[1,1,256]{2,1,0:T(1,128)S(1)} %compare_twin.1), channel_id=1, source_target_pairs={{0,17},{1,16},{2,19},{3,18},{4,21},{5,20},{6,23},{7,22},{8,25},{9,... | collective-permute-start | bytes 3080 | tf_op jit(solution)/shard_map/ppermute | solution.py:161
  35.3 1.7 %collective-permute-done.15 = f32[1,1,256]{2,1,0:T(1,128)S(1)} collective-permute-done((f32[1,1,256]{2,1,0:T(1,128)S(1)}, f32[1,1,256]{2,1,0:T(1,128)S(1)}, u32[]{:S(2)}, u32[]{:S(2)}) %collective-permute-start.15) | collective-permute-done | bytes 1056 | tf_op jit(solution)/shard_map/ppermute | solution.py:157
  37.1 0.2 collective-permute-done.18
  37.2 0.6 %maximum_maximum_fusion = f32[1,1,256]{2,1,0:T(1,128)} fusion(f32[1,1,256]{2,1,0:T(1,128)S(1)} %collective-permute-done.17, f32[1,1,256]{2,1,0:T(1,128)S(1)} %collective-permute-done.11, f32[1,1,256]{2,1,0:T(1,128)S(1)} %collective-permute-done.10, f32[1,1,256]{2,1,0:T(1,128)S(1)} %collective-permute-done.18, f32[1,1,256]{2,1,0:T(1,128)S(1)} %collective-permute-done.15, ...), kind=kLoop, calls=%fused_computation.4 | loop fusion | flops 1792 | bytes 9216 | tf_op jit(solution)/shard_map/max | solution.py:238
  (25 shorter events, 0.5 us)
Async XLA Ops:
  0.0 14.5 %collective-permute-start.7 = (bf16[256,768]{1,0:T(8,128)(2,1)}, bf16[256,768]{1,0:T(8,128)(2,1)S(1)}, u32[]{:S(2)}, u32[]{:S(2)}) collective-permute-start(bf16[256,768]{1,0:T(8,128)(2,1)} %emb_ref.1), channel_id=1, source_target_pairs={{0,8},{8,16},{16,24},{24,0},{1,9},{9,17},{17,25},{25,1},{2,10},{10... | collective-permute-start | bytes 1179656 | tf_op jit(solution)/shard_map/ppermute | solution.py:157
  3.0 0.7 %copy-start.2 = (s32[256]{0:T(256)S(1)}, s32[256]{0:T(256)}, u32[]{:S(2)}) copy-start(s32[256]{0:T(256)} %param.5) | copy-start | bytes 3076
  3.0 0.7 %copy-start.1 = (s32[256,1]{0,1:T(1,128)S(1)}, s32[256,1]{0,1:T(1,128)}, u32[]{:S(2)}) copy-start(s32[256,1]{0,1:T(1,128)} %param.4) | copy-start | bytes 3076
  3.7 1.0 %copy-start = (bf16[256,768]{1,0:T(8,128)(2,1)S(1)}, bf16[256,768]{1,0:T(8,128)(2,1)}, u32[]{:S(2)}) copy-start(bf16[256,768]{1,0:T(8,128)(2,1)} %emb_ref.1) | copy-start | bytes 1179652
  4.9 11.2 %collective-permute-start.2 = (bf16[1552,128]{1,0:T(8,128)(2,1)S(1)}, bf16[1552,128]{1,0:T(8,128)(2,1)S(1)}, u32[]{:S(2)}, u32[]{:S(2)}) collective-permute-start(bf16[1552,128]{1,0:T(8,128)(2,1)S(1)} %get-tuple-element.26.refs_0_.refs_3_.refs_2_), channel_id=1, source_target_pairs={{0,2},{1,3},{2,0},{3,1},{4,6},{5,7},{6,4},{7,5},{8,10},{9,11},{10,... | collective-permute-start | bytes 1191944 | tf_op jit(solution)/shard_map/ppermute | solution.py:151
  6.4 10.4 %collective-permute-start = (bf16[1552,128]{1,0:T(8,128)(2,1)S(1)}, bf16[1552,128]{1,0:T(8,128)(2,1)S(1)}, u32[]{:S(2)}, u32[]{:S(2)}) collective-permute-start(bf16[1552,128]{1,0:T(8,128)(2,1)S(1)} %get-tuple-element.26.refs_0_.refs_3_.refs_2_), channel_id=1, source_target_pairs={{0,4},{1,5},{2,6},{3,7},{4,0},{5,1},{6,2},{7,3},{8,12},{9,13},{10,... | collective-permute-start | bytes 1191944 | tf_op jit(solution)/shard_map/ppermute | solution.py:151
  8.0 6.5 %collective-permute-start.4 = (f32[1,256]{1,0:T(1,128)S(1)}, f32[1,256]{1,0:T(1,128)S(1)}, u32[]{:S(2)}, u32[]{:S(2)}) collective-permute-start(f32[1,256]{1,0:T(1,128)S(1)} %get-tuple-element.24), channel_id=1, source_target_pairs={{0,8},{8,16},{16,24},{24,0},{1,9},{9,17},{17,25},{25,1},{2,10},{10... | collective-permute-start | bytes 3080 | tf_op jit(solution)/shard_map/ppermute | solution.py:157
  9.5 4.9 %collective-permute-start.5 = (f32[1,256]{1,0:T(1,128)S(1)}, f32[1,256]{1,0:T(1,128)S(1)}, u32[]{:S(2)}, u32[]{:S(2)}) collective-permute-start(f32[1,256]{1,0:T(1,128)S(1)} %get-tuple-element.24), channel_id=1, source_target_pairs={{0,16},{8,24},{16,0},{24,8},{1,17},{9,25},{17,1},{25,9},{2,18},{10... | collective-permute-start | bytes 3080 | tf_op jit(solution)/shard_map/ppermute | solution.py:157
  14.5 3.9 %collective-permute-start.6 = (bf16[1552,128]{1,0:T(8,128)(2,1)S(1)}, bf16[1552,128]{1,0:T(8,128)(2,1)S(1)}, u32[]{:S(2)}, u32[]{:S(2)}) collective-permute-start(bf16[1552,128]{1,0:T(8,128)(2,1)S(1)} %get-tuple-element.26.refs_0_.refs_3_.refs_2_), channel_id=1, source_target_pairs={{0,1},{1,0},{2,3},{3,2},{4,5},{5,4},{6,7},{7,6},{8,9},{9,8},{10,11... | collective-permute-start | bytes 1191944 | tf_op jit(solution)/shard_map/ppermute | solution.py:151
  14.5 13.3 %collective-permute-start.14 = (bf16[256,768]{1,0:T(8,128)(2,1)S(1)}, bf16[256,768]{1,0:T(8,128)(2,1)S(1)}, u32[]{:S(2)}, u32[]{:S(2)}) collective-permute-start(bf16[256,768]{1,0:T(8,128)(2,1)S(1)} %collective-permute-done.7.emb_ref), channel_id=1, source_target_pairs={{0,8},{8,16},{16,24},{24,0},{1,9},{9,17},{17,25},{25,1},{2,10},{10... | collective-permute-start | bytes 1179656 | tf_op jit(solution)/shard_map/ppermute | solution.py:157
  15.8 3.3 %collective-permute-start.9 = (bf16[784,128]{1,0:T(8,128)(2,1)S(1)}, bf16[784,128]{1,0:T(8,128)(2,1)S(1)}, u32[]{:S(2)}, u32[]{:S(2)}) collective-permute-start(bf16[784,128]{1,0:T(8,128)(2,1)S(1)} %slice.19), channel_id=1, source_target_pairs={{0,1},{1,0},{2,3},{3,2},{4,5},{5,4},{6,7},{7,6},{8,9},{9,8},{10,11... | collective-permute-start | bytes 602120 | tf_op jit(solution)/shard_map/ppermute | solution.py:151
  16.1 3.0 %collective-permute-start.8 = (bf16[768,128]{1,0:T(8,128)(2,1)S(1)}, bf16[768,128]{1,0:T(8,128)(2,1)S(1)}, u32[]{:S(2)}, u32[]{:S(2)}) collective-permute-start(bf16[768,128]{1,0:T(8,128)(2,1)S(1)} %slice.18), channel_id=1, source_target_pairs={{0,1},{1,0},{2,3},{3,2},{4,5},{5,4},{6,7},{7,6},{8,9},{9,8},{10,11... | collective-permute-start | bytes 589832 | tf_op jit(solution)/shard_map/ppermute | solution.py:151
  16.8 8.8 %collective-permute-start.3 = (bf16[784,128]{1,0:T(8,128)(2,1)S(1)}, bf16[784,128]{1,0:T(8,128)(2,1)S(1)}, u32[]{:S(2)}, u32[]{:S(2)}) collective-permute-start(bf16[784,128]{1,0:T(8,128)(2,1)S(1)} %slice.17), channel_id=1, source_target_pairs={{0,4},{1,5},{2,6},{3,7},{4,0},{5,1},{6,2},{7,3},{8,12},{9,13},{10,... | collective-permute-start | bytes 602120 | tf_op jit(solution)/shard_map/ppermute | solution.py:151
  18.4 7.3 %collective-permute-start.1 = (bf16[768,128]{1,0:T(8,128)(2,1)S(1)}, bf16[768,128]{1,0:T(8,128)(2,1)S(1)}, u32[]{:S(2)}, u32[]{:S(2)}) collective-permute-start(bf16[768,128]{1,0:T(8,128)(2,1)S(1)} %slice.16), channel_id=1, source_target_pairs={{0,2},{1,3},{2,0},{3,1},{4,6},{5,7},{6,4},{7,5},{8,10},{9,11},{10,... | collective-permute-start | bytes 589832 | tf_op jit(solution)/shard_map/ppermute | solution.py:151
  20.6 3.8 %collective-permute-start.10 = (f32[1,1,256]{2,1,0:T(1,128)S(1)}, f32[1,1,256]{2,1,0:T(1,128)S(1)}, u32[]{:S(2)}, u32[]{:S(2)}) collective-permute-start(f32[1,1,256]{2,1,0:T(1,128)S(1)} %get-tuple-element.28), channel_id=1, source_target_pairs={{0,2},{1,3},{2,0},{3,1},{4,6},{5,7},{6,4},{7,5},{8,10},{9,11},{10,... | collective-permute-start | bytes 3080 | tf_op jit(solution)/shard_map/ppermute | solution.py:151
  22.1 3.6 %collective-permute-start.11 = (f32[1,1,256]{2,1,0:T(1,128)S(1)}, f32[1,1,256]{2,1,0:T(1,128)S(1)}, u32[]{:S(2)}, u32[]{:S(2)}) collective-permute-start(f32[1,1,256]{2,1,0:T(1,128)S(1)} %get-tuple-element.29), channel_id=1, source_target_pairs={{0,4},{1,5},{2,6},{3,7},{4,0},{5,1},{6,2},{7,3},{8,12},{9,13},{10,... | collective-permute-start | bytes 3080 | tf_op jit(solution)/shard_map/ppermute | solution.py:151
  26.3 1.2 %collective-permute-start.12 = (f32[2,1,256]{2,1,0:T(1,128)S(1)}, f32[2,1,256]{2,1,0:T(1,128)S(1)}, u32[]{:S(2)}, u32[]{:S(2)}) collective-permute-start(f32[2,1,256]{2,1,0:T(1,128)S(1)} %get-tuple-element.33), channel_id=1, source_target_pairs={{0,1},{1,0},{2,3},{3,2},{4,5},{5,4},{6,7},{7,6},{8,9},{9,8},{10,11... | collective-permute-start | bytes 6152 | tf_op jit(solution)/shard_map/ppermute | solution.py:151
  28.0 4.7 %collective-permute-start.16 = (bf16[1552,128]{1,0:T(8,128)(2,1)S(1)}, bf16[1552,128]{1,0:T(8,128)(2,1)S(1)}, u32[]{:S(2)}, u32[]{:S(2)}) collective-permute-start(bf16[1552,128]{1,0:T(8,128)(2,1)S(1)} %pack.3.refs_5_), channel_id=1, source_target_pairs={{0,1},{1,0},{2,3},{3,2},{4,5},{5,4},{6,7},{7,6},{8,9},{9,8},{10,11... | collective-permute-start | bytes 1191944 | tf_op jit(solution)/shard_map/ppermute | solution.py:151
  28.0 4.6 %collective-permute-start.17 = (f32[1,1,256]{2,1,0:T(1,128)S(1)}, f32[1,1,256]{2,1,0:T(1,128)S(1)}, u32[]{:S(2)}, u32[]{:S(2)}) collective-permute-start(f32[1,1,256]{2,1,0:T(1,128)S(1)} %get-tuple-element.39), channel_id=1, source_target_pairs={{0,6},{1,7},{2,4},{3,5},{4,2},{5,3},{6,0},{7,1},{8,14},{9,15},{10,... | collective-permute-start | bytes 3080 | tf_op jit(solution)/shard_map/ppermute | solution.py:151
  30.6 4.8 %collective-permute-start.13 = (f32[1,1,256]{2,1,0:T(1,128)S(1)}, f32[1,1,256]{2,1,0:T(1,128)S(1)}, u32[]{:S(2)}, u32[]{:S(2)}) collective-permute-start(f32[1,1,256]{2,1,0:T(1,128)S(1)} %bitcast.20), channel_id=1, source_target_pairs={{0,24},{8,0},{16,8},{24,16},{1,25},{9,1},{17,9},{25,17},{2,26},{10... | collective-permute-start | bytes 3080 | tf_op jit(solution)/shard_map/ppermute | solution.py:157
  32.5 4.5 %collective-permute-start.15 = (f32[1,1,256]{2,1,0:T(1,128)S(1)}, f32[1,1,256]{2,1,0:T(1,128)S(1)}, u32[]{:S(2)}, u32[]{:S(2)}) collective-permute-start(f32[1,1,256]{2,1,0:T(1,128)S(1)} %compare_half_way.1), channel_id=1, source_target_pairs={{0,16},{8,24},{16,0},{24,8},{1,17},{9,25},{17,1},{25,9},{2,18},{10... | collective-permute-start | bytes 3080 | tf_op jit(solution)/shard_map/ppermute | solution.py:157
  33.3 4.0 %collective-permute-start.18 = (f32[1,1,256]{2,1,0:T(1,128)S(1)}, f32[1,1,256]{2,1,0:T(1,128)S(1)}, u32[]{:S(2)}, u32[]{:S(2)}) collective-permute-start(f32[1,1,256]{2,1,0:T(1,128)S(1)} %compare_twin.1), channel_id=1, source_target_pairs={{0,17},{1,16},{2,19},{3,18},{4,21},{5,20},{6,23},{7,22},{8,25},{9,... | collective-permute-start | bytes 3080 | tf_op jit(solution)/shard_map/ppermute | solution.py:161

commit v8 on v7

--- a/solution.py
+++ b/solution.py
@@ -211,7 +211,7 @@
         [tuple(every)],
     )
     early = [plane_shift(best, mask) for best, mask in zip(rows_direct[1:], direct[1:])]
-    best = lax.optimization_barrier((best, early))[0]
+    best = lax.optimization_barrier((best, early[0]))[0]
     own, one_off_best, twins, *rows_relayed = score(
         "compare_relayed",
         rows,
@@ -223,6 +223,7 @@
         known=every,
         cols_in=[best],
     )
+    twins = lax.optimization_barrier((twins, early))[0]
     own, one_off_best = join([own, one_off_best], plane_shift(twins, 1))
     found = [own.reshape(1, 1, -1), rows_direct[0]]
     early += [plane_shift(best, mask) for best, mask in zip(rows_relayed, relayed)]

time: 38 us -> 37.9 us (level)
  waiting for transfers between devices: 10.4 us -> 11.3 us
  starting transfers between devices: 21 us -> 20.1 us
    ppermute x6, waiting for transfers between devices: 5.66 us -> 6.43 us  [grp_shift(): lax.ppermute(x, 'grp', [(z, (z + shift) % groups) for z in range(groups)])]
    ppermute x6, starting transfers between devices: 8.35 us -> 7.92 us  [grp_shift(): lax.ppermute(x, 'grp', [(z, (z + shift) % groups) for z in range(groups)])]
    ppermute x1, waiting for transfers between devices: 0.16 us -> 0.54 us  [grp_shift(): return lax.ppermute(x, ('grp', 'blk'), pairs)]
    ppermute x1, starting transfers between devices: 2.07 us -> 1.69 us  [grp_shift(): return lax.ppermute(x, ('grp', 'blk'), pairs)]
  transfers between devices with their start and end apart: 19 -> 19, of which waited for: 8 -> 9; matrix products, arithmetic and copies ran while one was open for 0% -> 0% of each run, Pallas kernels for 10% -> 10%
where the time goes in v8:
time: 37.9 us; the launch traced here: 37.7 us
  starting transfers between devices  20.1 us (53%)
  waiting for transfers between devices  11.3 us (30%)
  Pallas kernels  3.98 us (11%)
  local copies, waits for them, and re-layouts  1.75 us (5%)
  other arithmetic  0.57 us (2%)
    ppermute x12, starting transfers between devices, plane_shift(): return lax.ppermute(x, 'blk', [(i, i ^ mask) for i in range(size)])  10.5 us
    ppermute x6, starting transfers between devices, grp_shift(): lax.ppermute(x, 'grp', [(z, (z + shift) % groups) for z in range(groups)])  7.92 us
    ppermute x6, waiting for transfers between devices, grp_shift(): lax.ppermute(x, 'grp', [(z, (z + shift) % groups) for z in range(groups)])  6.43 us
    ppermute x12, waiting for transfers between devices, plane_shift(): return lax.ppermute(x, 'blk', [(i, i ^ mask) for i in range(size)])  4.28 us
    pallas_call x4, Pallas kernels, score(): pl.pallas_call(kernel, out_shape=[jax.ShapeDtypeStruct((count, 1, rows),...  3.49 us
    unnamed x6, local copies, waits for them, and re-layouts  1.69 us
    ppermute x1, starting transfers between devices, grp_shift(): return lax.ppermute(x, ('grp', 'blk'), pairs)  1.69 us
  transfers between devices with their start and end apart: 19, of which 9 were waited for; matrix products, arithmetic and copies ran while one was open for 0% of the time, Pallas kernels for 10%

profile of v8, /device:TPU:0, one launch (start us, length us, event | category | flops | bytes accessed | tf_op | source)
XLA Modules:
  0.0 37.7 jit_solution(17667779359277112044)
XLA Ops:
  0.0 3.0 %collective-permute-start.7 = (bf16[256,768]{1,0:T(8,128)(2,1)}, bf16[256,768]{1,0:T(8,128)(2,1)S(1)}, u32[]{:S(2)}, u32[]{:S(2)}) collective-permute-start(bf16[256,768]{1,0:T(8,128)(2,1)} %emb_ref.1), channel_id=1, source_target_pairs={{0,8},{8,16},{16,24},{24,0},{1,9},{9,17},{17,25},{25,1},{2,10},{10... | collective-permute-start | bytes 1179656 | tf_op jit(solution)/shard_map/ppermute | solution.py:157
  3.0 0.7 %copy-done.2 = s32[256]{0:T(256)S(1)} copy-done((s32[256]{0:T(256)S(1)}, s32[256]{0:T(256)}, u32[]{:S(2)}) %copy-start.2) | copy-done | bytes 1048
  3.7 1.0 %copy-done = bf16[256,768]{1,0:T(8,128)(2,1)S(1)} copy-done((bf16[256,768]{1,0:T(8,128)(2,1)S(1)}, bf16[256,768]{1,0:T(8,128)(2,1)}, u32[]{:S(2)}) %copy-start) | copy-done | bytes 393240
  4.9 1.6 %collective-permute-start.2 = (bf16[1552,128]{1,0:T(8,128)(2,1)S(1)}, bf16[1552,128]{1,0:T(8,128)(2,1)S(1)}, u32[]{:S(2)}, u32[]{:S(2)}) collective-permute-start(bf16[1552,128]{1,0:T(8,128)(2,1)S(1)} %get-tuple-element.27.refs_0_.refs_3_.refs_2_), channel_id=1, source_target_pairs={{0,2},{1,3},{2,0},{3,1},{4,6},{5,7},{6,4},{7,5},{8,10},{9,11},{10,... | collective-permute-start | bytes 1191944 | tf_op jit(solution)/shard_map/ppermute | solution.py:151
  6.4 1.5 %collective-permute-start = (bf16[1552,128]{1,0:T(8,128)(2,1)S(1)}, bf16[1552,128]{1,0:T(8,128)(2,1)S(1)}, u32[]{:S(2)}, u32[]{:S(2)}) collective-permute-start(bf16[1552,128]{1,0:T(8,128)(2,1)S(1)} %get-tuple-element.27.refs_0_.refs_3_.refs_2_), channel_id=1, source_target_pairs={{0,4},{1,5},{2,6},{3,7},{4,0},{5,1},{6,2},{7,3},{8,12},{9,13},{10,... | collective-permute-start | bytes 1191944 | tf_op jit(solution)/shard_map/ppermute | solution.py:151
  8.0 1.6 %collective-permute-start.4 = (f32[1,256]{1,0:T(1,128)S(1)}, f32[1,256]{1,0:T(1,128)S(1)}, u32[]{:S(2)}, u32[]{:S(2)}) collective-permute-start(f32[1,256]{1,0:T(1,128)S(1)} %get-tuple-element.25), channel_id=1, source_target_pairs={{0,8},{8,16},{16,24},{24,0},{1,9},{9,17},{17,25},{25,1},{2,10},{10... | collective-permute-start | bytes 3080 | tf_op jit(solution)/shard_map/ppermute | solution.py:157
  9.5 1.2 %collective-permute-start.5 = (f32[1,256]{1,0:T(1,128)S(1)}, f32[1,256]{1,0:T(1,128)S(1)}, u32[]{:S(2)}, u32[]{:S(2)}) collective-permute-start(f32[1,256]{1,0:T(1,128)S(1)} %get-tuple-element.25), channel_id=1, source_target_pairs={{0,16},{8,24},{16,0},{24,8},{1,17},{9,25},{17,1},{25,9},{2,18},{10... | collective-permute-start | bytes 3080 | tf_op jit(solution)/shard_map/ppermute | solution.py:157
  10.8 3.7 %collective-permute-done.4.key_ref = f32[1,256]{1,0:T(1,128)S(1)} collective-permute-done((f32[1,256]{1,0:T(1,128)S(1)}, f32[1,256]{1,0:T(1,128)S(1)}, u32[]{:S(2)}, u32[]{:S(2)}) %collective-permute-start.4) | collective-permute-done | bytes 1056 | tf_op jit(solution)/shard_map/ppermute | solution.py:157
  14.5 1.1 %collective-permute-start.14 = (bf16[256,768]{1,0:T(8,128)(2,1)S(1)}, bf16[256,768]{1,0:T(8,128)(2,1)S(1)}, u32[]{:S(2)}, u32[]{:S(2)}) collective-permute-start(bf16[256,768]{1,0:T(8,128)(2,1)S(1)} %collective-permute-done.7.emb_ref), channel_id=1, source_target_pairs={{0,8},{8,16},{16,24},{24,0},{1,9},{9,17},{17,25},{25,1},{2,10},{10... | collective-permute-start | bytes 1179656 | tf_op jit(solution)/shard_map/ppermute | solution.py:157
  15.6 0.2 pack.2.refs_5_.refs_4_
  15.8 0.3 collective-permute-start.9
  16.1 0.3 collective-permute-start.8
  16.5 0.4 collective-permute-done.refs_2_
  16.8 1.5 %collective-permute-start.3 = (bf16[784,128]{1,0:T(8,128)(2,1)S(1)}, bf16[784,128]{1,0:T(8,128)(2,1)S(1)}, u32[]{:S(2)}, u32[]{:S(2)}) collective-permute-start(bf16[784,128]{1,0:T(8,128)(2,1)S(1)} %slice.17), channel_id=1, source_target_pairs={{0,4},{1,5},{2,6},{3,7},{4,0},{5,1},{6,2},{7,3},{8,12},{9,13},{10,... | collective-permute-start | bytes 602120 | tf_op jit(solution)/shard_map/ppermute | solution.py:151
  18.4 0.7 %collective-permute-start.1 = (bf16[768,128]{1,0:T(8,128)(2,1)S(1)}, bf16[768,128]{1,0:T(8,128)(2,1)S(1)}, u32[]{:S(2)}, u32[]{:S(2)}) collective-permute-start(bf16[768,128]{1,0:T(8,128)(2,1)S(1)} %slice.16), channel_id=1, source_target_pairs={{0,2},{1,3},{2,0},{3,1},{4,6},{5,7},{6,4},{7,5},{8,10},{9,11},{10,... | collective-permute-start | bytes 589832 | tf_op jit(solution)/shard_map/ppermute | solution.py:151
  19.1 1.5 %compare_direct.1 = (f32[4,1,256]{2,1,0:T(1,128)S(1)}, f32[1,1,256]{2,1,0:T(1,128)S(1)}, f32[1,1,256]{2,1,0:T(1,128)S(1)}, f32[1,1,256]{2,1,0:T(1,128)S(1)}) custom-call(bf16[1552,128]{1,0:T(8,128)(2,1)S(1)} %get-tuple-element.27.refs_0_.refs_3_.refs_2_, bf16[1552,128]{1,0:T(8,128)(2,1)S(1)} %collective-permute-done.2.refs_1_, ...), custom_call_target="tpu_custom_call" | custom-call | flops 1220542464 | bytes 2781184 | tf_op jit(solution)/shard_map/compare_direct/pallas_call | solution.py:122
  20.6 1.5 %collective-permute-start.10 = (f32[1,1,256]{2,1,0:T(1,128)S(1)}, f32[1,1,256]{2,1,0:T(1,128)S(1)}, u32[]{:S(2)}, u32[]{:S(2)}) collective-permute-start(f32[1,1,256]{2,1,0:T(1,128)S(1)} %get-tuple-element.29), channel_id=1, source_target_pairs={{0,2},{1,3},{2,0},{3,1},{4,6},{5,7},{6,4},{7,5},{8,10},{9,11},{10,... | collective-permute-start | bytes 3080 | tf_op jit(solution)/shard_map/ppermute | solution.py:151
  22.1 0.5 %collective-permute-start.11 = (f32[1,1,256]{2,1,0:T(1,128)S(1)}, f32[1,1,256]{2,1,0:T(1,128)S(1)}, u32[]{:S(2)}, u32[]{:S(2)}) collective-permute-start(f32[1,1,256]{2,1,0:T(1,128)S(1)} %get-tuple-element.34), channel_id=1, source_target_pairs={{0,4},{1,5},{2,6},{3,7},{4,0},{5,1},{6,2},{7,3},{8,12},{9,13},{10,... | collective-permute-start | bytes 3080 | tf_op jit(solution)/shard_map/ppermute | solution.py:151
  22.6 1.8 %collective-permute-done.10 = f32[1,1,256]{2,1,0:T(1,128)S(1)} collective-permute-done((f32[1,1,256]{2,1,0:T(1,128)S(1)}, f32[1,1,256]{2,1,0:T(1,128)S(1)}, u32[]{:S(2)}, u32[]{:S(2)}) %collective-permute-start.10) | collective-permute-done | bytes 1056 | tf_op jit(solution)/shard_map/ppermute | solution.py:151
  24.4 0.7 %compare_relayed.1 = (f32[1,1,256]{2,1,0:T(1,128)S(1)}, f32[1,1,256]{2,1,0:T(1,128)S(1)}, f32[2,1,256]{2,1,0:T(1,128)S(1)}, f32[1,1,256]{2,1,0:T(1,128)S(1)}) custom-call(bf16[768,128]{1,0:T(8,128)(2,1)S(1)} %collective-permute-done.1.refs_0_.refs_3_, bf16[784,128]{1,0:T(8,128)(2,1)S(1)} %collective-permute-done.3.refs_1_.refs_4_, ...), custom_call_target="tpu_custom_call" | custom-call | flops 406847488 | bytes 1986560 | tf_op jit(solution)/shard_map/compare_relayed/pallas_call | solution.py:122
  25.1 0.5 %collective-permute-done.11 = f32[1,1,256]{2,1,0:T(1,128)S(1)} collective-permute-done((f32[1,1,256]{2,1,0:T(1,128)S(1)}, f32[1,1,256]{2,1,0:T(1,128)S(1)}, u32[]{:S(2)}, u32[]{:S(2)}) %collective-permute-start.11) | collective-permute-done | bytes 1056 | tf_op jit(solution)/shard_map/ppermute | solution.py:151
  25.6 1.2 %collective-permute-done.12.refs_2_ = f32[2,1,256]{2,1,0:T(1,128)S(1)} collective-permute-done((f32[2,1,256]{2,1,0:T(1,128)S(1)}, f32[2,1,256]{2,1,0:T(1,128)S(1)}, u32[]{:S(2)}, u32[]{:S(2)}) %collective-permute-start.12) | collective-permute-done | bytes 2080 | tf_op jit(solution)/shard_map/ppermute | solution.py:151
  26.8 1.0 %collective-permute-done.14.emb_ref = bf16[256,768]{1,0:T(8,128)(2,1)S(1)} collective-permute-done((bf16[256,768]{1,0:T(8,128)(2,1)S(1)}, bf16[256,768]{1,0:T(8,128)(2,1)S(1)}, u32[]{:S(2)}, u32[]{:S(2)}) %collective-permute-start.14) | collective-permute-done | bytes 393248 | tf_op jit(solution)/shard_map/ppermute | solution.py:157
  28.0 2.5 %collective-permute-start.17 = (f32[1,1,256]{2,1,0:T(1,128)S(1)}, f32[1,1,256]{2,1,0:T(1,128)S(1)}, u32[]{:S(2)}, u32[]{:S(2)}) collective-permute-start(f32[1,1,256]{2,1,0:T(1,128)S(1)} %get-tuple-element.41), channel_id=1, source_target_pairs={{0,6},{1,7},{2,4},{3,5},{4,2},{5,3},{6,0},{7,1},{8,14},{9,15},{10,... | collective-permute-start | bytes 3080 | tf_op jit(solution)/shard_map/ppermute | solution.py:151
  30.6 0.9 %collective-permute-start.13 = (f32[1,1,256]{2,1,0:T(1,128)S(1)}, f32[1,1,256]{2,1,0:T(1,128)S(1)}, u32[]{:S(2)}, u32[]{:S(2)}) collective-permute-start(f32[1,1,256]{2,1,0:T(1,128)S(1)} %bitcast.20), channel_id=1, source_target_pairs={{0,24},{8,0},{16,8},{24,16},{1,25},{9,1},{17,9},{25,17},{2,26},{10... | collective-permute-start | bytes 3080 | tf_op jit(solution)/shard_map/ppermute | solution.py:157
  31.5 0.6 %compare_half_way.1 = f32[1,1,256]{2,1,0:T(1,128)S(1)} custom-call(bf16[1552,128]{1,0:T(8,128)(2,1)S(1)} %get-tuple-element.27.refs_0_.refs_3_.refs_2_, bf16[1552,128]{1,0:T(8,128)(2,1)S(1)} %collective-permute-done.2.refs_1_, bf16[1552,128]{1,0:T(8,128)(2,1)S(1)} %collective-permute-done.refs_2_, ...), custom_call_target="tpu_custom_call" | custom-call | flops 406847488 | bytes 1986560 | tf_op jit(solution)/shard_map/compare_half_way/pallas_call | solution.py:122
  32.2 0.4 %collective-permute-done.17 = f32[1,1,256]{2,1,0:T(1,128)S(1)} collective-permute-done((f32[1,1,256]{2,1,0:T(1,128)S(1)}, f32[1,1,256]{2,1,0:T(1,128)S(1)}, u32[]{:S(2)}, u32[]{:S(2)}) %collective-permute-start.17) | collective-permute-done | bytes 1056 | tf_op jit(solution)/shard_map/ppermute | solution.py:151
  32.6 0.6 %compare_twin.1 = f32[1,1,256]{2,1,0:T(1,128)S(1)} custom-call(bf16[1552,128]{1,0:T(8,128)(2,1)S(1)} %get-tuple-element.27.refs_0_.refs_3_.refs_2_, bf16[1552,128]{1,0:T(8,128)(2,1)S(1)} %collective-permute-done.2.refs_1_, bf16[1552,128]{1,0:T(8,128)(2,1)S(1)} %collective-permute-done.refs_2_, bf16[768,128]{1,0:T(8,128)(2,1)S(1)} %collective-permute-done.1.refs_0_.refs_3_, ...), custom_call_target="tpu_custom_call" | custom-call | flops 406847488 | bytes 1986560 | tf_op jit(solution)/shard_map/compare_twin/pallas_call | solution.py:122
  33.2 1.7 %collective-permute-start.18 = (f32[1,1,256]{2,1,0:T(1,128)S(1)}, f32[1,1,256]{2,1,0:T(1,128)S(1)}, u32[]{:S(2)}, u32[]{:S(2)}) collective-permute-start(f32[1,1,256]{2,1,0:T(1,128)S(1)} %compare_twin.1), channel_id=1, source_target_pairs={{0,17},{1,16},{2,19},{3,18},{4,21},{5,20},{6,23},{7,22},{8,25},{9,... | collective-permute-start | bytes 3080 | tf_op jit(solution)/shard_map/ppermute | solution.py:161
  34.9 1.7 %collective-permute-done.15 = f32[1,1,256]{2,1,0:T(1,128)S(1)} collective-permute-done((f32[1,1,256]{2,1,0:T(1,128)S(1)}, f32[1,1,256]{2,1,0:T(1,128)S(1)}, u32[]{:S(2)}, u32[]{:S(2)}) %collective-permute-start.15) | collective-permute-done | bytes 1056 | tf_op jit(solution)/shard_map/ppermute | solution.py:157
  36.6 0.5 %collective-permute-done.18 = f32[1,1,256]{2,1,0:T(1,128)S(1)} collective-permute-done((f32[1,1,256]{2,1,0:T(1,128)S(1)}, f32[1,1,256]{2,1,0:T(1,128)S(1)}, u32[]{:S(2)}, u32[]{:S(2)}) %collective-permute-start.18) | collective-permute-done | bytes 1056 | tf_op jit(solution)/shard_map/ppermute | solution.py:161
  37.2 0.6 %maximum_maximum_fusion = f32[1,1,256]{2,1,0:T(1,128)} fusion(f32[1,1,256]{2,1,0:T(1,128)S(1)} %collective-permute-done.17, f32[1,1,256]{2,1,0:T(1,128)S(1)} %collective-permute-done.11, f32[1,1,256]{2,1,0:T(1,128)S(1)} %collective-permute-done.10, f32[1,1,256]{2,1,0:T(1,128)S(1)} %collective-permute-done.18, f32[1,1,256]{2,1,0:T(1,128)S(1)} %collective-permute-done.15, ...), kind=kLoop, calls=%fused_computation.4 | loop fusion | flops 1792 | bytes 9216 | tf_op jit(solution)/shard_map/max | solution.py:239
  (25 shorter events, 0.6 us)
Async XLA Ops:
  0.0 14.5 %collective-permute-start.7 = (bf16[256,768]{1,0:T(8,128)(2,1)}, bf16[256,768]{1,0:T(8,128)(2,1)S(1)}, u32[]{:S(2)}, u32[]{:S(2)}) collective-permute-start(bf16[256,768]{1,0:T(8,128)(2,1)} %emb_ref.1), channel_id=1, source_target_pairs={{0,8},{8,16},{16,24},{24,0},{1,9},{9,17},{17,25},{25,1},{2,10},{10... | collective-permute-start | bytes 1179656 | tf_op jit(solution)/shard_map/ppermute | solution.py:157
  3.0 0.7 %copy-start.2 = (s32[256]{0:T(256)S(1)}, s32[256]{0:T(256)}, u32[]{:S(2)}) copy-start(s32[256]{0:T(256)} %param.5) | copy-start | bytes 3076
  3.0 0.7 %copy-start.1 = (s32[256,1]{0,1:T(1,128)S(1)}, s32[256,1]{0,1:T(1,128)}, u32[]{:S(2)}) copy-start(s32[256,1]{0,1:T(1,128)} %param.4) | copy-start | bytes 3076
  3.7 1.0 %copy-start = (bf16[256,768]{1,0:T(8,128)(2,1)S(1)}, bf16[256,768]{1,0:T(8,128)(2,1)}, u32[]{:S(2)}) copy-start(bf16[256,768]{1,0:T(8,128)(2,1)} %emb_ref.1) | copy-start | bytes 1179652
  4.9 11.2 %collective-permute-start.2 = (bf16[1552,128]{1,0:T(8,128)(2,1)S(1)}, bf16[1552,128]{1,0:T(8,128)(2,1)S(1)}, u32[]{:S(2)}, u32[]{:S(2)}) collective-permute-start(bf16[1552,128]{1,0:T(8,128)(2,1)S(1)} %get-tuple-element.27.refs_0_.refs_3_.refs_2_), channel_id=1, source_target_pairs={{0,2},{1,3},{2,0},{3,1},{4,6},{5,7},{6,4},{7,5},{8,10},{9,11},{10,... | collective-permute-start | bytes 1191944 | tf_op jit(solution)/shard_map/ppermute | solution.py:151
  6.4 10.4 %collective-permute-start = (bf16[1552,128]{1,0:T(8,128)(2,1)S(1)}, bf16[1552,128]{1,0:T(8,128)(2,1)S(1)}, u32[]{:S(2)}, u32[]{:S(2)}) collective-permute-start(bf16[1552,128]{1,0:T(8,128)(2,1)S(1)} %get-tuple-element.27.refs_0_.refs_3_.refs_2_), channel_id=1, source_target_pairs={{0,4},{1,5},{2,6},{3,7},{4,0},{5,1},{6,2},{7,3},{8,12},{9,13},{10,... | collective-permute-start | bytes 1191944 | tf_op jit(solution)/shard_map/ppermute | solution.py:151
  8.0 6.5 %collective-permute-start.4 = (f32[1,256]{1,0:T(1,128)S(1)}, f32[1,256]{1,0:T(1,128)S(1)}, u32[]{:S(2)}, u32[]{:S(2)}) collective-permute-start(f32[1,256]{1,0:T(1,128)S(1)} %get-tuple-element.25), channel_id=1, source_target_pairs={{0,8},{8,16},{16,24},{24,0},{1,9},{9,17},{17,25},{25,1},{2,10},{10... | collective-permute-start | bytes 3080 | tf_op jit(solution)/shard_map/ppermute | solution.py:157
  9.5 4.9 %collective-permute-start.5 = (f32[1,256]{1,0:T(1,128)S(1)}, f32[1,256]{1,0:T(1,128)S(1)}, u32[]{:S(2)}, u32[]{:S(2)}) collective-permute-start(f32[1,256]{1,0:T(1,128)S(1)} %get-tuple-element.25), channel_id=1, source_target_pairs={{0,16},{8,24},{16,0},{24,8},{1,17},{9,25},{17,1},{25,9},{2,18},{10... | collective-permute-start | bytes 3080 | tf_op jit(solution)/shard_map/ppermute | solution.py:157
  14.5 3.9 %collective-permute-start.6 = (bf16[1552,128]{1,0:T(8,128)(2,1)S(1)}, bf16[1552,128]{1,0:T(8,128)(2,1)S(1)}, u32[]{:S(2)}, u32[]{:S(2)}) collective-permute-start(bf16[1552,128]{1,0:T(8,128)(2,1)S(1)} %get-tuple-element.27.refs_0_.refs_3_.refs_2_), channel_id=1, source_target_pairs={{0,1},{1,0},{2,3},{3,2},{4,5},{5,4},{6,7},{7,6},{8,9},{9,8},{10,11... | collective-permute-start | bytes 1191944 | tf_op jit(solution)/shard_map/ppermute | solution.py:151
  14.5 13.3 %collective-permute-start.14 = (bf16[256,768]{1,0:T(8,128)(2,1)S(1)}, bf16[256,768]{1,0:T(8,128)(2,1)S(1)}, u32[]{:S(2)}, u32[]{:S(2)}) collective-permute-start(bf16[256,768]{1,0:T(8,128)(2,1)S(1)} %collective-permute-done.7.emb_ref), channel_id=1, source_target_pairs={{0,8},{8,16},{16,24},{24,0},{1,9},{9,17},{17,25},{25,1},{2,10},{10... | collective-permute-start | bytes 1179656 | tf_op jit(solution)/shard_map/ppermute | solution.py:157
  15.8 3.3 %collective-permute-start.9 = (bf16[784,128]{1,0:T(8,128)(2,1)S(1)}, bf16[784,128]{1,0:T(8,128)(2,1)S(1)}, u32[]{:S(2)}, u32[]{:S(2)}) collective-permute-start(bf16[784,128]{1,0:T(8,128)(2,1)S(1)} %slice.19), channel_id=1, source_target_pairs={{0,1},{1,0},{2,3},{3,2},{4,5},{5,4},{6,7},{7,6},{8,9},{9,8},{10,11... | collective-permute-start | bytes 602120 | tf_op jit(solution)/shard_map/ppermute | solution.py:151
  16.1 3.0 %collective-permute-start.8 = (bf16[768,128]{1,0:T(8,128)(2,1)S(1)}, bf16[768,128]{1,0:T(8,128)(2,1)S(1)}, u32[]{:S(2)}, u32[]{:S(2)}) collective-permute-start(bf16[768,128]{1,0:T(8,128)(2,1)S(1)} %slice.18), channel_id=1, source_target_pairs={{0,1},{1,0},{2,3},{3,2},{4,5},{5,4},{6,7},{7,6},{8,9},{9,8},{10,11... | collective-permute-start | bytes 589832 | tf_op jit(solution)/shard_map/ppermute | solution.py:151
  16.8 7.6 %collective-permute-start.3 = (bf16[784,128]{1,0:T(8,128)(2,1)S(1)}, bf16[784,128]{1,0:T(8,128)(2,1)S(1)}, u32[]{:S(2)}, u32[]{:S(2)}) collective-permute-start(bf16[784,128]{1,0:T(8,128)(2,1)S(1)} %slice.17), channel_id=1, source_target_pairs={{0,4},{1,5},{2,6},{3,7},{4,0},{5,1},{6,2},{7,3},{8,12},{9,13},{10,... | collective-permute-start | bytes 602120 | tf_op jit(solution)/shard_map/ppermute | solution.py:151
  18.4 6.0 %collective-permute-start.1 = (bf16[768,128]{1,0:T(8,128)(2,1)S(1)}, bf16[768,128]{1,0:T(8,128)(2,1)S(1)}, u32[]{:S(2)}, u32[]{:S(2)}) collective-permute-start(bf16[768,128]{1,0:T(8,128)(2,1)S(1)} %slice.16), channel_id=1, source_target_pairs={{0,2},{1,3},{2,0},{3,1},{4,6},{5,7},{6,4},{7,5},{8,10},{9,11},{10,... | collective-permute-start | bytes 589832 | tf_op jit(solution)/shard_map/ppermute | solution.py:151
  20.6 3.8 %collective-permute-start.10 = (f32[1,1,256]{2,1,0:T(1,128)S(1)}, f32[1,1,256]{2,1,0:T(1,128)S(1)}, u32[]{:S(2)}, u32[]{:S(2)}) collective-permute-start(f32[1,1,256]{2,1,0:T(1,128)S(1)} %get-tuple-element.29), channel_id=1, source_target_pairs={{0,2},{1,3},{2,0},{3,1},{4,6},{5,7},{6,4},{7,5},{8,10},{9,11},{10,... | collective-permute-start | bytes 3080 | tf_op jit(solution)/shard_map/ppermute | solution.py:151
  22.1 3.6 %collective-permute-start.11 = (f32[1,1,256]{2,1,0:T(1,128)S(1)}, f32[1,1,256]{2,1,0:T(1,128)S(1)}, u32[]{:S(2)}, u32[]{:S(2)}) collective-permute-start(f32[1,1,256]{2,1,0:T(1,128)S(1)} %get-tuple-element.34), channel_id=1, source_target_pairs={{0,4},{1,5},{2,6},{3,7},{4,0},{5,1},{6,2},{7,3},{8,12},{9,13},{10,... | collective-permute-start | bytes 3080 | tf_op jit(solution)/shard_map/ppermute | solution.py:151
  25.6 1.2 %collective-permute-start.12 = (f32[2,1,256]{2,1,0:T(1,128)S(1)}, f32[2,1,256]{2,1,0:T(1,128)S(1)}, u32[]{:S(2)}, u32[]{:S(2)}) collective-permute-start(f32[2,1,256]{2,1,0:T(1,128)S(1)} %get-tuple-element.35), channel_id=1, source_target_pairs={{0,1},{1,0},{2,3},{3,2},{4,5},{5,4},{6,7},{7,6},{8,9},{9,8},{10,11... | collective-permute-start | bytes 6152 | tf_op jit(solution)/shard_map/ppermute | solution.py:151
  28.0 4.6 %collective-permute-start.16 = (bf16[1552,128]{1,0:T(8,128)(2,1)S(1)}, bf16[1552,128]{1,0:T(8,128)(2,1)S(1)}, u32[]{:S(2)}, u32[]{:S(2)}) collective-permute-start(bf16[1552,128]{1,0:T(8,128)(2,1)S(1)} %pack.3.refs_5_), channel_id=1, source_target_pairs={{0,1},{1,0},{2,3},{3,2},{4,5},{5,4},{6,7},{7,6},{8,9},{9,8},{10,11... | collective-permute-start | bytes 1191944 | tf_op jit(solution)/shard_map/ppermute | solution.py:151
  28.0 4.5 %collective-permute-start.17 = (f32[1,1,256]{2,1,0:T(1,128)S(1)}, f32[1,1,256]{2,1,0:T(1,128)S(1)}, u32[]{:S(2)}, u32[]{:S(2)}) collective-permute-start(f32[1,1,256]{2,1,0:T(1,128)S(1)} %get-tuple-element.41), channel_id=1, source_target_pairs={{0,6},{1,7},{2,4},{3,5},{4,2},{5,3},{6,0},{7,1},{8,14},{9,15},{10,... | collective-permute-start | bytes 3080 | tf_op jit(solution)/shard_map/ppermute | solution.py:151
  30.6 4.3 %collective-permute-start.13 = (f32[1,1,256]{2,1,0:T(1,128)S(1)}, f32[1,1,256]{2,1,0:T(1,128)S(1)}, u32[]{:S(2)}, u32[]{:S(2)}) collective-permute-start(f32[1,1,256]{2,1,0:T(1,128)S(1)} %bitcast.20), channel_id=1, source_target_pairs={{0,24},{8,0},{16,8},{24,16},{1,25},{9,1},{17,9},{25,17},{2,26},{10... | collective-permute-start | bytes 3080 | tf_op jit(solution)/shard_map/ppermute | solution.py:157
  32.1 4.5 %collective-permute-start.15 = (f32[1,1,256]{2,1,0:T(1,128)S(1)}, f32[1,1,256]{2,1,0:T(1,128)S(1)}, u32[]{:S(2)}, u32[]{:S(2)}) collective-permute-start(f32[1,1,256]{2,1,0:T(1,128)S(1)} %compare_half_way.1), channel_id=1, source_target_pairs={{0,16},{8,24},{16,0},{24,8},{1,17},{9,25},{17,1},{25,9},{2,18},{10... | collective-permute-start | bytes 3080 | tf_op jit(solution)/shard_map/ppermute | solution.py:157
  33.2 4.0 %collective-permute-start.18 = (f32[1,1,256]{2,1,0:T(1,128)S(1)}, f32[1,1,256]{2,1,0:T(1,128)S(1)}, u32[]{:S(2)}, u32[]{:S(2)}) collective-permute-start(f32[1,1,256]{2,1,0:T(1,128)S(1)} %compare_twin.1), channel_id=1, source_target_pairs={{0,17},{1,16},{2,19},{3,18},{4,21},{5,20},{6,23},{7,22},{8,25},{9,... | collective-permute-start | bytes 3080 | tf_op jit(solution)/shard_map/ppermute | solution.py:161

commit v9 on v7

--- a/solution.py
+++ b/solution.py
@@ -225,17 +225,18 @@
     )
     own, one_off_best = join([own, one_off_best], plane_shift(twins, 1))
     found = [own.reshape(1, 1, -1), rows_direct[0]]
-    early += [plane_shift(best, mask) for best, mask in zip(rows_relayed, relayed)]
+    hops = [plane_shift(best, 1 << (mask.bit_length() - 1)) for best, mask in zip(rows_relayed, relayed)]
+    late = [plane_shift(hop, mask ^ (1 << (mask.bit_length() - 1))) for hop, mask in zip(hops, relayed)]
     found.append(grp_shift(one_off_best.reshape(1, 1, -1), -1))
 
     blocks = list(plane.values())
     pairs = [(k, 0, False) for k in range(len(blocks))]
-    half_then = lax.optimization_barrier((half_way, own))[0]
+    half_then = lax.optimization_barrier((half_way, own, hops))[0]
     half_twin = lax.optimization_barrier((plane_shift(half_then, 1), early))[0]
     for name, block, mask in (("compare_half_way", half_way, 0), ("compare_twin", half_twin, 1)):
         (half_best,) = score(name, rows, blocks, [(block,)], pairs, (), [(0,)])
         found.append(grp_shift(half_best, groups // 2, mask))
-    return functools.reduce(jnp.maximum, found + early).reshape(-1)
+    return functools.reduce(jnp.maximum, found + early + late).reshape(-1)
 
 
 def solution(mesh):

time: 38 us -> 40.1 us (1.055)
  waiting for transfers between devices: 10.4 us -> 11.7 us
  starting transfers between devices: 21 us -> 21.8 us
    ppermute x6, starting transfers between devices: 8.35 us -> 10.4 us  [grp_shift(): lax.ppermute(x, 'grp', [(z, (z + shift) % groups) for z in range(groups)])]
    ppermute x12 -> x13, waiting for transfers between devices: 4.58 us -> 6.1 us  [plane_shift(): return lax.ppermute(x, 'blk', [(i, i ^ mask) for i in range(size)])]
    ppermute x12 -> x13, starting transfers between devices: 10.6 us -> 9.18 us  [plane_shift(): return lax.ppermute(x, 'blk', [(i, i ^ mask) for i in range(size)])]
  transfers between devices with their start and end apart: 19 -> 20, of which waited for: 8 -> 9; matrix products, arithmetic and copies ran while one was open for 0% -> 0% of each run, Pallas kernels for 10% -> 10%
where the time goes in v9:
time: 40.1 us; the launch traced here: 39.9 us
  starting transfers between devices  21.8 us (54%)
  waiting for transfers between devices  11.7 us (29%)
  Pallas kernels  3.98 us (10%)
  local copies, waits for them, and re-layouts  1.75 us (4%)
  other arithmetic  0.57 us (1%)
    ppermute x6, starting transfers between devices, grp_shift(): lax.ppermute(x, 'grp', [(z, (z + shift) % groups) for z in range(groups)])  10.4 us
    ppermute x13, starting transfers between devices, plane_shift(): return lax.ppermute(x, 'blk', [(i, i ^ mask) for i in range(size)])  9.18 us
    ppermute x13, waiting for transfers between devices, plane_shift(): return lax.ppermute(x, 'blk', [(i, i ^ mask) for i in range(size)])  6.1 us
    ppermute x6, waiting for transfers between devices, grp_shift(): lax.ppermute(x, 'grp', [(z, (z + shift) % groups) for z in range(groups)])  5.49 us
    pallas_call x4, Pallas kernels, score(): pl.pallas_call(kernel, out_shape=[jax.ShapeDtypeStruct((count, 1, rows),...  3.49 us
    ppermute x1, starting transfers between devices, grp_shift(): return lax.ppermute(x, ('grp', 'blk'), pairs)  2.24 us
    unnamed x6, local copies, waits for them, and re-layouts  1.69 us
  transfers between devices with their start and end apart: 20, of which 9 were waited for; matrix products, arithmetic and copies ran while one was open for 0% of the time, Pallas kernels for 10%

profile of v9, /device:TPU:0, one launch (start us, length us, event | category | flops | bytes accessed | tf_op | source)
XLA Modules:
  0.0 39.9 jit_solution(9453183426916166892)
XLA Ops:
  0.0 3.0 %collective-permute-start.7 = (bf16[256,768]{1,0:T(8,128)(2,1)}, bf16[256,768]{1,0:T(8,128)(2,1)S(1)}, u32[]{:S(2)}, u32[]{:S(2)}) collective-permute-start(bf16[256,768]{1,0:T(8,128)(2,1)} %emb_ref.1), channel_id=1, source_target_pairs={{0,8},{8,16},{16,24},{24,0},{1,9},{9,17},{17,25},{25,1},{2,10},{10... | collective-permute-start | bytes 1179656 | tf_op jit(solution)/shard_map/ppermute | solution.py:157
  3.0 0.7 %copy-done.2 = s32[256]{0:T(256)S(1)} copy-done((s32[256]{0:T(256)S(1)}, s32[256]{0:T(256)}, u32[]{:S(2)}) %copy-start.2) | copy-done | bytes 1048
  3.7 1.0 %copy-done = bf16[256,768]{1,0:T(8,128)(2,1)S(1)} copy-done((bf16[256,768]{1,0:T(8,128)(2,1)S(1)}, bf16[256,768]{1,0:T(8,128)(2,1)}, u32[]{:S(2)}) %copy-start) | copy-done | bytes 393240
  4.7 0.2 pack_own.1
  4.9 1.6 %collective-permute-start.2 = (bf16[1552,128]{1,0:T(8,128)(2,1)S(1)}, bf16[1552,128]{1,0:T(8,128)(2,1)S(1)}, u32[]{:S(2)}, u32[]{:S(2)}) collective-permute-start(bf16[1552,128]{1,0:T(8,128)(2,1)S(1)} %get-tuple-element.26.refs_0_.refs_3_.refs_2_), channel_id=1, source_target_pairs={{0,2},{1,3},{2,0},{3,1},{4,6},{5,7},{6,4},{7,5},{8,10},{9,11},{10,... | collective-permute-start | bytes 1191944 | tf_op jit(solution)/shard_map/ppermute | solution.py:151
  6.4 1.5 %collective-permute-start = (bf16[1552,128]{1,0:T(8,128)(2,1)S(1)}, bf16[1552,128]{1,0:T(8,128)(2,1)S(1)}, u32[]{:S(2)}, u32[]{:S(2)}) collective-permute-start(bf16[1552,128]{1,0:T(8,128)(2,1)S(1)} %get-tuple-element.26.refs_0_.refs_3_.refs_2_), channel_id=1, source_target_pairs={{0,4},{1,5},{2,6},{3,7},{4,0},{5,1},{6,2},{7,3},{8,12},{9,13},{10,... | collective-permute-start | bytes 1191944 | tf_op jit(solution)/shard_map/ppermute | solution.py:151
  8.0 1.6 %collective-permute-start.4 = (f32[1,256]{1,0:T(1,128)S(1)}, f32[1,256]{1,0:T(1,128)S(1)}, u32[]{:S(2)}, u32[]{:S(2)}) collective-permute-start(f32[1,256]{1,0:T(1,128)S(1)} %get-tuple-element.24), channel_id=1, source_target_pairs={{0,8},{8,16},{16,24},{24,0},{1,9},{9,17},{17,25},{25,1},{2,10},{10... | collective-permute-start | bytes 3080 | tf_op jit(solution)/shard_map/ppermute | solution.py:157
  9.5 1.2 %collective-permute-start.5 = (f32[1,256]{1,0:T(1,128)S(1)}, f32[1,256]{1,0:T(1,128)S(1)}, u32[]{:S(2)}, u32[]{:S(2)}) collective-permute-start(f32[1,256]{1,0:T(1,128)S(1)} %get-tuple-element.24), channel_id=1, source_target_pairs={{0,16},{8,24},{16,0},{24,8},{1,17},{9,25},{17,1},{25,9},{2,18},{10... | collective-permute-start | bytes 3080 | tf_op jit(solution)/shard_map/ppermute | solution.py:157
  10.8 3.7 %collective-permute-done.4.key_ref = f32[1,256]{1,0:T(1,128)S(1)} collective-permute-done((f32[1,256]{1,0:T(1,128)S(1)}, f32[1,256]{1,0:T(1,128)S(1)}, u32[]{:S(2)}, u32[]{:S(2)}) %collective-permute-start.4) | collective-permute-done | bytes 1056 | tf_op jit(solution)/shard_map/ppermute | solution.py:157
  14.5 1.1 %collective-permute-start.14 = (bf16[256,768]{1,0:T(8,128)(2,1)S(1)}, bf16[256,768]{1,0:T(8,128)(2,1)S(1)}, u32[]{:S(2)}, u32[]{:S(2)}) collective-permute-start(bf16[256,768]{1,0:T(8,128)(2,1)S(1)} %collective-permute-done.7.emb_ref), channel_id=1, source_target_pairs={{0,8},{8,16},{16,24},{24,0},{1,9},{9,17},{17,25},{25,1},{2,10},{10... | collective-permute-start | bytes 1179656 | tf_op jit(solution)/shard_map/ppermute | solution.py:157
  15.8 0.3 collective-permute-start.9
  16.1 0.3 collective-permute-start.8
  16.5 0.4 collective-permute-done.refs_2_
  16.8 1.5 %collective-permute-start.3 = (bf16[784,128]{1,0:T(8,128)(2,1)S(1)}, bf16[784,128]{1,0:T(8,128)(2,1)S(1)}, u32[]{:S(2)}, u32[]{:S(2)}) collective-permute-start(bf16[784,128]{1,0:T(8,128)(2,1)S(1)} %slice.17), channel_id=1, source_target_pairs={{0,4},{1,5},{2,6},{3,7},{4,0},{5,1},{6,2},{7,3},{8,12},{9,13},{10,... | collective-permute-start | bytes 602120 | tf_op jit(solution)/shard_map/ppermute | solution.py:151
  18.4 0.7 %collective-permute-start.1 = (bf16[768,128]{1,0:T(8,128)(2,1)S(1)}, bf16[768,128]{1,0:T(8,128)(2,1)S(1)}, u32[]{:S(2)}, u32[]{:S(2)}) collective-permute-start(bf16[768,128]{1,0:T(8,128)(2,1)S(1)} %slice.16), channel_id=1, source_target_pairs={{0,2},{1,3},{2,0},{3,1},{4,6},{5,7},{6,4},{7,5},{8,10},{9,11},{10,... | collective-permute-start | bytes 589832 | tf_op jit(solution)/shard_map/ppermute | solution.py:151
  19.1 1.5 %compare_direct.1 = (f32[4,1,256]{2,1,0:T(1,128)S(1)}, f32[1,1,256]{2,1,0:T(1,128)S(1)}, f32[1,1,256]{2,1,0:T(1,128)S(1)}, f32[1,1,256]{2,1,0:T(1,128)S(1)}) custom-call(bf16[1552,128]{1,0:T(8,128)(2,1)S(1)} %get-tuple-element.26.refs_0_.refs_3_.refs_2_, bf16[1552,128]{1,0:T(8,128)(2,1)S(1)} %collective-permute-done.2.refs_1_, ...), custom_call_target="tpu_custom_call" | custom-call | flops 1220542464 | bytes 2781184 | tf_op jit(solution)/shard_map/compare_direct/pallas_call | solution.py:122
  20.6 1.5 %collective-permute-start.10 = (f32[1,1,256]{2,1,0:T(1,128)S(1)}, f32[1,1,256]{2,1,0:T(1,128)S(1)}, u32[]{:S(2)}, u32[]{:S(2)}) collective-permute-start(f32[1,1,256]{2,1,0:T(1,128)S(1)} %get-tuple-element.28), channel_id=1, source_target_pairs={{0,2},{1,3},{2,0},{3,1},{4,6},{5,7},{6,4},{7,5},{8,10},{9,11},{10,... | collective-permute-start | bytes 3080 | tf_op jit(solution)/shard_map/ppermute | solution.py:151
  22.1 0.5 %collective-permute-start.11 = (f32[1,1,256]{2,1,0:T(1,128)S(1)}, f32[1,1,256]{2,1,0:T(1,128)S(1)}, u32[]{:S(2)}, u32[]{:S(2)}) collective-permute-start(f32[1,1,256]{2,1,0:T(1,128)S(1)} %get-tuple-element.29), channel_id=1, source_target_pairs={{0,4},{1,5},{2,6},{3,7},{4,0},{5,1},{6,2},{7,3},{8,12},{9,13},{10,... | collective-permute-start | bytes 3080 | tf_op jit(solution)/shard_map/ppermute | solution.py:151
  22.6 1.8 %collective-permute-done.10 = f32[1,1,256]{2,1,0:T(1,128)S(1)} collective-permute-done((f32[1,1,256]{2,1,0:T(1,128)S(1)}, f32[1,1,256]{2,1,0:T(1,128)S(1)}, u32[]{:S(2)}, u32[]{:S(2)}) %collective-permute-start.10) | collective-permute-done | bytes 1056 | tf_op jit(solution)/shard_map/ppermute | solution.py:151
  24.4 1.2 %collective-permute-done.11 = f32[1,1,256]{2,1,0:T(1,128)S(1)} collective-permute-done((f32[1,1,256]{2,1,0:T(1,128)S(1)}, f32[1,1,256]{2,1,0:T(1,128)S(1)}, u32[]{:S(2)}, u32[]{:S(2)}) %collective-permute-start.11) | collective-permute-done | bytes 1056 | tf_op jit(solution)/shard_map/ppermute | solution.py:151
  25.6 0.7 %compare_relayed.1 = (f32[1,1,256]{2,1,0:T(1,128)S(1)}, f32[1,1,256]{2,1,0:T(1,128)S(1)}, f32[2,1,256]{2,1,0:T(1,128)S(1)}, f32[1,1,256]{2,1,0:T(1,128)S(1)}) custom-call(bf16[768,128]{1,0:T(8,128)(2,1)S(1)} %collective-permute-done.1.refs_0_.refs_3_, bf16[784,128]{1,0:T(8,128)(2,1)S(1)} %collective-permute-done.3.refs_1_.refs_4_, ...), custom_call_target="tpu_custom_call" | custom-call | flops 406847488 | bytes 1986560 | tf_op jit(solution)/shard_map/compare_relayed/pallas_call | solution.py:122
  26.4 0.6 %collective-permute-start.16 = (f32[1,1,256]{2,1,0:T(1,128)S(1)}, f32[1,1,256]{2,1,0:T(1,128)S(1)}, u32[]{:S(2)}, u32[]{:S(2)}) collective-permute-start(f32[1,1,256]{2,1,0:T(1,128)S(1)} %get-tuple-element.38), channel_id=1, source_target_pairs={{0,4},{1,5},{2,6},{3,7},{4,0},{5,1},{6,2},{7,3},{8,12},{9,13},{10,... | collective-permute-start | bytes 3080 | tf_op jit(solution)/shard_map/ppermute | solution.py:151
  27.0 0.6 %collective-permute-done.12.refs_2_ = f32[2,1,256]{2,1,0:T(1,128)S(1)} collective-permute-done((f32[2,1,256]{2,1,0:T(1,128)S(1)}, f32[2,1,256]{2,1,0:T(1,128)S(1)}, u32[]{:S(2)}, u32[]{:S(2)}) %collective-permute-start.12) | collective-permute-done | bytes 2080 | tf_op jit(solution)/shard_map/ppermute | solution.py:151
  27.6 0.2 collective-permute-done.14.emb_ref
  28.0 2.1 %collective-permute-done.16 = f32[1,1,256]{2,1,0:T(1,128)S(1)} collective-permute-done((f32[1,1,256]{2,1,0:T(1,128)S(1)}, f32[1,1,256]{2,1,0:T(1,128)S(1)}, u32[]{:S(2)}, u32[]{:S(2)}) %collective-permute-start.16) | collective-permute-done | bytes 1056 | tf_op jit(solution)/shard_map/ppermute | solution.py:151
  30.1 0.6 %collective-permute-start.19 = (f32[1,1,256]{2,1,0:T(1,128)S(1)}, f32[1,1,256]{2,1,0:T(1,128)S(1)}, u32[]{:S(2)}, u32[]{:S(2)}) collective-permute-start(f32[1,1,256]{2,1,0:T(1,128)S(1)} %collective-permute-done.16), channel_id=1, source_target_pairs={{0,2},{1,3},{2,0},{3,1},{4,6},{5,7},{6,4},{7,5},{8,10},{9,11},{10,... | collective-permute-start | bytes 3080 | tf_op jit(solution)/shard_map/ppermute | solution.py:151
  30.7 3.3 %collective-permute-start.13 = (f32[1,1,256]{2,1,0:T(1,128)S(1)}, f32[1,1,256]{2,1,0:T(1,128)S(1)}, u32[]{:S(2)}, u32[]{:S(2)}) collective-permute-start(f32[1,1,256]{2,1,0:T(1,128)S(1)} %bitcast.20), channel_id=1, source_target_pairs={{0,24},{8,0},{16,8},{24,16},{1,25},{9,1},{17,9},{25,17},{2,26},{10... | collective-permute-start | bytes 3080 | tf_op jit(solution)/shard_map/ppermute | solution.py:157
  34.0 0.6 %compare_half_way.1 = f32[1,1,256]{2,1,0:T(1,128)S(1)} custom-call(bf16[1552,128]{1,0:T(8,128)(2,1)S(1)} %get-tuple-element.26.refs_0_.refs_3_.refs_2_, bf16[1552,128]{1,0:T(8,128)(2,1)S(1)} %collective-permute-done.2.refs_1_, bf16[1552,128]{1,0:T(8,128)(2,1)S(1)} %collective-permute-done.refs_2_, ...), custom_call_target="tpu_custom_call" | custom-call | flops 406847488 | bytes 1986560 | tf_op jit(solution)/shard_map/compare_half_way/pallas_call | solution.py:122
  34.8 0.6 %compare_twin.1 = f32[1,1,256]{2,1,0:T(1,128)S(1)} custom-call(bf16[1552,128]{1,0:T(8,128)(2,1)S(1)} %get-tuple-element.26.refs_0_.refs_3_.refs_2_, bf16[1552,128]{1,0:T(8,128)(2,1)S(1)} %collective-permute-done.2.refs_1_, bf16[1552,128]{1,0:T(8,128)(2,1)S(1)} %collective-permute-done.refs_2_, bf16[768,128]{1,0:T(8,128)(2,1)S(1)} %collective-permute-done.1.refs_0_.refs_3_, ...), custom_call_target="tpu_custom_call" | custom-call | flops 406847488 | bytes 1986560 | tf_op jit(solution)/shard_map/compare_twin/pallas_call | solution.py:122
  35.4 2.2 %collective-permute-start.18 = (f32[1,1,256]{2,1,0:T(1,128)S(1)}, f32[1,1,256]{2,1,0:T(1,128)S(1)}, u32[]{:S(2)}, u32[]{:S(2)}) collective-permute-start(f32[1,1,256]{2,1,0:T(1,128)S(1)} %compare_twin.1), channel_id=1, source_target_pairs={{0,17},{1,16},{2,19},{3,18},{4,21},{5,20},{6,23},{7,22},{8,25},{9,... | collective-permute-start | bytes 3080 | tf_op jit(solution)/shard_map/ppermute | solution.py:161
  37.6 1.6 %collective-permute-done.15 = f32[1,1,256]{2,1,0:T(1,128)S(1)} collective-permute-done((f32[1,1,256]{2,1,0:T(1,128)S(1)}, f32[1,1,256]{2,1,0:T(1,128)S(1)}, u32[]{:S(2)}, u32[]{:S(2)}) %collective-permute-start.15) | collective-permute-done | bytes 1056 | tf_op jit(solution)/shard_map/ppermute | solution.py:157
  39.3 0.6 %maximum_maximum_fusion = f32[1,1,256]{2,1,0:T(1,128)} fusion(f32[1,1,256]{2,1,0:T(1,128)S(1)} %collective-permute-done.19, f32[1,1,256]{2,1,0:T(1,128)S(1)} %collective-permute-done.11, f32[1,1,256]{2,1,0:T(1,128)S(1)} %collective-permute-done.10, f32[1,1,256]{2,1,0:T(1,128)S(1)} %collective-permute-done.18, f32[1,1,256]{2,1,0:T(1,128)S(1)} %collective-permute-done.15, ...), kind=kLoop, calls=%fused_computation.4 | loop fusion | flops 1792 | bytes 9216 | tf_op jit(solution)/shard_map/max | solution.py:239
  (27 shorter events, 0.7 us)
Async XLA Ops:
  0.0 14.5 %collective-permute-start.7 = (bf16[256,768]{1,0:T(8,128)(2,1)}, bf16[256,768]{1,0:T(8,128)(2,1)S(1)}, u32[]{:S(2)}, u32[]{:S(2)}) collective-permute-start(bf16[256,768]{1,0:T(8,128)(2,1)} %emb_ref.1), channel_id=1, source_target_pairs={{0,8},{8,16},{16,24},{24,0},{1,9},{9,17},{17,25},{25,1},{2,10},{10... | collective-permute-start | bytes 1179656 | tf_op jit(solution)/shard_map/ppermute | solution.py:157
  3.0 0.7 %copy-start.2 = (s32[256]{0:T(256)S(1)}, s32[256]{0:T(256)}, u32[]{:S(2)}) copy-start(s32[256]{0:T(256)} %param.5) | copy-start | bytes 3076
  3.0 0.7 %copy-start.1 = (s32[256,1]{0,1:T(1,128)S(1)}, s32[256,1]{0,1:T(1,128)}, u32[]{:S(2)}) copy-start(s32[256,1]{0,1:T(1,128)} %param.4) | copy-start | bytes 3076
  3.7 1.0 %copy-start = (bf16[256,768]{1,0:T(8,128)(2,1)S(1)}, bf16[256,768]{1,0:T(8,128)(2,1)}, u32[]{:S(2)}) copy-start(bf16[256,768]{1,0:T(8,128)(2,1)} %emb_ref.1) | copy-start | bytes 1179652
  4.9 11.2 %collective-permute-start.2 = (bf16[1552,128]{1,0:T(8,128)(2,1)S(1)}, bf16[1552,128]{1,0:T(8,128)(2,1)S(1)}, u32[]{:S(2)}, u32[]{:S(2)}) collective-permute-start(bf16[1552,128]{1,0:T(8,128)(2,1)S(1)} %get-tuple-element.26.refs_0_.refs_3_.refs_2_), channel_id=1, source_target_pairs={{0,2},{1,3},{2,0},{3,1},{4,6},{5,7},{6,4},{7,5},{8,10},{9,11},{10,... | collective-permute-start | bytes 1191944 | tf_op jit(solution)/shard_map/ppermute | solution.py:151
  6.4 10.4 %collective-permute-start = (bf16[1552,128]{1,0:T(8,128)(2,1)S(1)}, bf16[1552,128]{1,0:T(8,128)(2,1)S(1)}, u32[]{:S(2)}, u32[]{:S(2)}) collective-permute-start(bf16[1552,128]{1,0:T(8,128)(2,1)S(1)} %get-tuple-element.26.refs_0_.refs_3_.refs_2_), channel_id=1, source_target_pairs={{0,4},{1,5},{2,6},{3,7},{4,0},{5,1},{6,2},{7,3},{8,12},{9,13},{10,... | collective-permute-start | bytes 1191944 | tf_op jit(solution)/shard_map/ppermute | solution.py:151
  8.0 6.5 %collective-permute-start.4 = (f32[1,256]{1,0:T(1,128)S(1)}, f32[1,256]{1,0:T(1,128)S(1)}, u32[]{:S(2)}, u32[]{:S(2)}) collective-permute-start(f32[1,256]{1,0:T(1,128)S(1)} %get-tuple-element.24), channel_id=1, source_target_pairs={{0,8},{8,16},{16,24},{24,0},{1,9},{9,17},{17,25},{25,1},{2,10},{10... | collective-permute-start | bytes 3080 | tf_op jit(solution)/shard_map/ppermute | solution.py:157
  9.5 4.9 %collective-permute-start.5 = (f32[1,256]{1,0:T(1,128)S(1)}, f32[1,256]{1,0:T(1,128)S(1)}, u32[]{:S(2)}, u32[]{:S(2)}) collective-permute-start(f32[1,256]{1,0:T(1,128)S(1)} %get-tuple-element.24), channel_id=1, source_target_pairs={{0,16},{8,24},{16,0},{24,8},{1,17},{9,25},{17,1},{25,9},{2,18},{10... | collective-permute-start | bytes 3080 | tf_op jit(solution)/shard_map/ppermute | solution.py:157
  14.5 3.9 %collective-permute-start.6 = (bf16[1552,128]{1,0:T(8,128)(2,1)S(1)}, bf16[1552,128]{1,0:T(8,128)(2,1)S(1)}, u32[]{:S(2)}, u32[]{:S(2)}) collective-permute-start(bf16[1552,128]{1,0:T(8,128)(2,1)S(1)} %get-tuple-element.26.refs_0_.refs_3_.refs_2_), channel_id=1, source_target_pairs={{0,1},{1,0},{2,3},{3,2},{4,5},{5,4},{6,7},{7,6},{8,9},{9,8},{10,11... | collective-permute-start | bytes 1191944 | tf_op jit(solution)/shard_map/ppermute | solution.py:151
  14.5 13.3 %collective-permute-start.14 = (bf16[256,768]{1,0:T(8,128)(2,1)S(1)}, bf16[256,768]{1,0:T(8,128)(2,1)S(1)}, u32[]{:S(2)}, u32[]{:S(2)}) collective-permute-start(bf16[256,768]{1,0:T(8,128)(2,1)S(1)} %collective-permute-done.7.emb_ref), channel_id=1, source_target_pairs={{0,8},{8,16},{16,24},{24,0},{1,9},{9,17},{17,25},{25,1},{2,10},{10... | collective-permute-start | bytes 1179656 | tf_op jit(solution)/shard_map/ppermute | solution.py:157
  15.8 3.3 %collective-permute-start.9 = (bf16[784,128]{1,0:T(8,128)(2,1)S(1)}, bf16[784,128]{1,0:T(8,128)(2,1)S(1)}, u32[]{:S(2)}, u32[]{:S(2)}) collective-permute-start(bf16[784,128]{1,0:T(8,128)(2,1)S(1)} %slice.19), channel_id=1, source_target_pairs={{0,1},{1,0},{2,3},{3,2},{4,5},{5,4},{6,7},{7,6},{8,9},{9,8},{10,11... | collective-permute-start | bytes 602120 | tf_op jit(solution)/shard_map/ppermute | solution.py:151
  16.1 3.0 %collective-permute-start.8 = (bf16[768,128]{1,0:T(8,128)(2,1)S(1)}, bf16[768,128]{1,0:T(8,128)(2,1)S(1)}, u32[]{:S(2)}, u32[]{:S(2)}) collective-permute-start(bf16[768,128]{1,0:T(8,128)(2,1)S(1)} %slice.18), channel_id=1, source_target_pairs={{0,1},{1,0},{2,3},{3,2},{4,5},{5,4},{6,7},{7,6},{8,9},{9,8},{10,11... | collective-permute-start | bytes 589832 | tf_op jit(solution)/shard_map/ppermute | solution.py:151
  16.8 8.8 %collective-permute-start.3 = (bf16[784,128]{1,0:T(8,128)(2,1)S(1)}, bf16[784,128]{1,0:T(8,128)(2,1)S(1)}, u32[]{:S(2)}, u32[]{:S(2)}) collective-permute-start(bf16[784,128]{1,0:T(8,128)(2,1)S(1)} %slice.17), channel_id=1, source_target_pairs={{0,4},{1,5},{2,6},{3,7},{4,0},{5,1},{6,2},{7,3},{8,12},{9,13},{10,... | collective-permute-start | bytes 602120 | tf_op jit(solution)/shard_map/ppermute | solution.py:151
  18.4 7.3 %collective-permute-start.1 = (bf16[768,128]{1,0:T(8,128)(2,1)S(1)}, bf16[768,128]{1,0:T(8,128)(2,1)S(1)}, u32[]{:S(2)}, u32[]{:S(2)}) collective-permute-start(bf16[768,128]{1,0:T(8,128)(2,1)S(1)} %slice.16), channel_id=1, source_target_pairs={{0,2},{1,3},{2,0},{3,1},{4,6},{5,7},{6,4},{7,5},{8,10},{9,11},{10,... | collective-permute-start | bytes 589832 | tf_op jit(solution)/shard_map/ppermute | solution.py:151
  20.6 3.8 %collective-permute-start.10 = (f32[1,1,256]{2,1,0:T(1,128)S(1)}, f32[1,1,256]{2,1,0:T(1,128)S(1)}, u32[]{:S(2)}, u32[]{:S(2)}) collective-permute-start(f32[1,1,256]{2,1,0:T(1,128)S(1)} %get-tuple-element.28), channel_id=1, source_target_pairs={{0,2},{1,3},{2,0},{3,1},{4,6},{5,7},{6,4},{7,5},{8,10},{9,11},{10,... | collective-permute-start | bytes 3080 | tf_op jit(solution)/shard_map/ppermute | solution.py:151
  22.1 3.6 %collective-permute-start.11 = (f32[1,1,256]{2,1,0:T(1,128)S(1)}, f32[1,1,256]{2,1,0:T(1,128)S(1)}, u32[]{:S(2)}, u32[]{:S(2)}) collective-permute-start(f32[1,1,256]{2,1,0:T(1,128)S(1)} %get-tuple-element.29), channel_id=1, source_target_pairs={{0,4},{1,5},{2,6},{3,7},{4,0},{5,1},{6,2},{7,3},{8,12},{9,13},{10,... | collective-permute-start | bytes 3080 | tf_op jit(solution)/shard_map/ppermute | solution.py:151
  26.3 1.2 %collective-permute-start.12 = (f32[2,1,256]{2,1,0:T(1,128)S(1)}, f32[2,1,256]{2,1,0:T(1,128)S(1)}, u32[]{:S(2)}, u32[]{:S(2)}) collective-permute-start(f32[2,1,256]{2,1,0:T(1,128)S(1)} %get-tuple-element.33), channel_id=1, source_target_pairs={{0,1},{1,0},{2,3},{3,2},{4,5},{5,4},{6,7},{7,6},{8,9},{9,8},{10,11... | collective-permute-start | bytes 6152 | tf_op jit(solution)/shard_map/ppermute | solution.py:151
  26.4 3.6 %collective-permute-start.16 = (f32[1,1,256]{2,1,0:T(1,128)S(1)}, f32[1,1,256]{2,1,0:T(1,128)S(1)}, u32[]{:S(2)}, u32[]{:S(2)}) collective-permute-start(f32[1,1,256]{2,1,0:T(1,128)S(1)} %get-tuple-element.38), channel_id=1, source_target_pairs={{0,4},{1,5},{2,6},{3,7},{4,0},{5,1},{6,2},{7,3},{8,12},{9,13},{10,... | collective-permute-start | bytes 3080 | tf_op jit(solution)/shard_map/ppermute | solution.py:151
  30.1 4.7 %collective-permute-start.17 = (bf16[1552,128]{1,0:T(8,128)(2,1)S(1)}, bf16[1552,128]{1,0:T(8,128)(2,1)S(1)}, u32[]{:S(2)}, u32[]{:S(2)}) collective-permute-start(bf16[1552,128]{1,0:T(8,128)(2,1)S(1)} %pack.3.refs_5_), channel_id=1, source_target_pairs={{0,1},{1,0},{2,3},{3,2},{4,5},{5,4},{6,7},{7,6},{8,9},{9,8},{10,11... | collective-permute-start | bytes 1191944 | tf_op jit(solution)/shard_map/ppermute | solution.py:151
  30.1 7.6 %collective-permute-start.19 = (f32[1,1,256]{2,1,0:T(1,128)S(1)}, f32[1,1,256]{2,1,0:T(1,128)S(1)}, u32[]{:S(2)}, u32[]{:S(2)}) collective-permute-start(f32[1,1,256]{2,1,0:T(1,128)S(1)} %collective-permute-done.16), channel_id=1, source_target_pairs={{0,2},{1,3},{2,0},{3,1},{4,6},{5,7},{6,4},{7,5},{8,10},{9,11},{10,... | collective-permute-start | bytes 3080 | tf_op jit(solution)/shard_map/ppermute | solution.py:151
  30.7 6.9 %collective-permute-start.13 = (f32[1,1,256]{2,1,0:T(1,128)S(1)}, f32[1,1,256]{2,1,0:T(1,128)S(1)}, u32[]{:S(2)}, u32[]{:S(2)}) collective-permute-start(f32[1,1,256]{2,1,0:T(1,128)S(1)} %bitcast.20), channel_id=1, source_target_pairs={{0,24},{8,0},{16,8},{24,16},{1,25},{9,1},{17,9},{25,17},{2,26},{10... | collective-permute-start | bytes 3080 | tf_op jit(solution)/shard_map/ppermute | solution.py:157
  34.7 4.5 %collective-permute-start.15 = (f32[1,1,256]{2,1,0:T(1,128)S(1)}, f32[1,1,256]{2,1,0:T(1,128)S(1)}, u32[]{:S(2)}, u32[]{:S(2)}) collective-permute-start(f32[1,1,256]{2,1,0:T(1,128)S(1)} %compare_half_way.1), channel_id=1, source_target_pairs={{0,16},{8,24},{16,0},{24,8},{1,17},{9,25},{17,1},{25,9},{2,18},{10... | collective-permute-start | bytes 3080 | tf_op jit(solution)/shard_map/ppermute | solution.py:157
  35.4 4.0 %collective-permute-start.18 = (f32[1,1,256]{2,1,0:T(1,128)S(1)}, f32[1,1,256]{2,1,0:T(1,128)S(1)}, u32[]{:S(2)}, u32[]{:S(2)}) collective-permute-start(f32[1,1,256]{2,1,0:T(1,128)S(1)} %compare_twin.1), channel_id=1, source_target_pairs={{0,17},{1,16},{2,19},{3,18},{4,21},{5,20},{6,23},{7,22},{8,25},{9,... | collective-permute-start | bytes 3080 | tf_op jit(solution)/shard_map/ppermute | solution.py:161

commit v10 on v8

--- a/solution.py
+++ b/solution.py
@@ -232,9 +232,10 @@
     blocks = list(plane.values())
     pairs = [(k, 0, False) for k in range(len(blocks))]
     half_then = lax.optimization_barrier((half_way, own))[0]
-    half_twin = lax.optimization_barrier((plane_shift(half_then, 1), early))[0]
-    for name, block, mask in (("compare_half_way", half_way, 0), ("compare_twin", half_twin, 1)):
-        (half_best,) = score(name, rows, blocks, [(block,)], pairs, (), [(0,)])
+    half_twin = [plane_shift(piece, 1) for piece in cut(half_then, rows)]
+    half_twin = lax.optimization_barrier((half_twin, early))[0]
+    for name, block, mask in (("compare_half_way", [half_way], 0), ("compare_twin", half_twin, 1)):
+        (half_best,) = score(name, rows, blocks, [block], pairs, (), [(0,)])
         found.append(grp_shift(half_best, groups // 2, mask))
     return functools.reduce(jnp.maximum, found + early).reshape(-1)
 

time: 37.9 us -> 38.5 us (1.016)
    ppermute x12 -> x13, starting transfers between devices: 10.5 us -> 11 us  [plane_shift(): return lax.ppermute(x, 'blk', [(i, i ^ mask) for i in range(size)])]
    ppermute x12 -> x13, waiting for transfers between devices: 4.28 us -> 4.38 us  [plane_shift(): return lax.ppermute(x, 'blk', [(i, i ^ mask) for i in range(size)])]
  transfers between devices with their start and end apart: 19 -> 20, of which waited for: 9 -> 9; matrix products, arithmetic and copies ran while one was open for 0% -> 0% of each run, Pallas kernels for 10% -> 10%
where the time goes in v10:
time: 38.5 us; the launch traced here: 38.3 us
  starting transfers between devices  20.2 us (52%)
  waiting for transfers between devices  11.6 us (30%)
  Pallas kernels  3.98 us (10%)
  local copies, waits for them, and re-layouts  1.78 us (5%)
  other arithmetic  0.57 us (1%)
    ppermute x13, starting transfers between devices, plane_shift(): return lax.ppermute(x, 'blk', [(i, i ^ mask) for i in range(size)])  11 us
    ppermute x6, starting transfers between devices, grp_shift(): lax.ppermute(x, 'grp', [(z, (z + shift) % groups) for z in range(groups)])  7.83 us
    ppermute x6, waiting for transfers between devices, grp_shift(): lax.ppermute(x, 'grp', [(z, (z + shift) % groups) for z in range(groups)])  6.6 us
    ppermute x13, waiting for transfers between devices, plane_shift(): return lax.ppermute(x, 'blk', [(i, i ^ mask) for i in range(size)])  4.38 us
    pallas_call x4, Pallas kernels, score(): pl.pallas_call(kernel, out_shape=[jax.ShapeDtypeStruct((count, 1, rows),...  3.49 us
    unnamed x6, local copies, waits for them, and re-layouts  1.69 us
    ppermute x1, starting transfers between devices, grp_shift(): return lax.ppermute(x, ('grp', 'blk'), pairs)  1.42 us
  transfers between devices with their start and end apart: 20, of which 9 were waited for; matrix products, arithmetic and copies ran while one was open for 0% of the time, Pallas kernels for 10%

profile of v10, /device:TPU:0, one launch (start us, length us, event | category | flops | bytes accessed | tf_op | source)
XLA Modules:
  0.0 38.3 jit_solution(7410088622045312366)
XLA Ops:
  0.0 3.0 %collective-permute-start.7 = (bf16[256,768]{1,0:T(8,128)(2,1)}, bf16[256,768]{1,0:T(8,128)(2,1)S(1)}, u32[]{:S(2)}, u32[]{:S(2)}) collective-permute-start(bf16[256,768]{1,0:T(8,128)(2,1)} %emb_ref.1), channel_id=1, source_target_pairs={{0,8},{8,16},{16,24},{24,0},{1,9},{9,17},{17,25},{25,1},{2,10},{10... | collective-permute-start | bytes 1179656 | tf_op jit(solution)/shard_map/ppermute | solution.py:157
  3.0 0.7 %copy-done.2 = s32[256]{0:T(256)S(1)} copy-done((s32[256]{0:T(256)S(1)}, s32[256]{0:T(256)}, u32[]{:S(2)}) %copy-start.2) | copy-done | bytes 1048
  3.7 1.0 %copy-done = bf16[256,768]{1,0:T(8,128)(2,1)S(1)} copy-done((bf16[256,768]{1,0:T(8,128)(2,1)S(1)}, bf16[256,768]{1,0:T(8,128)(2,1)}, u32[]{:S(2)}) %copy-start) | copy-done | bytes 393240
  4.9 1.6 %collective-permute-start.2 = (bf16[1552,128]{1,0:T(8,128)(2,1)S(1)}, bf16[1552,128]{1,0:T(8,128)(2,1)S(1)}, u32[]{:S(2)}, u32[]{:S(2)}) collective-permute-start(bf16[1552,128]{1,0:T(8,128)(2,1)S(1)} %get-tuple-element.28.refs_0_.refs_3_.refs_2_), channel_id=1, source_target_pairs={{0,2},{1,3},{2,0},{3,1},{4,6},{5,7},{6,4},{7,5},{8,10},{9,11},{10,... | collective-permute-start | bytes 1191944 | tf_op jit(solution)/shard_map/ppermute | solution.py:151
  6.4 1.5 %collective-permute-start = (bf16[1552,128]{1,0:T(8,128)(2,1)S(1)}, bf16[1552,128]{1,0:T(8,128)(2,1)S(1)}, u32[]{:S(2)}, u32[]{:S(2)}) collective-permute-start(bf16[1552,128]{1,0:T(8,128)(2,1)S(1)} %get-tuple-element.28.refs_0_.refs_3_.refs_2_), channel_id=1, source_target_pairs={{0,4},{1,5},{2,6},{3,7},{4,0},{5,1},{6,2},{7,3},{8,12},{9,13},{10,... | collective-permute-start | bytes 1191944 | tf_op jit(solution)/shard_map/ppermute | solution.py:151
  8.0 1.6 %collective-permute-start.4 = (f32[1,256]{1,0:T(1,128)S(1)}, f32[1,256]{1,0:T(1,128)S(1)}, u32[]{:S(2)}, u32[]{:S(2)}) collective-permute-start(f32[1,256]{1,0:T(1,128)S(1)} %get-tuple-element.26), channel_id=1, source_target_pairs={{0,8},{8,16},{16,24},{24,0},{1,9},{9,17},{17,25},{25,1},{2,10},{10... | collective-permute-start | bytes 3080 | tf_op jit(solution)/shard_map/ppermute | solution.py:157
  9.5 1.2 %collective-permute-start.5 = (f32[1,256]{1,0:T(1,128)S(1)}, f32[1,256]{1,0:T(1,128)S(1)}, u32[]{:S(2)}, u32[]{:S(2)}) collective-permute-start(f32[1,256]{1,0:T(1,128)S(1)} %get-tuple-element.26), channel_id=1, source_target_pairs={{0,16},{8,24},{16,0},{24,8},{1,17},{9,25},{17,1},{25,9},{2,18},{10... | collective-permute-start | bytes 3080 | tf_op jit(solution)/shard_map/ppermute | solution.py:157
  10.8 3.7 %collective-permute-done.4.key_ref = f32[1,256]{1,0:T(1,128)S(1)} collective-permute-done((f32[1,256]{1,0:T(1,128)S(1)}, f32[1,256]{1,0:T(1,128)S(1)}, u32[]{:S(2)}, u32[]{:S(2)}) %collective-permute-start.4) | collective-permute-done | bytes 1056 | tf_op jit(solution)/shard_map/ppermute | solution.py:157
  14.5 1.1 %collective-permute-start.14 = (bf16[256,768]{1,0:T(8,128)(2,1)S(1)}, bf16[256,768]{1,0:T(8,128)(2,1)S(1)}, u32[]{:S(2)}, u32[]{:S(2)}) collective-permute-start(bf16[256,768]{1,0:T(8,128)(2,1)S(1)} %collective-permute-done.7.emb_ref), channel_id=1, source_target_pairs={{0,8},{8,16},{16,24},{24,0},{1,9},{9,17},{17,25},{25,1},{2,10},{10... | collective-permute-start | bytes 1179656 | tf_op jit(solution)/shard_map/ppermute | solution.py:157
  15.8 0.3 collective-permute-start.9
  16.1 0.3 collective-permute-start.8
  16.5 0.4 collective-permute-done.refs_2_
  16.8 1.5 %collective-permute-start.3 = (bf16[784,128]{1,0:T(8,128)(2,1)S(1)}, bf16[784,128]{1,0:T(8,128)(2,1)S(1)}, u32[]{:S(2)}, u32[]{:S(2)}) collective-permute-start(bf16[784,128]{1,0:T(8,128)(2,1)S(1)} %slice.25), channel_id=1, source_target_pairs={{0,4},{1,5},{2,6},{3,7},{4,0},{5,1},{6,2},{7,3},{8,12},{9,13},{10,... | collective-permute-start | bytes 602120 | tf_op jit(solution)/shard_map/ppermute | solution.py:151
  18.4 0.7 %collective-permute-start.1 = (bf16[768,128]{1,0:T(8,128)(2,1)S(1)}, bf16[768,128]{1,0:T(8,128)(2,1)S(1)}, u32[]{:S(2)}, u32[]{:S(2)}) collective-permute-start(bf16[768,128]{1,0:T(8,128)(2,1)S(1)} %slice.24), channel_id=1, source_target_pairs={{0,2},{1,3},{2,0},{3,1},{4,6},{5,7},{6,4},{7,5},{8,10},{9,11},{10,... | collective-permute-start | bytes 589832 | tf_op jit(solution)/shard_map/ppermute | solution.py:151
  19.1 1.5 %compare_direct.1 = (f32[4,1,256]{2,1,0:T(1,128)S(1)}, f32[1,1,256]{2,1,0:T(1,128)S(1)}, f32[1,1,256]{2,1,0:T(1,128)S(1)}, f32[1,1,256]{2,1,0:T(1,128)S(1)}) custom-call(bf16[1552,128]{1,0:T(8,128)(2,1)S(1)} %get-tuple-element.28.refs_0_.refs_3_.refs_2_, bf16[1552,128]{1,0:T(8,128)(2,1)S(1)} %collective-permute-done.2.refs_1_, ...), custom_call_target="tpu_custom_call" | custom-call | flops 1220542464 | bytes 2781184 | tf_op jit(solution)/shard_map/compare_direct/pallas_call | solution.py:122
  20.6 1.5 %collective-permute-start.10 = (f32[1,1,256]{2,1,0:T(1,128)S(1)}, f32[1,1,256]{2,1,0:T(1,128)S(1)}, u32[]{:S(2)}, u32[]{:S(2)}) collective-permute-start(f32[1,1,256]{2,1,0:T(1,128)S(1)} %get-tuple-element.30), channel_id=1, source_target_pairs={{0,2},{1,3},{2,0},{3,1},{4,6},{5,7},{6,4},{7,5},{8,10},{9,11},{10,... | collective-permute-start | bytes 3080 | tf_op jit(solution)/shard_map/ppermute | solution.py:151
  22.1 0.5 %collective-permute-start.11 = (f32[1,1,256]{2,1,0:T(1,128)S(1)}, f32[1,1,256]{2,1,0:T(1,128)S(1)}, u32[]{:S(2)}, u32[]{:S(2)}) collective-permute-start(f32[1,1,256]{2,1,0:T(1,128)S(1)} %get-tuple-element.35), channel_id=1, source_target_pairs={{0,4},{1,5},{2,6},{3,7},{4,0},{5,1},{6,2},{7,3},{8,12},{9,13},{10,... | collective-permute-start | bytes 3080 | tf_op jit(solution)/shard_map/ppermute | solution.py:151
  22.6 1.8 %collective-permute-done.10 = f32[1,1,256]{2,1,0:T(1,128)S(1)} collective-permute-done((f32[1,1,256]{2,1,0:T(1,128)S(1)}, f32[1,1,256]{2,1,0:T(1,128)S(1)}, u32[]{:S(2)}, u32[]{:S(2)}) %collective-permute-start.10) | collective-permute-done | bytes 1056 | tf_op jit(solution)/shard_map/ppermute | solution.py:151
  24.4 0.7 %compare_relayed.1 = (f32[1,1,256]{2,1,0:T(1,128)S(1)}, f32[1,1,256]{2,1,0:T(1,128)S(1)}, f32[2,1,256]{2,1,0:T(1,128)S(1)}, f32[1,1,256]{2,1,0:T(1,128)S(1)}) custom-call(bf16[768,128]{1,0:T(8,128)(2,1)S(1)} %collective-permute-done.1.refs_0_.refs_3_, bf16[784,128]{1,0:T(8,128)(2,1)S(1)} %collective-permute-done.3.refs_1_.refs_4_, ...), custom_call_target="tpu_custom_call" | custom-call | flops 406847488 | bytes 1986560 | tf_op jit(solution)/shard_map/compare_relayed/pallas_call | solution.py:122
  25.1 0.5 %collective-permute-done.11 = f32[1,1,256]{2,1,0:T(1,128)S(1)} collective-permute-done((f32[1,1,256]{2,1,0:T(1,128)S(1)}, f32[1,1,256]{2,1,0:T(1,128)S(1)}, u32[]{:S(2)}, u32[]{:S(2)}) %collective-permute-start.11) | collective-permute-done | bytes 1056 | tf_op jit(solution)/shard_map/ppermute | solution.py:151
  25.6 1.2 %collective-permute-done.12.refs_2_ = f32[2,1,256]{2,1,0:T(1,128)S(1)} collective-permute-done((f32[2,1,256]{2,1,0:T(1,128)S(1)}, f32[2,1,256]{2,1,0:T(1,128)S(1)}, u32[]{:S(2)}, u32[]{:S(2)}) %collective-permute-start.12) | collective-permute-done | bytes 2080 | tf_op jit(solution)/shard_map/ppermute | solution.py:151
  26.8 1.0 %collective-permute-done.14.emb_ref = bf16[256,768]{1,0:T(8,128)(2,1)S(1)} collective-permute-done((bf16[256,768]{1,0:T(8,128)(2,1)S(1)}, bf16[256,768]{1,0:T(8,128)(2,1)S(1)}, u32[]{:S(2)}, u32[]{:S(2)}) %collective-permute-start.14) | collective-permute-done | bytes 393248 | tf_op jit(solution)/shard_map/ppermute | solution.py:157
  28.1 0.6 %collective-permute-start.16 = (bf16[768,128]{1,0:T(8,128)(2,1)S(1)}, bf16[768,128]{1,0:T(8,128)(2,1)S(1)}, u32[]{:S(2)}, u32[]{:S(2)}) collective-permute-start(bf16[768,128]{1,0:T(8,128)(2,1)S(1)} %slice.22), channel_id=1, source_target_pairs={{0,1},{1,0},{2,3},{3,2},{4,5},{5,4},{6,7},{7,6},{8,9},{9,8},{10,11... | collective-permute-start | bytes 589832 | tf_op jit(solution)/shard_map/ppermute | solution.py:151
  28.6 2.4 %collective-permute-start.18 = (f32[1,1,256]{2,1,0:T(1,128)S(1)}, f32[1,1,256]{2,1,0:T(1,128)S(1)}, u32[]{:S(2)}, u32[]{:S(2)}) collective-permute-start(f32[1,1,256]{2,1,0:T(1,128)S(1)} %get-tuple-element.42), channel_id=1, source_target_pairs={{0,6},{1,7},{2,4},{3,5},{4,2},{5,3},{6,0},{7,1},{8,14},{9,15},{10,... | collective-permute-start | bytes 3080 | tf_op jit(solution)/shard_map/ppermute | solution.py:151
  31.1 0.8 %collective-permute-start.13 = (f32[1,1,256]{2,1,0:T(1,128)S(1)}, f32[1,1,256]{2,1,0:T(1,128)S(1)}, u32[]{:S(2)}, u32[]{:S(2)}) collective-permute-start(f32[1,1,256]{2,1,0:T(1,128)S(1)} %bitcast.20), channel_id=1, source_target_pairs={{0,24},{8,0},{16,8},{24,16},{1,25},{9,1},{17,9},{25,17},{2,26},{10... | collective-permute-start | bytes 3080 | tf_op jit(solution)/shard_map/ppermute | solution.py:157
  31.9 0.6 %compare_half_way.1 = f32[1,1,256]{2,1,0:T(1,128)S(1)} custom-call(bf16[1552,128]{1,0:T(8,128)(2,1)S(1)} %get-tuple-element.28.refs_0_.refs_3_.refs_2_, bf16[1552,128]{1,0:T(8,128)(2,1)S(1)} %collective-permute-done.2.refs_1_, bf16[1552,128]{1,0:T(8,128)(2,1)S(1)} %collective-permute-done.refs_2_, ...), custom_call_target="tpu_custom_call" | custom-call | flops 406847488 | bytes 1986560 | tf_op jit(solution)/shard_map/compare_half_way/pallas_call | solution.py:122
  32.6 0.5 %collective-permute-done.18 = f32[1,1,256]{2,1,0:T(1,128)S(1)} collective-permute-done((f32[1,1,256]{2,1,0:T(1,128)S(1)}, f32[1,1,256]{2,1,0:T(1,128)S(1)}, u32[]{:S(2)}, u32[]{:S(2)}) %collective-permute-start.18) | collective-permute-done | bytes 1056 | tf_op jit(solution)/shard_map/ppermute | solution.py:151
  33.1 0.6 %compare_twin.1 = f32[1,1,256]{2,1,0:T(1,128)S(1)} custom-call(bf16[1552,128]{1,0:T(8,128)(2,1)S(1)} %get-tuple-element.28.refs_0_.refs_3_.refs_2_, bf16[1552,128]{1,0:T(8,128)(2,1)S(1)} %collective-permute-done.2.refs_1_, bf16[1552,128]{1,0:T(8,128)(2,1)S(1)} %collective-permute-done.refs_2_, bf16[768,128]{1,0:T(8,128)(2,1)S(1)} %collective-permute-done.1.refs_0_.refs_3_, ...), custom_call_target="tpu_custom_call" | custom-call | flops 406847488 | bytes 1986560 | tf_op jit(solution)/shard_map/compare_twin/pallas_call | solution.py:122
  33.8 1.4 %collective-permute-start.19 = (f32[1,1,256]{2,1,0:T(1,128)S(1)}, f32[1,1,256]{2,1,0:T(1,128)S(1)}, u32[]{:S(2)}, u32[]{:S(2)}) collective-permute-start(f32[1,1,256]{2,1,0:T(1,128)S(1)} %compare_twin.1), channel_id=1, source_target_pairs={{0,17},{1,16},{2,19},{3,18},{4,21},{5,20},{6,23},{7,22},{8,25},{9,... | collective-permute-start | bytes 3080 | tf_op jit(solution)/shard_map/ppermute | solution.py:161
  35.2 1.9 %collective-permute-done.15 = f32[1,1,256]{2,1,0:T(1,128)S(1)} collective-permute-done((f32[1,1,256]{2,1,0:T(1,128)S(1)}, f32[1,1,256]{2,1,0:T(1,128)S(1)}, u32[]{:S(2)}, u32[]{:S(2)}) %collective-permute-start.15) | collective-permute-done | bytes 1056 | tf_op jit(solution)/shard_map/ppermute | solution.py:157
  37.1 0.6 %collective-permute-done.19 = f32[1,1,256]{2,1,0:T(1,128)S(1)} collective-permute-done((f32[1,1,256]{2,1,0:T(1,128)S(1)}, f32[1,1,256]{2,1,0:T(1,128)S(1)}, u32[]{:S(2)}, u32[]{:S(2)}) %collective-permute-start.19) | collective-permute-done | bytes 1056 | tf_op jit(solution)/shard_map/ppermute | solution.py:161
  37.7 0.6 %maximum_maximum_fusion = f32[1,1,256]{2,1,0:T(1,128)} fusion(f32[1,1,256]{2,1,0:T(1,128)S(1)} %collective-permute-done.18, f32[1,1,256]{2,1,0:T(1,128)S(1)} %collective-permute-done.11, f32[1,1,256]{2,1,0:T(1,128)S(1)} %collective-permute-done.10, f32[1,1,256]{2,1,0:T(1,128)S(1)} %collective-permute-done.19, f32[1,1,256]{2,1,0:T(1,128)S(1)} %collective-permute-done.15, ...), kind=kLoop, calls=%fused_computation.4 | loop fusion | flops 1792 | bytes 9216 | tf_op jit(solution)/shard_map/max | solution.py:240
  (29 shorter events, 0.8 us)
Async XLA Ops:
  0.0 14.5 %collective-permute-start.7 = (bf16[256,768]{1,0:T(8,128)(2,1)}, bf16[256,768]{1,0:T(8,128)(2,1)S(1)}, u32[]{:S(2)}, u32[]{:S(2)}) collective-permute-start(bf16[256,768]{1,0:T(8,128)(2,1)} %emb_ref.1), channel_id=1, source_target_pairs={{0,8},{8,16},{16,24},{24,0},{1,9},{9,17},{17,25},{25,1},{2,10},{10... | collective-permute-start | bytes 1179656 | tf_op jit(solution)/shard_map/ppermute | solution.py:157
  3.0 0.7 %copy-start.2 = (s32[256]{0:T(256)S(1)}, s32[256]{0:T(256)}, u32[]{:S(2)}) copy-start(s32[256]{0:T(256)} %param.5) | copy-start | bytes 3076
  3.0 0.7 %copy-start.1 = (s32[256,1]{0,1:T(1,128)S(1)}, s32[256,1]{0,1:T(1,128)}, u32[]{:S(2)}) copy-start(s32[256,1]{0,1:T(1,128)} %param.4) | copy-start | bytes 3076
  3.7 1.0 %copy-start = (bf16[256,768]{1,0:T(8,128)(2,1)S(1)}, bf16[256,768]{1,0:T(8,128)(2,1)}, u32[]{:S(2)}) copy-start(bf16[256,768]{1,0:T(8,128)(2,1)} %emb_ref.1) | copy-start | bytes 1179652
  4.9 11.2 %collective-permute-start.2 = (bf16[1552,128]{1,0:T(8,128)(2,1)S(1)}, bf16[1552,128]{1,0:T(8,128)(2,1)S(1)}, u32[]{:S(2)}, u32[]{:S(2)}) collective-permute-start(bf16[1552,128]{1,0:T(8,128)(2,1)S(1)} %get-tuple-element.28.refs_0_.refs_3_.refs_2_), channel_id=1, source_target_pairs={{0,2},{1,3},{2,0},{3,1},{4,6},{5,7},{6,4},{7,5},{8,10},{9,11},{10,... | collective-permute-start | bytes 1191944 | tf_op jit(solution)/shard_map/ppermute | solution.py:151
  6.4 10.4 %collective-permute-start = (bf16[1552,128]{1,0:T(8,128)(2,1)S(1)}, bf16[1552,128]{1,0:T(8,128)(2,1)S(1)}, u32[]{:S(2)}, u32[]{:S(2)}) collective-permute-start(bf16[1552,128]{1,0:T(8,128)(2,1)S(1)} %get-tuple-element.28.refs_0_.refs_3_.refs_2_), channel_id=1, source_target_pairs={{0,4},{1,5},{2,6},{3,7},{4,0},{5,1},{6,2},{7,3},{8,12},{9,13},{10,... | collective-permute-start | bytes 1191944 | tf_op jit(solution)/shard_map/ppermute | solution.py:151
  8.0 6.5 %collective-permute-start.4 = (f32[1,256]{1,0:T(1,128)S(1)}, f32[1,256]{1,0:T(1,128)S(1)}, u32[]{:S(2)}, u32[]{:S(2)}) collective-permute-start(f32[1,256]{1,0:T(1,128)S(1)} %get-tuple-element.26), channel_id=1, source_target_pairs={{0,8},{8,16},{16,24},{24,0},{1,9},{9,17},{17,25},{25,1},{2,10},{10... | collective-permute-start | bytes 3080 | tf_op jit(solution)/shard_map/ppermute | solution.py:157
  9.5 4.9 %collective-permute-start.5 = (f32[1,256]{1,0:T(1,128)S(1)}, f32[1,256]{1,0:T(1,128)S(1)}, u32[]{:S(2)}, u32[]{:S(2)}) collective-permute-start(f32[1,256]{1,0:T(1,128)S(1)} %get-tuple-element.26), channel_id=1, source_target_pairs={{0,16},{8,24},{16,0},{24,8},{1,17},{9,25},{17,1},{25,9},{2,18},{10... | collective-permute-start | bytes 3080 | tf_op jit(solution)/shard_map/ppermute | solution.py:157
  14.5 3.9 %collective-permute-start.6 = (bf16[1552,128]{1,0:T(8,128)(2,1)S(1)}, bf16[1552,128]{1,0:T(8,128)(2,1)S(1)}, u32[]{:S(2)}, u32[]{:S(2)}) collective-permute-start(bf16[1552,128]{1,0:T(8,128)(2,1)S(1)} %get-tuple-element.28.refs_0_.refs_3_.refs_2_), channel_id=1, source_target_pairs={{0,1},{1,0},{2,3},{3,2},{4,5},{5,4},{6,7},{7,6},{8,9},{9,8},{10,11... | collective-permute-start | bytes 1191944 | tf_op jit(solution)/shard_map/ppermute | solution.py:151
  14.5 13.3 %collective-permute-start.14 = (bf16[256,768]{1,0:T(8,128)(2,1)S(1)}, bf16[256,768]{1,0:T(8,128)(2,1)S(1)}, u32[]{:S(2)}, u32[]{:S(2)}) collective-permute-start(bf16[256,768]{1,0:T(8,128)(2,1)S(1)} %collective-permute-done.7.emb_ref), channel_id=1, source_target_pairs={{0,8},{8,16},{16,24},{24,0},{1,9},{9,17},{17,25},{25,1},{2,10},{10... | collective-permute-start | bytes 1179656 | tf_op jit(solution)/shard_map/ppermute | solution.py:157
  15.8 3.3 %collective-permute-start.9 = (bf16[784,128]{1,0:T(8,128)(2,1)S(1)}, bf16[784,128]{1,0:T(8,128)(2,1)S(1)}, u32[]{:S(2)}, u32[]{:S(2)}) collective-permute-start(bf16[784,128]{1,0:T(8,128)(2,1)S(1)} %slice.27), channel_id=1, source_target_pairs={{0,1},{1,0},{2,3},{3,2},{4,5},{5,4},{6,7},{7,6},{8,9},{9,8},{10,11... | collective-permute-start | bytes 602120 | tf_op jit(solution)/shard_map/ppermute | solution.py:151
  16.1 3.0 %collective-permute-start.8 = (bf16[768,128]{1,0:T(8,128)(2,1)S(1)}, bf16[768,128]{1,0:T(8,128)(2,1)S(1)}, u32[]{:S(2)}, u32[]{:S(2)}) collective-permute-start(bf16[768,128]{1,0:T(8,128)(2,1)S(1)} %slice.26), channel_id=1, source_target_pairs={{0,1},{1,0},{2,3},{3,2},{4,5},{5,4},{6,7},{7,6},{8,9},{9,8},{10,11... | collective-permute-start | bytes 589832 | tf_op jit(solution)/shard_map/ppermute | solution.py:151
  16.8 7.6 %collective-permute-start.3 = (bf16[784,128]{1,0:T(8,128)(2,1)S(1)}, bf16[784,128]{1,0:T(8,128)(2,1)S(1)}, u32[]{:S(2)}, u32[]{:S(2)}) collective-permute-start(bf16[784,128]{1,0:T(8,128)(2,1)S(1)} %slice.25), channel_id=1, source_target_pairs={{0,4},{1,5},{2,6},{3,7},{4,0},{5,1},{6,2},{7,3},{8,12},{9,13},{10,... | collective-permute-start | bytes 602120 | tf_op jit(solution)/shard_map/ppermute | solution.py:151
  18.4 6.0 %collective-permute-start.1 = (bf16[768,128]{1,0:T(8,128)(2,1)S(1)}, bf16[768,128]{1,0:T(8,128)(2,1)S(1)}, u32[]{:S(2)}, u32[]{:S(2)}) collective-permute-start(bf16[768,128]{1,0:T(8,128)(2,1)S(1)} %slice.24), channel_id=1, source_target_pairs={{0,2},{1,3},{2,0},{3,1},{4,6},{5,7},{6,4},{7,5},{8,10},{9,11},{10,... | collective-permute-start | bytes 589832 | tf_op jit(solution)/shard_map/ppermute | solution.py:151
  20.6 3.8 %collective-permute-start.10 = (f32[1,1,256]{2,1,0:T(1,128)S(1)}, f32[1,1,256]{2,1,0:T(1,128)S(1)}, u32[]{:S(2)}, u32[]{:S(2)}) collective-permute-start(f32[1,1,256]{2,1,0:T(1,128)S(1)} %get-tuple-element.30), channel_id=1, source_target_pairs={{0,2},{1,3},{2,0},{3,1},{4,6},{5,7},{6,4},{7,5},{8,10},{9,11},{10,... | collective-permute-start | bytes 3080 | tf_op jit(solution)/shard_map/ppermute | solution.py:151
  22.1 3.6 %collective-permute-start.11 = (f32[1,1,256]{2,1,0:T(1,128)S(1)}, f32[1,1,256]{2,1,0:T(1,128)S(1)}, u32[]{:S(2)}, u32[]{:S(2)}) collective-permute-start(f32[1,1,256]{2,1,0:T(1,128)S(1)} %get-tuple-element.35), channel_id=1, source_target_pairs={{0,4},{1,5},{2,6},{3,7},{4,0},{5,1},{6,2},{7,3},{8,12},{9,13},{10,... | collective-permute-start | bytes 3080 | tf_op jit(solution)/shard_map/ppermute | solution.py:151
  25.6 1.2 %collective-permute-start.12 = (f32[2,1,256]{2,1,0:T(1,128)S(1)}, f32[2,1,256]{2,1,0:T(1,128)S(1)}, u32[]{:S(2)}, u32[]{:S(2)}) collective-permute-start(f32[2,1,256]{2,1,0:T(1,128)S(1)} %get-tuple-element.36), channel_id=1, source_target_pairs={{0,1},{1,0},{2,3},{3,2},{4,5},{5,4},{6,7},{7,6},{8,9},{9,8},{10,11... | collective-permute-start | bytes 6152 | tf_op jit(solution)/shard_map/ppermute | solution.py:151
  28.0 5.1 %collective-permute-start.17 = (bf16[784,128]{1,0:T(8,128)(2,1)S(1)}, bf16[784,128]{1,0:T(8,128)(2,1)S(1)}, u32[]{:S(2)}, u32[]{:S(2)}) collective-permute-start(bf16[784,128]{1,0:T(8,128)(2,1)S(1)} %slice.23), channel_id=1, source_target_pairs={{0,1},{1,0},{2,3},{3,2},{4,5},{5,4},{6,7},{7,6},{8,9},{9,8},{10,11... | collective-permute-start | bytes 602120 | tf_op jit(solution)/shard_map/ppermute | solution.py:151
  28.1 5.0 %collective-permute-start.16 = (bf16[768,128]{1,0:T(8,128)(2,1)S(1)}, bf16[768,128]{1,0:T(8,128)(2,1)S(1)}, u32[]{:S(2)}, u32[]{:S(2)}) collective-permute-start(bf16[768,128]{1,0:T(8,128)(2,1)S(1)} %slice.22), channel_id=1, source_target_pairs={{0,1},{1,0},{2,3},{3,2},{4,5},{5,4},{6,7},{7,6},{8,9},{9,8},{10,11... | collective-permute-start | bytes 589832 | tf_op jit(solution)/shard_map/ppermute | solution.py:151
  28.6 4.5 %collective-permute-start.18 = (f32[1,1,256]{2,1,0:T(1,128)S(1)}, f32[1,1,256]{2,1,0:T(1,128)S(1)}, u32[]{:S(2)}, u32[]{:S(2)}) collective-permute-start(f32[1,1,256]{2,1,0:T(1,128)S(1)} %get-tuple-element.42), channel_id=1, source_target_pairs={{0,6},{1,7},{2,4},{3,5},{4,2},{5,3},{6,0},{7,1},{8,14},{9,15},{10,... | collective-permute-start | bytes 3080 | tf_op jit(solution)/shard_map/ppermute | solution.py:151
  31.1 4.1 %collective-permute-start.13 = (f32[1,1,256]{2,1,0:T(1,128)S(1)}, f32[1,1,256]{2,1,0:T(1,128)S(1)}, u32[]{:S(2)}, u32[]{:S(2)}) collective-permute-start(f32[1,1,256]{2,1,0:T(1,128)S(1)} %bitcast.20), channel_id=1, source_target_pairs={{0,24},{8,0},{16,8},{24,16},{1,25},{9,1},{17,9},{25,17},{2,26},{10... | collective-permute-start | bytes 3080 | tf_op jit(solution)/shard_map/ppermute | solution.py:157
  32.5 4.5 %collective-permute-start.15 = (f32[1,1,256]{2,1,0:T(1,128)S(1)}, f32[1,1,256]{2,1,0:T(1,128)S(1)}, u32[]{:S(2)}, u32[]{:S(2)}) collective-permute-start(f32[1,1,256]{2,1,0:T(1,128)S(1)} %compare_half_way.1), channel_id=1, source_target_pairs={{0,16},{8,24},{16,0},{24,8},{1,17},{9,25},{17,1},{25,9},{2,18},{10... | collective-permute-start | bytes 3080 | tf_op jit(solution)/shard_map/ppermute | solution.py:157
  33.8 4.0 %collective-permute-start.19 = (f32[1,1,256]{2,1,0:T(1,128)S(1)}, f32[1,1,256]{2,1,0:T(1,128)S(1)}, u32[]{:S(2)}, u32[]{:S(2)}) collective-permute-start(f32[1,1,256]{2,1,0:T(1,128)S(1)} %compare_twin.1), channel_id=1, source_target_pairs={{0,17},{1,16},{2,19},{3,18},{4,21},{5,20},{6,23},{7,22},{8,25},{9,... | collective-permute-start | bytes 3080 | tf_op jit(solution)/shard_map/ppermute | solution.py:161
